TPU v7x, 128 devices: a whole 4x4x4 slice. The times are simulated.
128 devices in a mesh: row: 8 (over z, core), col: 16 (over y, x).
Axes of the slice: x: 4, y: 4, z: 4, core: 2. Of those that a mesh axis runs over, the one named last changes fastest.
Arguments:
- object_slices: float32 [2, 2, 4096, 8192], P(None, None, 'row', 'col'), may hold values from -4.2 to 4.2
- probe: float32 [12, 2, 128, 128], replicated
- measured: float32 [8, 64, 128, 128], P('row', 'col'), may hold values from 0 to 2.2
- positions: int32 [2, 8, 64], P(None, 'row', 'col'), may hold values from 0 to 512, as said below
- counts: int32 [8, 16], P('row', 'col'), may hold values from 1 to 4, as said below
Outputs:
- object_next: float32 [2, 2, 4096, 8192], P(None, None, 'row', 'col')
- probe_next: float32 [12, 2, 128, 128], replicated
Inputs may be any that keep to these rules, and one draw needn't show every extreme that they name: `positions`: row offsets are at most 512 and column offsets at most 512; in the last tile row row offsets are at most 384, in the last tile column column offsets at most 384, so each window lies within its tile and the first 128 rows and columns of the tiles below and to the right. Only the first counts[r, c] slots of a tile are live.
All inputs are finite; a program needn't handle non-finite values.
Results may differ from a plain program's by a relative error of at most 0.0003.
Values sent between devices are 32-bit elements; how exact they have to be, the bound alone decides.
No kernel may reach another device: no remote copies, remote signals or barrier semaphores. Data moves between devices by JAX's collectives and lax.ppermute only.
A program may use at most 320 MiB of HBM per device.

v0:
```python
import math

import jax
import jax.numpy as jnp
from jax import lax
from jax.sharding import PartitionSpec as P

FRESNEL = 40.0
highest = lax.Precision.HIGHEST


def passed_along(shard, axis, by):
    size = lax.axis_size(axis)
    pairs = [(i, i + by) for i in range(size) if 0 <= i + by < size]
    return lax.ppermute(shard, axis, pairs)


def make_tables(width):
    grid_index = jnp.arange(width, dtype=jnp.int32)
    product = grid_index[:, None] * grid_index[None, :] % width
    angles = -2.0 * math.pi / width * product.astype(jnp.float32)
    scaling = 1.0 / math.sqrt(width)
    four_re = jnp.cos(angles) * scaling
    four_im = jnp.sin(angles) * scaling
    frequency = (
        jnp.where(grid_index < width // 2, grid_index, grid_index - width).astype(jnp.float32)
        / width
    )
    phases = -FRESNEL * (frequency[:, None] ** 2 + frequency[None, :] ** 2)
    return (four_re, four_im, jnp.cos(phases), jnp.sin(phases))


def along_last(values, matrix):
    return jnp.einsum("...yk,kx->...yx", values, matrix, precision=highest)


def along_rows(values, matrix):
    return jnp.einsum("yk,...kx->...yx", matrix, values, precision=highest)


def transform(real_part, imag_part, four_re, four_im):
    rows_re = along_last(real_part, four_re) - along_last(imag_part, four_im)
    rows_im = along_last(real_part, four_im) + along_last(imag_part, four_re)
    cols_re = along_rows(rows_re, four_re) - along_rows(rows_im, four_im)
    cols_im = along_rows(rows_re, four_im) + along_rows(rows_im, four_re)
    return (cols_re, cols_im)


def complex_mul(left_re, left_im, right_re, right_im):
    return (left_re * right_re - left_im * right_im, left_re * right_im + left_im * right_re)


def propagate(real_part, imag_part, tables, direction):
    four_re, four_im, prop_re, prop_im = tables
    spec_re, spec_im = transform(real_part, imag_part, four_re, four_im)
    spec_re, spec_im = complex_mul(spec_re, spec_im, prop_re, direction * prop_im)
    return transform(spec_re, spec_im, four_re, -four_im)


def slot_terms(window, pattern, probe, tables):
    four_re, four_im = (tables[0], tables[1])
    slices = window.shape[0]
    wave_re, wave_im = (probe[:, 0], probe[:, 1])
    incoming = []
    for layer_no in range(slices):
        incoming.append((wave_re, wave_im))
        exit_re, exit_im = complex_mul(wave_re, wave_im, window[layer_no, 0], window[layer_no, 1])
        if layer_no + 1 < slices:
            wave_re, wave_im = propagate(exit_re, exit_im, tables, 1.0)
    far_re, far_im = transform(exit_re, exit_im, four_re, four_im)
    residual = jnp.sum(far_re * far_re + far_im * far_im, axis=0) - pattern
    back_re, back_im = transform(residual * far_re, residual * far_im, four_re, -four_im)
    slice_terms = [None] * slices
    for layer_no in reversed(range(slices)):
        input_re, input_im = incoming[layer_no]
        slice_terms[layer_no] = jnp.stack(
            [
                jnp.sum(input_re * back_re + input_im * back_im, axis=0),
                jnp.sum(input_re * back_im - input_im * back_re, axis=0),
            ]
        )
        back_re, back_im = complex_mul(back_re, back_im, window[layer_no, 0], -window[layer_no, 1])
        if layer_no > 0:
            back_re, back_im = propagate(back_re, back_im, tables, -1.0)
    return (jnp.stack(slice_terms), jnp.stack([back_re, back_im], axis=1))


def inner_sum(left_part, right_part):
    return jnp.einsum("jp,kp->jk", left_part, right_part, precision=highest)


def gram_parts(flattened):
    real_part, imag_part = (flattened[:, 0], flattened[:, 1])
    gram_re = inner_sum(real_part, real_part) + inner_sum(imag_part, imag_part)
    gram_im = inner_sum(real_part, imag_part) - inner_sum(imag_part, real_part)
    return (gram_re, gram_im)


def mode_coefficients(gram_re, gram_im):
    modes = gram_re.shape[0]
    zero_val = jnp.zeros_like(gram_re[0, 0])
    one_val = jnp.ones_like(gram_re[0, 0])
    lower = [[(zero_val, zero_val) for col_no in range(modes)] for row_no in range(modes)]
    for col_no in range(modes):
        pivot_sq = gram_re[col_no, col_no]
        for inner in range(col_no):
            entry_re, entry_im = lower[col_no][inner]
            pivot_sq = pivot_sq - (entry_re * entry_re + entry_im * entry_im)
        pivot = jnp.sqrt(pivot_sq)
        lower[col_no][col_no] = (pivot, zero_val)
        for row_no in range(col_no + 1, modes):
            value_re = gram_re[row_no, col_no]
            value_im = gram_im[row_no, col_no]
            for inner in range(col_no):
                left_re, left_im = lower[row_no][inner]
                right_re, right_im = lower[col_no][inner]
                value_re = value_re - (left_re * right_re + left_im * right_im)
                value_im = value_im - (left_im * right_re - left_re * right_im)
            lower[row_no][col_no] = (value_re / pivot, value_im / pivot)
    coef = [[(zero_val, zero_val) for col_no in range(modes)] for row_no in range(modes)]
    for col_no in range(modes):
        coef[col_no][col_no] = (one_val, zero_val)
        for row_no in reversed(range(col_no)):
            acc_re, acc_im = (zero_val, zero_val)
            for inner in range(row_no + 1, col_no + 1):
                upper_re, upper_im = (lower[inner][row_no][0], -lower[inner][row_no][1])
                coef_re_val, coef_im_val = coef[inner][col_no]
                acc_re = acc_re + upper_re * coef_re_val - upper_im * coef_im_val
                acc_im = acc_im + upper_re * coef_im_val + upper_im * coef_re_val
            pivot_val = lower[row_no][row_no][0]
            coef[row_no][col_no] = (-acc_re / pivot_val, -acc_im / pivot_val)
    coef_re = jnp.stack(
        [jnp.stack([coef[row_no][col_no][0] for col_no in range(modes)]) for row_no in range(modes)]
    )
    coef_im = jnp.stack(
        [jnp.stack([coef[row_no][col_no][1] for col_no in range(modes)]) for row_no in range(modes)]
    )
    return (coef_re, coef_im)


def combine_modes(coefs, values):
    return jnp.einsum("jk,jp->kp", coefs, values, precision=highest)


def orthogonal_modes(flattened, coef_re, coef_im):
    real_part, imag_part = (flattened[:, 0], flattened[:, 1])
    out_re = combine_modes(coef_re, real_part) - combine_modes(coef_im, imag_part)
    out_im = combine_modes(coef_re, imag_part) + combine_modes(coef_im, real_part)
    return jnp.stack([out_re, out_im], axis=1)


def local(object_slices, probe, measured, positions, counts):
    slices = object_slices.shape[0]
    tile_rows = object_slices.shape[2]
    tile_cols = object_slices.shape[3]
    modes = probe.shape[0]
    width = probe.shape[-1]
    capacity = positions.shape[2]
    tables = make_tables(width)
    from_right = passed_along(object_slices[:, :, :, :width], "col", -1)
    widened = jnp.concatenate([object_slices, from_right], axis=3)
    from_below = passed_along(widened[:, :, :width, :], "row", -1)
    extended = jnp.concatenate([widened, from_below], axis=2)
    top_rows = positions[0, 0]
    left_cols = positions[1, 0]
    anchor = jnp.int32(0)
    windows = jnp.stack(
        [
            lax.dynamic_slice(
                extended,
                (anchor, anchor, top_rows[slot_no], left_cols[slot_no]),
                (slices, 2, width, width),
            )
            for slot_no in range(capacity)
        ]
    )
    patterns = measured[0]
    own_count = counts[0, 0]
    empty_probe = jnp.zeros_like(probe)
    buffer = jnp.zeros((capacity, slices, 2, width, width), jnp.float32)

    def visit(step_no, carried):
        buffer_now, probe_total = carried
        slot_place = 0 + step_no
        window = lax.dynamic_index_in_dim(windows, slot_place, 0, keepdims=False)
        pattern = lax.dynamic_index_in_dim(patterns, slot_place, 0, keepdims=False)
        obj_term, probe_term = slot_terms(window, pattern, probe, tables)
        buffer_now = lax.dynamic_update_index_in_dim(buffer_now, obj_term, slot_place, 0)
        return (buffer_now, probe_total + probe_term)

    slot_grads, probe_grad = lax.fori_loop(0, own_count, visit, (buffer, empty_probe))
    grad_ext = jnp.zeros_like(extended)
    for slot_no in range(capacity):
        corner = (anchor, anchor, top_rows[slot_no], left_cols[slot_no])
        current = lax.dynamic_slice(grad_ext, corner, (slices, 2, width, width))
        grad_ext = lax.dynamic_update_slice(grad_ext, current + slot_grads[slot_no], corner)
    upward = passed_along(grad_ext[:, :, tile_rows:, :], "row", 1)
    upper_part = grad_ext[:, :, :tile_rows, :]
    upper_part = upper_part.at[:, :, :width, :].add(upward)
    leftward = passed_along(upper_part[:, :, :, tile_cols:], "col", 1)
    grad_tile = upper_part[:, :, :, :tile_cols].at[:, :, :, :width].add(leftward)
    object_next = object_slices - grad_tile
    divisor = math.sqrt(lax.axis_size("row") * lax.axis_size("col") * capacity)
    pixels = width * width
    grad_total = lax.psum(probe_grad, ("row", "col"))
    stepped = (probe - grad_total / divisor).reshape(modes, 2, pixels)
    gram_re, gram_im = gram_parts(stepped)
    coef_re, coef_im = mode_coefficients(gram_re, gram_im)
    probe_next = orthogonal_modes(stepped, coef_re, coef_im).reshape(modes, 2, width, width)
    return (object_next, probe_next)


def solution(mesh):
    return jax.shard_map(
        local,
        mesh=mesh,
        in_specs=(
            P(None, None, "row", "col"),
            P(),
            P("row", "col", None, None),
            P(None, "row", "col"),
            P("row", "col"),
        ),
        out_specs=(P(None, None, "row", "col"), P()),
        check_vma=False,
    )
```

profile of v0, /device:TPU:1, one launch (start us, length us, event | category | flops | bytes accessed | tf_op | source)
XLA Modules:
  0.0 729.8 jit_solution(9925926040009886206)
XLA Ops:
  9.8 2.6 constant_dynamic-update-slice_fusion.2
  12.5 22.4 %collective-permute-done = f32[2,2,512,128]{3,2,1,0:T(8,128)S(1)} collective-permute-done((f32[2,2,512,128]{3,2,1,0:T(8,128)S(1)}, f32[2,2,512,128]{3,2,1,0:T(8,128)S(1)}, u32[]{:S(2)}, u32[]{:S(2)}) %collective-permute-start) | collective-permute-done | bytes 1048608 | tf_op jit(solution)/shard_map/ppermute | solution.py:15
  34.9 2.3 copy-done
  38.4 3.6 collective-permute-start.1
  59.4 2.4 fusion.403
  65.8 90.1 %while.18 = (s32[]{:T(128)}, f32[4,2,2,128,128]{4,3,2,1,0:T(8,128)}, f32[12,2,128,128]{2,3,0,1:T(8,128)}, s32[]{:T(128)}, f32[12,2,128,128]{2,3,0,1:T(8,128)S(1)...) while((s32[]{:T(128)}, ...), condition=%wide.region_6.7_spmd.clone.clone.clone, body=%wide.region_0.6_spmd.clone.clone.clone.sunk | while | flops 14530854912 | bytes 130351832 | solution.py:191
  68.3 1.6 fusion.642
  69.9 1.6 convolution_add_fusion.20
  71.5 1.6 fusion.640
  73.1 1.6 convolution_subtract_fusion.20
  79.3 1.7 fusion.643
  81.0 1.6 fusion.648
  82.6 1.6 convolution_add_fusion.21
  84.3 1.6 fusion.646
  85.9 1.6 convolution_subtract_fusion.21
  87.5 1.5 fusion.650
  90.5 1.7 fusion.647
  92.3 1.5 fusion.649
  93.8 1.6 fusion.654
  95.5 1.6 convolution_add_fusion.22
  97.1 1.6 fusion.652
  98.7 1.6 convolution_subtract_fusion.22
  103.4 1.9 fusion.655
  105.4 1.6 add_reduce_fusion.4
  107.0 1.6 fusion.660
  108.5 1.6 convolution_add_fusion.23
  110.1 1.6 fusion.658
  111.7 1.6 convolution_subtract_fusion.23
  114.8 1.7 fusion.659
  116.5 1.5 fusion.661
  118.1 1.7 add_reduce_fusion.5
  119.7 1.6 fusion.666
  121.4 1.6 convolution_add_fusion.24
  123.0 1.6 fusion.664
  124.7 1.6 convolution_subtract_fusion.24
  127.8 1.8 fusion.669
  131.1 1.5 fusion.667
  132.6 1.6 fusion.672
  134.3 1.6 convolution_add_fusion.25
  135.9 1.6 fusion.670
  137.5 1.6 convolution_subtract_fusion.25
  140.6 1.9 fusion.671
  142.6 1.5 fusion.673
  144.1 1.9 subtract_bitcast_fusion.2
  148.5 2.8 maximum_add_fusion.2
  157.1 3.1 broadcast_in_dim.10
  160.3 4.3 dynamic_update_slice.17
  165.8 4.4 dynamic_update_slice.18
  171.4 4.4 dynamic_update_slice.19
  177.0 4.4 dynamic_update_slice.20
  181.4 2.5 slice.795
  183.9 5.2 slice.793
  189.0 3.2 collective-permute-start.2
  192.2 371.8 %all-reduce.2.cloned.1.call-done = f32[12,2,128,128]{2,3,0,1:T(8,128)} async-done(((f32[12,2,128,128]{2,3,0,1:T(8,128)}), f32[12,2,128,128]{2,3,0,1:T(8,128)}) %all-reduce.2.cloned.1.call-update) | async-done | bytes 1572880 | tf_op jit(solution)/shard_map/psum | solution.py:205
  564.0 1.6 multiply_subtract_fusion.12
  567.0 1.6 fusion.409
  568.6 1.7 fusion.395
  570.3 2.2 fusion.382
  572.5 1.8 convolution_add_fusion.13
  578.9 2.1 convolution_subtract_fusion.13
  692.5 2.9 fusion.376
  696.7 2.0 collective-permute-start.3
  705.4 14.1 %collective-permute-done.3 = f32[2,2,512,128]{3,2,1,0:T(8,128)S(1)} collective-permute-done((f32[2,2,512,128]{3,2,1,0:T(8,128)S(1)}, f32[2,2,512,128]{3,2,1,0:T(8,128)S(1)}, u32[]{:S(2)}, u32[]{:S(2)}) %collective-permute-start.3) | collective-permute-done | bytes 1048608 | tf_op jit(solution)/shard_map/ppermute | solution.py:15
  719.7 3.0 sub.3137
  (112 shorter events, 53.0 us)
Async XLA Ops:
  7.2 556.9 %all-reduce.2.cloned.1.call-start = ((), (), s32[]{:S(2)}) async-start(), calls=%async_computation | async-start | bytes 3145728 | tf_op jit(solution)/shard_map/psum | solution.py:205
  8.5 26.3 %collective-permute-start = (f32[2,2,512,128]{3,2,1,0:T(8,128)S(1)}, f32[2,2,512,128]{3,2,1,0:T(8,128)S(1)}, u32[]{:S(2)}, u32[]{:S(2)}) collective-permute-start(f32[2,2,512,128]{3,2,1,0:T(8,128)S(1)} %slice.605), channel_id=1, source_target_pairs={{1,0},{2,1},{3,2},{4,3},{5,4},{6,5},{7,6},{8,7},{9,8},{10,9},{11,1... | collective-permute-start | bytes 3145736 | tf_op jit(solution)/shard_map/ppermute | solution.py:15
  34.9 2.3 copy-start
  37.2 4.8 copy-start.7
  37.2 15.5 %copy-start.6 = (f32[1,4,128,128]{3,2,1,0:T(8,128)S(1)}, f32[1,4,128,128]{3,2,1,0:T(8,128)}, u32[]{:S(2)}) copy-start(f32[1,4,128,128]{3,2,1,0:T(8,128)} %param.13) | copy-start | bytes 786436
  37.2 15.6 %copy-start.3 = (f32[12,2,128,128]{3,2,1,0:T(8,128)S(1)}, f32[12,2,128,128]{3,2,1,0:T(8,128)}, u32[]{:S(2)}) copy-start(f32[12,2,128,128]{3,2,1,0:T(8,128)} %param.12) | copy-start | bytes 4718596
  38.4 21.0 %collective-permute-start.1 = (f32[2,2,128,640]{3,2,1,0:T(8,128)}, f32[2,2,128,640]{3,2,1,0:T(8,128)}, u32[]{:S(2)}, u32[]{:S(2)}) collective-permute-start(f32[2,2,128,640]{3,2,1,0:T(8,128)} %slice.792), channel_id=1, source_target_pairs={{16,0},{32,16},{48,32},{64,48},{80,64},{96,80},{112,96},{17,1},{33... | collective-permute-start | bytes 3932168 | tf_op jit(solution)/shard_map/ppermute | solution.py:15
  66.9 40.0 %copy-start.4 = (f32[4,128,128]{1,2,0:T(8,128)}, f32[4,128,128]{1,2,0:T(8,128)S(1)}, u32[]{:S(2)}) copy-start(f32[4,128,128]{1,2,0:T(8,128)S(1)} %get-tuple-element.770) | copy-start | bytes 786436 | tf_op jit(solution)/shard_map/while
  148.5 2.8 copy-start.5
  155.9 1.2 copy-start.2
  189.0 503.4 %collective-permute-start.2 = (f32[2,2,128,640]{3,2,1,0:T(8,128)}, f32[2,2,128,640]{3,2,1,0:T(8,128)}, u32[]{:S(2)}, u32[]{:S(2)}) collective-permute-start(f32[2,2,128,640]{3,2,1,0:T(8,128)} %slice.795), channel_id=1, source_target_pairs={{0,16},{16,32},{32,48},{48,64},{64,80},{80,96},{96,112},{1,17},{17... | collective-permute-start | bytes 3932168 | tf_op jit(solution)/shard_map/ppermute | solution.py:15
  682.0 9.1 %copy-start.8 = (f32[1,12]{1,0:T(1,128)S(1)}, f32[1,12]{1,0:T(1,128)}, u32[]{:S(2)}) copy-start(f32[1,12]{1,0:T(1,128)} %constant.126.clone.1) | copy-start | bytes 148
  696.7 22.9 %collective-permute-start.3 = (f32[2,2,512,128]{3,2,1,0:T(8,128)S(1)}, f32[2,2,512,128]{3,2,1,0:T(8,128)S(1)}, u32[]{:S(2)}, u32[]{:S(2)}) collective-permute-start(f32[2,2,512,128]{3,2,1,0:T(8,128)S(1)} %slice.798), channel_id=1, source_target_pairs={{0,1},{1,2},{2,3},{3,4},{4,5},{5,6},{6,7},{7,8},{8,9},{9,10},{10,1... | collective-permute-start | bytes 3145736 | tf_op jit(solution)/shard_map/ppermute | solution.py:15
  700.4 4.5 slice-start
  703.2 1.7 slice-start.1
  704.8 14.9 %copy-start.1 = (f32[2,2,512,512]{3,2,1,0:T(8,128)S(1)}, f32[2,2,512,512]{3,2,1,0:T(8,128)}, u32[]{:S(2)}) copy-start(f32[2,2,512,512]{3,2,1,0:T(8,128)} %param.11) | copy-start | bytes 12582916
Sparse Core Ops, SparseCore 0:
  156.0 407.9 all-reduce.1
where the time goes:
time: 740 us; the launch traced here: 730 us
  waiting for transfers between devices  409 us (55%)
  between operations  136 us (18%)
  matrix products  90.6 us (12%)
  local copies, waits for them, and re-layouts  57.5 us (8%)
  other arithmetic  19.9 us (3%)
  starting transfers between devices  10.1 us (1%)
    psum x1, waiting for transfers between devices, local(): grad_total = lax.psum(probe_grad, ('row', 'col'))  372 us
    dot_general x24, matrix products, along_rows(): return jnp.einsum('yk,...kx->...yx', matrix, values, precision=highest)  38.7 us
    dot_general x24, matrix products, along_last(): return jnp.einsum('...yk,kx->...yx', values, matrix, precision=highest)  38.6 us
    ppermute x4, waiting for transfers between devices, passed_along(): return lax.ppermute(shard, axis, pairs)  37.5 us
    dynamic_update_slice x4, local copies, waits for them, and re-layouts, local(): lax.dynamic_update_slice(grad_ext, current + slot_grads[slot_no], corner)  17.6 us
  transfers between devices with their start and end apart: 5, of which 4 were waited for; matrix products, arithmetic and copies ran while one was open for 9% of the time, Pallas kernels for 0%

commit v1 on v0

v1 whole, which is shorter than its diff:
```python
import functools
import math

import jax
import jax.numpy as jnp
import numpy as np
from jax import lax
from jax.experimental import pallas as pl
from jax.experimental.pallas import tpu as pltpu
from jax.sharding import PartitionSpec as P

FRESNEL = 40.0
f32 = jnp.float32
bf16 = jnp.bfloat16


def complex_block(matrix):
    return np.block([[matrix.real, matrix.imag], [-matrix.imag, matrix.real]])


def split_table(block):
    block = block.astype(np.float32)
    high = block.astype(jnp.bfloat16)
    low = (block - high.astype(np.float32)).astype(jnp.bfloat16)
    return np.stack([high, low])


def make_tables(width):
    index = np.arange(width)
    fourier = np.exp(-2j * np.pi / width * (index[:, None] * index[None, :] % width)) / np.sqrt(width)
    frequency = np.where(index < width // 2, index, index - width) / width
    chirp = np.exp(-1j * FRESNEL * frequency**2)
    spread = fourier.conj() @ (chirp[:, None] * fourier)
    forward = complex_block(fourier)
    step = complex_block(spread)
    return np.stack(
        [split_table(forward), split_table(forward.T), split_table(step), split_table(step.T)]
    )


def split(values):
    high = values.astype(bf16)
    low = (values - high.astype(f32)).astype(bf16)
    return high, low


def mm(left, right):
    return jnp.dot(left, right, preferred_element_type=f32)


def times_right(planes, table):
    a_re, a_im, b_re, b_im = planes
    stacked = jnp.concatenate(
        [jnp.concatenate([a_re, a_im], axis=1), jnp.concatenate([b_re, b_im], axis=1)], axis=0
    )
    high, low = split(stacked)
    out = mm(high, table[0]) + mm(low, table[0]) + mm(high, table[1])
    w = a_re.shape[0]
    return out[:w, :w], out[:w, w:], out[w:, :w], out[w:, w:]


def times_left(planes, table):
    a_re, a_im, b_re, b_im = planes
    stacked = jnp.concatenate(
        [jnp.concatenate([a_re, b_re], axis=1), jnp.concatenate([a_im, b_im], axis=1)], axis=0
    )
    high, low = split(stacked)
    out = mm(table[0], high) + mm(table[0], low) + mm(table[1], high)
    w = a_re.shape[0]
    return out[:w, :w], out[w:, :w], out[:w, w:], out[w:, w:]


def cmul(planes, re, im):
    a_re, a_im, b_re, b_im = planes
    return (
        a_re * re - a_im * im,
        a_re * im + a_im * re,
        b_re * re - b_im * im,
        b_re * im + b_im * re,
    )


def cmul_conj(planes, re, im):
    a_re, a_im, b_re, b_im = planes
    return (
        a_re * re + a_im * im,
        a_im * re - a_re * im,
        b_re * re + b_im * im,
        b_im * re - b_re * im,
    )


def overlap(wave, grad):
    re = wave[0] * grad[0] + wave[1] * grad[1] + wave[2] * grad[2] + wave[3] * grad[3]
    im = wave[0] * grad[1] - wave[1] * grad[0] + wave[2] * grad[3] - wave[3] * grad[2]
    return re, im


D_RIGHT, D_LEFT, P_RIGHT, P_LEFT = 0, 1, 2, 3


def slots_kernel(
    group,
    count_ref, pos_ref, tile, right, below, corner, probe_ref, pattern_ref, table_ref,
    pgrad_ref, tile_out, right_out, below_out, corner_out,
    ext, nxt, win, psi, far, inten, obj, sem_in, sem_out,
):
    width = probe_ref.shape[-1]
    rows, cols = tile.shape[2:]
    pairs = probe_ref.shape[0] // 4

    def region(ref, part):
        r, c = {"tile": (0, 0), "right": (0, 1), "below": (1, 0), "corner": (1, 1)}[part]
        rs = pl.ds(rows, width) if r else pl.ds(0, rows)
        cs = pl.ds(cols, width) if c else pl.ds(0, cols)
        return ref.at[:, :, rs, cs]

    loads = [
        pltpu.make_async_copy(src, region(ext, name), sem_in.at[i])
        for i, (src, name) in enumerate(
            [(tile, "tile"), (right, "right"), (below, "below"), (corner, "corner")]
        )
    ]
    loads.append(pltpu.make_async_copy(tile, region(nxt, "tile"), sem_in.at[4]))
    for copy in loads:
        copy.start()
    nxt[:, :, 0 : rows + width, cols : cols + width] = jnp.zeros((2, 2, rows + width, width), f32)
    nxt[:, :, rows : rows + width, 0:cols] = jnp.zeros((2, 2, width, cols), f32)
    pgrad_ref[...] = jnp.zeros_like(pgrad_ref)
    for copy in loads:
        copy.wait()

    def table(which):
        return table_ref[which, 0], table_ref[which, 1]

    def load4(ref, pair):
        return tuple(ref[pair * 4 + i] for i in range(4))

    def visit(slot, carry):
        top = pos_ref[0, slot]
        left = pos_ref[1, slot]
        top8 = pl.multiple_of((top // 8) * 8, 8)
        left128 = pl.multiple_of((left // width) * width, width)
        drop_r = top - top8
        drop_c = left - left128
        for s in range(2):
            for c in range(2):
                wide = ext[s, c, pl.ds(top8, width + 8), pl.ds(left128, 2 * width)]
                wide = pltpu.roll(wide, 2 * width - drop_c, 1)[:, :width]
                win[s, c] = pltpu.roll(wide, width + 8 - drop_r, 0)[:width]
        inten[...] = jnp.zeros_like(inten)

        def forward(step, carry):
            ids = [step * group + i for i in range(group)]
            waves = [cmul(load4(probe_ref, p), win[0, 0], win[0, 1]) for p in ids]
            waves = [times_right(v, table(P_RIGHT)) for v in waves]
            waves = [times_left(v, table(P_LEFT)) for v in waves]
            for p, v in zip(ids, waves):
                for i in range(4):
                    psi[p * 4 + i] = v[i]
            waves = [cmul(v, win[1, 0], win[1, 1]) for v in waves]
            waves = [times_right(v, table(D_RIGHT)) for v in waves]
            waves = [times_left(v, table(D_LEFT)) for v in waves]
            total = inten[...]
            for p, v in zip(ids, waves):
                for i in range(4):
                    far[p * 4 + i] = v[i]
                total = total + (v[0] * v[0] + v[1] * v[1] + v[2] * v[2] + v[3] * v[3])
            inten[...] = total
            return carry

        lax.fori_loop(0, pairs // group, forward, 0)
        inten[...] = inten[...] - pattern_ref[slot]
        obj[...] = jnp.zeros_like(obj)

        def backward(step, carry):
            ids = [step * group + i for i in range(group)]
            residual = inten[...]
            grads = [tuple(residual * x for x in load4(far, p)) for p in ids]
            grads = [times_right(v, table(D_LEFT)) for v in grads]
            grads = [times_left(v, table(D_RIGHT)) for v in grads]
            for p, v in zip(ids, grads):
                re, im = overlap(load4(psi, p), v)
                obj[1, 0] += re
                obj[1, 1] += im
            grads = [cmul_conj(v, win[1, 0], win[1, 1]) for v in grads]
            grads = [times_right(v, table(P_LEFT)) for v in grads]
            grads = [times_left(v, table(P_RIGHT)) for v in grads]
            for p, v in zip(ids, grads):
                re, im = overlap(load4(probe_ref, p), v)
                obj[0, 0] += re
                obj[0, 1] += im
            grads = [cmul_conj(v, win[0, 0], win[0, 1]) for v in grads]
            for p, v in zip(ids, grads):
                for i in range(4):
                    pgrad_ref[p * 4 + i] += v[i]
            return carry

        lax.fori_loop(0, pairs // group, backward, 0)
        for s in range(2):
            for c in range(2):
                wide = jnp.concatenate([obj[s, c], jnp.zeros((8, width), f32)], axis=0)
                wide = pltpu.roll(wide, drop_r, 0)
                wide = jnp.concatenate([wide, jnp.zeros_like(wide)], axis=1)
                wide = pltpu.roll(wide, drop_c, 1)
                place = (s, c, pl.ds(top8, width + 8), pl.ds(left128, 2 * width))
                nxt[place] = nxt[place] - wide
        return carry

    lax.fori_loop(0, count_ref[0, 0], visit, 0)
    stores = [
        pltpu.make_async_copy(region(nxt, name), dst, sem_out.at[i])
        for i, (dst, name) in enumerate(
            [(tile_out, "tile"), (right_out, "right"), (below_out, "below"), (corner_out, "corner")]
        )
    ]
    for copy in stores:
        copy.start()
    for copy in stores:
        copy.wait()


def run_slots(tile, right, below, corner, probe, patterns, positions, counts, group=2):
    width = probe.shape[-1]
    rows, cols = tile.shape[2:]
    planes = 2 * probe.shape[0]
    tables = jnp.asarray(make_tables(width))
    vmem = pl.BlockSpec(memory_space=pltpu.VMEM)
    smem = pl.BlockSpec(memory_space=pltpu.SMEM)
    hbm = pl.BlockSpec(memory_space=pl.ANY)
    padded = (2, 2, rows + width + 8, cols + 2 * width)
    shapes = [
        jax.ShapeDtypeStruct((planes, width, width), f32),
        jax.ShapeDtypeStruct(tile.shape, f32),
        jax.ShapeDtypeStruct(right.shape, f32),
        jax.ShapeDtypeStruct(below.shape, f32),
        jax.ShapeDtypeStruct(corner.shape, f32),
    ]
    return pl.pallas_call(
        functools.partial(slots_kernel, group),
        out_shape=shapes,
        in_specs=[smem, smem, hbm, hbm, hbm, hbm, vmem, vmem, vmem],
        out_specs=[vmem, hbm, hbm, hbm, hbm],
        scratch_shapes=[
            pltpu.VMEM(padded, f32),
            pltpu.VMEM(padded, f32),
            pltpu.VMEM((2, 2, width, width), f32),
            pltpu.VMEM((planes, width, width), f32),
            pltpu.VMEM((planes, width, width), f32),
            pltpu.VMEM((width, width), f32),
            pltpu.VMEM((2, 2, width, width), f32),
            pltpu.SemaphoreType.DMA((5,)),
            pltpu.SemaphoreType.DMA((4,)),
        ],
        compiler_params=pltpu.CompilerParams(vmem_limit_bytes=56 * 1024 * 1024),
        name="slots",
    )(counts, positions, tile, right, below, corner, probe.reshape(planes, width, width), patterns, tables)


def core_groups(rows, cols, split):
    return [
        [r * cols + c for r in range(part, rows, split) for c in range(cols)]
        for part in range(split)
    ]


def orthogonal_kernel(scale, probe_ref, total_ref, out_ref, stepped, sums, gram, coef):
    planes, width = probe_ref.shape[0], probe_ref.shape[-1]
    modes = planes // 2
    sub = 8
    chunks = width // sub
    stepped[...] = probe_ref[...] - total_ref[...] * scale

    block = 3
    sums[...] = jnp.zeros_like(sums)
    for jb in range(0, modes, block):
        for kb in range(jb, modes, block):
            pairs = [
                (j, k) for j in range(jb, jb + block) for k in range(kb, kb + block) if j <= k
            ]

            def accumulate(chunk, carried):
                rows = pl.ds(pl.multiple_of(chunk * sub, sub), sub)
                left = {j: (stepped[2 * j, rows], stepped[2 * j + 1, rows]) for j in range(jb, jb + block)}
                right = {k: (stepped[2 * k, rows], stepped[2 * k + 1, rows]) for k in range(kb, kb + block)}
                out = []
                for (j, k), (acc_re, acc_im) in zip(pairs, carried):
                    (l_re, l_im), (r_re, r_im) = left[j], right[k]
                    out.append(
                        (
                            acc_re + l_re * r_re + l_im * r_im,
                            acc_im + l_re * r_im - l_im * r_re,
                        )
                    )
                return out

            zero = jnp.zeros((sub, width), f32)
            result = lax.fori_loop(
                0, chunks, accumulate, [(zero, zero) for _ in pairs], unroll=4
            )
            for (j, k), (acc_re, acc_im) in zip(pairs, result):
                s_re = jnp.sum(acc_re, axis=0, keepdims=True)
                s_im = jnp.sum(acc_im, axis=0, keepdims=True)
                sums[0, j, k : k + 1] = s_re
                sums[1, j, k : k + 1] = s_im
                if j != k:
                    sums[0, k, j : j + 1] = s_re
                    sums[1, k, j : j + 1] = -s_im
    side = sums.shape[1]
    ones = jnp.ones((sub, width), f32)
    for part in range(2):
        for j in range(modes):
            row = lax.dot_general(
                ones, sums[part, j], (((1,), (1,)), ((), ())),
                precision=lax.Precision.HIGHEST, preferred_element_type=f32,
            )
            gram[part, j : j + 1, 0:side] = row[0:1]

    row_id = lax.broadcasted_iota(jnp.int32, (side, width), 0)
    lane_id = lax.broadcasted_iota(jnp.int32, (side, width), 1)
    valid = (row_id < modes) & (lane_id < modes)
    eye = jnp.where((lane_id == row_id + side) & (row_id < modes), 1.0, 0.0)
    work_re = jnp.where(valid, gram[0], 0.0) + eye
    work_im = jnp.where(valid, gram[1], 0.0)
    for k in range(modes - 1):
        row_re = work_re[k : k + 1]
        row_im = work_im[k : k + 1]
        inverse = 1.0 / work_re[k : k + 1, k : k + 1]
        f_re = jnp.where(row_id[:, :1] > k, work_re[:, k : k + 1] * inverse, 0.0)
        f_im = jnp.where(row_id[:, :1] > k, work_im[:, k : k + 1] * inverse, 0.0)
        work_re, work_im = (
            work_re - (f_re * row_re - f_im * row_im),
            work_im - (f_re * row_im + f_im * row_re),
        )
    place = 0
    for k in range(modes):
        for j in range(k):
            coef[place] = jnp.broadcast_to(work_re[k : k + 1, side + j : side + j + 1], (sub, width))
            coef[place + 1] = jnp.broadcast_to(work_im[k : k + 1, side + j : side + j + 1], (sub, width))
            place += 2

    def combine(chunk, carry):
        rows = pl.ds(pl.multiple_of(chunk * sub, sub), sub)
        values = [stepped[i, rows] for i in range(planes)]
        place = 0
        for k in range(modes):
            acc_re, acc_im = values[2 * k], values[2 * k + 1]
            for j in range(k):
                c_re, c_im = coef[place], coef[place + 1]
                place += 2
                acc_re = acc_re + (c_re * values[2 * j] + c_im * values[2 * j + 1])
                acc_im = acc_im + (c_re * values[2 * j + 1] - c_im * values[2 * j])
            out_ref[2 * k, rows] = acc_re
            out_ref[2 * k + 1, rows] = acc_im
        return carry

    lax.fori_loop(0, chunks, combine, 0)


def orthogonalize(probe, total, divisor):
    planes, width = probe.shape[0], probe.shape[-1]
    modes = planes // 2
    side = 16
    vmem = pl.BlockSpec(memory_space=pltpu.VMEM)
    return pl.pallas_call(
        functools.partial(orthogonal_kernel, 1.0 / divisor),
        out_shape=jax.ShapeDtypeStruct(probe.shape, f32),
        in_specs=[vmem, vmem],
        out_specs=vmem,
        scratch_shapes=[
            pltpu.VMEM(probe.shape, f32),
            pltpu.VMEM((2, side, side, width), f32),
            pltpu.VMEM((2, side, width), f32),
            pltpu.VMEM((modes * (modes - 1), 8, width), f32),
        ],
        compiler_params=pltpu.CompilerParams(vmem_limit_bytes=32 * 1024 * 1024),
        name="orthogonalize",
    )(probe, total)


def moved(shard, axes, pairs):
    return lax.ppermute(shard, axes, pairs)


def shifted(size, by):
    return [(i, i + by) for i in range(size) if 0 <= i + by < size]


def shifted_both(rows, cols, by):
    return [
        (r * cols + c, (r + by) * cols + c + by)
        for r in range(rows)
        for c in range(cols)
        if 0 <= r + by < rows and 0 <= c + by < cols
    ]


def total_over_devices(own, rows, cols):
    planes, width = own.shape[0], own.shape[-1]
    core = lax.axis_index("row") % 2
    swap = [(r, r ^ 1) for r in range(rows)]
    halves = own.reshape(2, planes // 2 * width, width)
    keep = lax.dynamic_index_in_dim(halves, core, 0, keepdims=False)
    give = lax.dynamic_index_in_dim(halves, 1 - core, 0, keepdims=False)
    keep = keep + moved(give, "row", swap)
    members = rows * cols // 2
    groups = core_groups(rows, cols, 2)
    parts = keep.reshape(members, -1, width)
    parts = lax.all_to_all(parts, ("row", "col"), 0, 0, axis_index_groups=groups)
    share = jnp.sum(parts, axis=0, keepdims=True)
    share = jnp.broadcast_to(share, parts.shape)
    mine = lax.all_to_all(share, ("row", "col"), 0, 0, axis_index_groups=groups)
    mine = mine.reshape(keep.shape)
    other = moved(mine, "row", swap)
    first = jnp.where(core == 0, mine, other)
    second = jnp.where(core == 0, other, mine)
    return jnp.concatenate([first, second]).reshape(own.shape)


def local(object_slices, probe, measured, positions, counts):
    rows, cols = lax.axis_size("row"), lax.axis_size("col")
    modes, width = probe.shape[0], probe.shape[-1]
    capacity = positions.shape[2]
    left_one, right_one = shifted(cols, -1), shifted(cols, 1)
    up_one, down_one = shifted(rows, -1), shifted(rows, 1)
    right = moved(object_slices[:, :, :, :width], "col", left_one)
    below = moved(object_slices[:, :, :width, :], "row", up_one)
    corner = moved(
        object_slices[:, :, :width, :width], ("row", "col"), shifted_both(rows, cols, -1)
    )
    probe_grad, partial, right_grad, below_grad, corner_grad = run_slots(
        object_slices, right, below, corner, probe, measured[0], positions[:, 0], counts, group=6
    )
    from_left = moved(right_grad, "col", right_one)
    from_above = moved(below_grad, "row", down_one)
    from_corner = moved(corner_grad, ("row", "col"), shifted_both(rows, cols, 1))
    total = total_over_devices(probe_grad, rows, cols)
    object_next = partial.at[:, :, :, :width].add(from_left)
    object_next = object_next.at[:, :, :width, :].add(from_above)
    object_next = object_next.at[:, :, :width, :width].add(from_corner)
    divisor = math.sqrt(rows * cols * capacity)
    planes = probe.reshape(2 * modes, width, width)
    probe_next = orthogonalize(planes, total, divisor).reshape(probe.shape)
    return (object_next, probe_next)


def solution(mesh):
    return jax.shard_map(
        local,
        mesh=mesh,
        in_specs=(
            P(None, None, "row", "col"),
            P(),
            P("row", "col", None, None),
            P(None, "row", "col"),
            P("row", "col"),
        ),
        out_specs=(P(None, None, "row", "col"), P()),
        check_vma=False,
    )
```

time: 740 us -> 151 us (0.20); the launches traced: 730 us -> 151 us
  waiting for transfers between devices: 409 us -> 57.5 us
  between operations: 136 us -> 1.45 us
  matrix products: 90.6 us -> 0 us
  local copies, waits for them, and re-layouts: 57.5 us -> 9.33 us
  starting transfers between devices: 10.1 us -> 52.9 us
  Pallas kernels: 0 us -> 22.2 us
  other arithmetic: 19.9 us -> 7.86 us
    psum x1 -> x0, waiting for transfers between devices: 372 us -> none  [local(): grad_total = lax.psum(probe_grad, ('row', 'col'))]
    dot_general x56 -> x0, matrix products: 90.6 us -> none  [the longest x24 38.7 us: along_rows(): return jnp.einsum('yk,...kx->...yx', matrix, values, precision=highest)]
    all_to_all x0 -> x2, starting transfers between devices: none -> 34.2 us  [the longest x1 29.6 us: total_over_devices(): lax.all_to_all(parts, ('row', 'col'), 0, 0, axis_index_groups=groups)]
    all_to_all x0 -> x2, waiting for transfers between devices: none -> 31.2 us  [the longest x1 18.7 us: total_over_devices(): mine = lax.all_to_all(share, ('row', 'col'), 0, 0, axis_index_groups=groups)]
    pallas_call x0 -> x2, Pallas kernels: none -> 22.2 us  [the longest x1 16.2 us: run_slots(): pl.pallas_call(functools.partial(slots_kernel, group), out_shape=shapes,...]
    dynamic_update_slice x6 -> x0, local copies, waits for them, and re-layouts: 19.4 us -> none  [the longest x4 17.6 us: local(): lax.dynamic_update_slice(grad_ext, current + slot_grads[slot_no], corner)]
    slice x17 -> x3, local copies, waits for them, and re-layouts: 20.5 us -> 5.25 us  [the longest x1 2.27 us: local(): below = moved(object_slices[:, :, :width, :], 'row', up_one)]
    ppermute x4 -> x8, waiting for transfers between devices: 37.5 us -> 26.3 us  [moved(): return lax.ppermute(shard, axes, pairs)]
  transfers between devices with their start and end apart: 5 -> 10, of which waited for: 4 -> 4; matrix products, arithmetic and copies ran while one was open for 9% -> 7% of each run, Pallas kernels for 0% -> 0%
where the time goes in v1:
time: 151 us
  waiting for transfers between devices  57.5 us (38%)
  starting transfers between devices  52.9 us (35%)
  Pallas kernels  22.2 us (15%)
  local copies, waits for them, and re-layouts  9.33 us (6%)
  other arithmetic  7.86 us (5%)
    all_to_all x1, starting transfers between devices, total_over_devices(): lax.all_to_all(parts, ('row', 'col'), 0, 0, axis_index_groups=groups)  29.6 us
    ppermute x8, waiting for transfers between devices, moved(): return lax.ppermute(shard, axes, pairs)  26.3 us
    all_to_all x1, waiting for transfers between devices, total_over_devices(): mine = lax.all_to_all(share, ('row', 'col'), 0, 0, axis_index_groups=groups)  18.7 us
    ppermute x8, starting transfers between devices, moved(): return lax.ppermute(shard, axes, pairs)  18.7 us
    pallas_call x1, Pallas kernels, run_slots(): pl.pallas_call(functools.partial(slots_kernel, group), out_shape=shapes,...  16.2 us
    all_to_all x1, waiting for transfers between devices, total_over_devices(): lax.all_to_all(parts, ('row', 'col'), 0, 0, axis_index_groups=groups)  12.5 us
    pallas_call x1, Pallas kernels, orthogonalize(): pl.pallas_call(functools.partial(orthogonal_kernel, 1.0 / divisor), out_s...  5.97 us
    all_to_all x1, starting transfers between devices, total_over_devices(): mine = lax.all_to_all(share, ('row', 'col'), 0, 0, axis_index_groups=groups)  4.64 us
  transfers between devices with their start and end apart: 10, of which 4 were waited for; matrix products, arithmetic and copies ran while one was open for 7% of the time, Pallas kernels for 0%

profile of v1, /device:TPU:1, one launch (start us, length us, event | category | flops | bytes accessed | tf_op | source)
XLA Modules:
  0.0 151.2 jit_solution(4482973160844587392)
XLA Ops:
  0.6 1.3 slice.101
  1.9 1.3 collective-permute-start
  3.2 2.3 %slice.102 = f32[2,2,128,512]{3,2,1,0:T(8,128)} slice(f32[2,2,512,512]{3,2,1,0:T(8,128)} %tile.1), slice={[0:2], [0:2], [0:128], [0:512]} | slice | bytes 2097152 | tf_op jit(solution)/shard_map/slice | solution.py:427
  5.5 3.3 %collective-permute-start.1 = (f32[2,2,128,512]{3,2,1,0:T(8,128)}, f32[2,2,128,512]{3,2,1,0:T(8,128)S(1)}, u32[]{:S(2)}, u32[]{:S(2)}) collective-permute-start(f32[2,2,128,512]{3,2,1,0:T(8,128)} %slice.102), channel_id=1, source_target_pairs={{16,0},{32,16},{48,32},{64,48},{80,64},{96,80},{112,96},{17,1},{33... | collective-permute-start | bytes 3145736 | tf_op jit(solution)/shard_map/ppermute | solution.py:382
  8.8 1.7 %slice.103 = f32[2,2,128,128]{3,2,1,0:T(8,128)} slice(f32[2,2,512,512]{3,2,1,0:T(8,128)} %tile.1), slice={[0:2], [0:2], [0:128], [0:128]} | slice | bytes 524288 | tf_op jit(solution)/shard_map/slice | solution.py:429
  10.5 1.3 collective-permute-start.2
  12.5 24.1 %collective-permute-done.2.corner = f32[2,2,128,128]{3,2,1,0:T(8,128)S(1)} collective-permute-done((f32[2,2,128,128]{3,2,1,0:T(8,128)}, f32[2,2,128,128]{3,2,1,0:T(8,128)S(1)}, u32[]{:S(2)}, u32[]{:S(2)}) %collective-permute-start.2) | collective-permute-done | bytes 262176 | tf_op jit(solution)/shard_map/ppermute | solution.py:382
  36.5 0.0 copy-start.3
  36.5 0.0 collective-permute-done.right
  36.5 0.0 copy-start.1
  36.5 0.0 collective-permute-done.1.below
  36.5 0.0 copy-start.2
  36.5 0.7 copy-done.3
  37.2 0.3 copy-done.1
  37.6 0.4 copy-done.2
  37.9 16.2 %slots.1 = (f32[24,128,128]{2,1,0:T(8,128)}, f32[2,2,512,512]{3,2,1,0:T(8,128)}, f32[2,2,512,128]{3,2,1,0:T(8,128)}, f32[2,2,128,512]{3,2,1,0:T(8,128)}, f32[2,2,128,128]{3,2,1,0:T(8,128)}) custom-call(s32[1,1]{1,0:T(1,128)S(6)} %copy.11.count_ref, s32[2,4]{1,0:T(2,128)} %bitcast.22, f32[2,2,512,512]{3,2,1,0:T(8,128)} %tile.1, f32[2,2,512,128]{3,2,1,0:T(8,128)} %copy-done.1, ...), custom_call_target="tpu_custom_call" | custom-call | tf_op jit(solution)/shard_map/slots/pallas_call | solution.py:239
  54.1 0.0 copy-start.4
  54.1 1.2 dynamic-slice_bitcast_fusion
  55.4 0.1 collective-permute-start.6
  55.5 2.3 %collective-permute-done.6 = f32[1536,128]{1,0:T(8,128)S(1)} collective-permute-done((f32[1536,128]{1,0:T(8,128)S(1)}, f32[1536,128]{1,0:T(8,128)S(1)}, u32[]{:S(2)}, u32[]{:S(2)}) %collective-permute-start.6) | collective-permute-done | bytes 786464 | tf_op jit(solution)/shard_map/ppermute | solution.py:382
  57.7 2.1 %bitcast_add_fusion = f32[1536,128]{1,0:T(8,128)} fusion(f32[1536,128]{1,0:T(8,128)S(1)} %collective-permute-done.6, f32[2,1536,128]{2,1,0:T(8,128)} %bitcast.19, s32[]{:T(128)S(6)} %select_n.28), kind=kLoop, calls=%fused_computation.3 | loop fusion | flops 196608 | bytes 2359300 | tf_op jit(solution)/shard_map/add | solution.py:405
  59.8 29.6 %all-to-all-start = ((f32[64,24,128]{2,1,0:T(8,128)}), f32[64,24,128]{2,1,0:T(8,128)S(1)}, u32[]{:S(2)}, u32[]{:S(2)}) async-start(f32[64,24,128]{2,1,0:T(8,128)} %bitcast.6), calls=%async_computation | async-start | bytes 1572864 | tf_op jit(solution)/shard_map/all_to_all | solution.py:409
  89.4 3.0 %collective-permute-start.3 = (f32[2,2,512,128]{3,2,1,0:T(8,128)}, f32[2,2,512,128]{3,2,1,0:T(8,128)S(1)}, u32[]{:S(2)}, u32[]{:S(2)}) collective-permute-start(f32[2,2,512,128]{3,2,1,0:T(8,128)} %get-tuple-element.44), channel_id=1, source_target_pairs={{0,1},{1,2},{2,3},{3,4},{4,5},{5,6},{6,7},{7,8},{8,9},{9,10},{10,1... | collective-permute-start | bytes 3145736 | tf_op jit(solution)/shard_map/ppermute | solution.py:382
  92.4 12.5 %all-to-all-done = f32[64,24,128]{2,1,0:T(8,128)S(1)} async-done(((f32[64,24,128]{2,1,0:T(8,128)}), f32[64,24,128]{2,1,0:T(8,128)S(1)}, u32[]{:S(2)}, u32[]{:S(2)}) %all-to-all-start) | async-done | bytes 786464 | tf_op jit(solution)/shard_map/all_to_all | solution.py:409
  104.9 0.1 reduce_sum.9
  105.0 0.9 broadcast_in_dim.2
  105.9 4.6 %all-to-all-start.1 = ((f32[64,24,128]{2,1,0:T(8,128)}), f32[64,24,128]{2,1,0:T(8,128)S(1)}, u32[]{:S(2)}, u32[]{:S(2)}) async-start(f32[64,24,128]{2,1,0:T(8,128)} %broadcast_in_dim.2), calls=%async_computation.1 | async-start | bytes 1572864 | tf_op jit(solution)/shard_map/all_to_all | solution.py:412
  110.6 5.4 %collective-permute-start.4 = (f32[2,2,128,512]{3,2,1,0:T(8,128)}, f32[2,2,128,512]{3,2,1,0:T(8,128)S(1)}, u32[]{:S(2)}, u32[]{:S(2)}) collective-permute-start(f32[2,2,128,512]{3,2,1,0:T(8,128)} %get-tuple-element.45), channel_id=1, source_target_pairs={{0,16},{16,32},{32,48},{48,64},{64,80},{80,96},{96,112},{1,17},{17... | collective-permute-start | bytes 3145736 | tf_op jit(solution)/shard_map/ppermute | solution.py:382
  116.0 0.0 copy-done.4
  116.0 2.8 %collective-permute-start.5 = (f32[2,2,128,128]{3,2,1,0:T(8,128)S(1)}, f32[2,2,128,128]{3,2,1,0:T(8,128)S(1)}, u32[]{:S(2)}, u32[]{:S(2)}) collective-permute-start(f32[2,2,128,128]{3,2,1,0:T(8,128)S(1)} %copy-done.4), channel_id=1, source_target_pairs={{0,17},{1,18},{2,19},{3,20},{4,21},{5,22},{6,23},{7,24},{8,25},{9,... | collective-permute-start | bytes 786440 | tf_op jit(solution)/shard_map/ppermute | solution.py:382
  118.9 18.7 %all-to-all-done.1 = f32[64,24,128]{2,1,0:T(8,128)S(1)} async-done(((f32[64,24,128]{2,1,0:T(8,128)}), f32[64,24,128]{2,1,0:T(8,128)S(1)}, u32[]{:S(2)}, u32[]{:S(2)}) %all-to-all-start.1) | async-done | bytes 786464 | tf_op jit(solution)/shard_map/all_to_all | solution.py:412
  137.6 1.4 collective-permute-start.7
  139.0 0.0 collective-permute-done.3
  139.0 2.3 %add_dynamic-update-slice_fusion = f32[2,2,512,512]{3,2,1,0:T(8,128)} fusion(f32[2,2,512,512]{3,2,1,0:T(8,128)} %get-tuple-element.43, f32[2,2,512,128]{3,2,1,0:T(8,128)S(1)} %collective-permute-done.3), kind=kLoop, calls=%fused_computation.2 | loop fusion | flops 262144 | bytes 3145728 | tf_op jit(solution)/shard_map/scatter-add | solution.py:438
  141.3 0.0 collective-permute-done.4
  141.3 2.4 %constant_dynamic-update-slice_fusion = (f32[2,2,512,512]{3,2,1,0:T(8,128)}, f32[2,2,128,512]{3,2,1,0:T(8,128)S(1)}) fusion(f32[2,2,512,512]{3,2,1,0:T(8,128)} %add_dynamic-update-slice_fusion, f32[2,2,128,512]{3,2,1,0:T(8,128)S(1)} %collective-permute-done.4), kind=kLoop, calls=%fused_computation.9 | loop fusion | flops 262144 | bytes 4194304 | tf_op jit(solution)/shard_map/scatter-add | solution.py:439
  143.8 0.0 copy-start
  143.8 0.0 collective-permute-done.5
  143.8 0.7 fusion
  144.5 0.0 collective-permute-done.7
  144.5 0.1 broadcast_select_fusion.1
  144.6 0.1 pad_maximum_fusion
  144.7 0.5 copy-done
  145.3 6.0 %orthogonalize.1 = f32[24,128,128]{2,1,0:T(8,128)} custom-call(f32[24,128,128]{2,1,0:T(8,128)S(1)} %bitcast.15, f32[24,128,128]{2,1,0:T(8,128)S(1)} %bitcast.16), custom_call_target="tpu_custom_call" | custom-call | tf_op jit(solution)/shard_map/orthogonalize/pallas_call | solution.py:365
Async XLA Ops:
  1.9 34.6 %collective-permute-start = (f32[2,2,512,128]{3,2,1,0:T(8,128)S(1)}, f32[2,2,512,128]{3,2,1,0:T(8,128)S(1)}, u32[]{:S(2)}, u32[]{:S(2)}) collective-permute-start(f32[2,2,512,128]{3,2,1,0:T(8,128)S(1)} %slice.101), channel_id=1, source_target_pairs={{1,0},{2,1},{3,2},{4,3},{5,4},{6,5},{7,6},{8,7},{9,8},{10,9},{11,1... | collective-permute-start | bytes 3145736 | tf_op jit(solution)/shard_map/ppermute | solution.py:382
  5.5 31.0 %collective-permute-start.1 = (f32[2,2,128,512]{3,2,1,0:T(8,128)}, f32[2,2,128,512]{3,2,1,0:T(8,128)S(1)}, u32[]{:S(2)}, u32[]{:S(2)}) collective-permute-start(f32[2,2,128,512]{3,2,1,0:T(8,128)} %slice.102), channel_id=1, source_target_pairs={{16,0},{32,16},{48,32},{64,48},{80,64},{96,80},{112,96},{17,1},{33... | collective-permute-start | bytes 3145736 | tf_op jit(solution)/shard_map/ppermute | solution.py:382
  10.5 26.0 %collective-permute-start.2 = (f32[2,2,128,128]{3,2,1,0:T(8,128)}, f32[2,2,128,128]{3,2,1,0:T(8,128)S(1)}, u32[]{:S(2)}, u32[]{:S(2)}) collective-permute-start(f32[2,2,128,128]{3,2,1,0:T(8,128)} %slice.103), channel_id=1, source_target_pairs={{17,0},{18,1},{19,2},{20,3},{21,4},{22,5},{23,6},{24,7},{25,8},{26... | collective-permute-start | bytes 786440 | tf_op jit(solution)/shard_map/ppermute | solution.py:382
  36.5 0.7 copy-start.3
  36.5 1.0 copy-start.1
  36.5 1.4 copy-start.2
  54.1 61.9 %copy-start.4 = (f32[2,2,128,128]{3,2,1,0:T(8,128)S(1)}, f32[2,2,128,128]{3,2,1,0:T(8,128)}, u32[]{:S(2)}) copy-start(f32[2,2,128,128]{3,2,1,0:T(8,128)} %get-tuple-element.46) | copy-start | bytes 786436
  55.4 2.4 %collective-permute-start.6 = (f32[1536,128]{1,0:T(8,128)S(1)}, f32[1536,128]{1,0:T(8,128)S(1)}, u32[]{:S(2)}, u32[]{:S(2)}) collective-permute-start(f32[1536,128]{1,0:T(8,128)S(1)} %dynamic-slice_bitcast_fusion), channel_id=1, source_target_pairs={{0,16},{16,0},{32,48},{48,32},{64,80},{80,64},{96,112},{112,96},{1... | collective-permute-start | bytes 2359304 | tf_op jit(solution)/shard_map/ppermute | solution.py:382
  59.8 45.1 %all-to-all-start = ((f32[64,24,128]{2,1,0:T(8,128)}), f32[64,24,128]{2,1,0:T(8,128)S(1)}, u32[]{:S(2)}, u32[]{:S(2)}) async-start(f32[64,24,128]{2,1,0:T(8,128)} %bitcast.6), calls=%async_computation | async-start | bytes 1572864 | tf_op jit(solution)/shard_map/all_to_all | solution.py:409
  89.4 49.6 %collective-permute-start.3 = (f32[2,2,512,128]{3,2,1,0:T(8,128)}, f32[2,2,512,128]{3,2,1,0:T(8,128)S(1)}, u32[]{:S(2)}, u32[]{:S(2)}) collective-permute-start(f32[2,2,512,128]{3,2,1,0:T(8,128)} %get-tuple-element.44), channel_id=1, source_target_pairs={{0,1},{1,2},{2,3},{3,4},{4,5},{5,6},{6,7},{7,8},{8,9},{9,10},{10,1... | collective-permute-start | bytes 3145736 | tf_op jit(solution)/shard_map/ppermute | solution.py:382
  105.9 31.7 %all-to-all-start.1 = ((f32[64,24,128]{2,1,0:T(8,128)}), f32[64,24,128]{2,1,0:T(8,128)S(1)}, u32[]{:S(2)}, u32[]{:S(2)}) async-start(f32[64,24,128]{2,1,0:T(8,128)} %broadcast_in_dim.2), calls=%async_computation.1 | async-start | bytes 1572864 | tf_op jit(solution)/shard_map/all_to_all | solution.py:412
  110.6 30.8 %collective-permute-start.4 = (f32[2,2,128,512]{3,2,1,0:T(8,128)}, f32[2,2,128,512]{3,2,1,0:T(8,128)S(1)}, u32[]{:S(2)}, u32[]{:S(2)}) collective-permute-start(f32[2,2,128,512]{3,2,1,0:T(8,128)} %get-tuple-element.45), channel_id=1, source_target_pairs={{0,16},{16,32},{32,48},{48,64},{64,80},{80,96},{96,112},{1,17},{17... | collective-permute-start | bytes 3145736 | tf_op jit(solution)/shard_map/ppermute | solution.py:382
  116.0 27.8 %collective-permute-start.5 = (f32[2,2,128,128]{3,2,1,0:T(8,128)S(1)}, f32[2,2,128,128]{3,2,1,0:T(8,128)S(1)}, u32[]{:S(2)}, u32[]{:S(2)}) collective-permute-start(f32[2,2,128,128]{3,2,1,0:T(8,128)S(1)} %copy-done.4), channel_id=1, source_target_pairs={{0,17},{1,18},{2,19},{3,20},{4,21},{5,22},{6,23},{7,24},{8,25},{9,... | collective-permute-start | bytes 786440 | tf_op jit(solution)/shard_map/ppermute | solution.py:382
  137.6 6.9 %collective-permute-start.7 = (f32[1536,128]{1,0:T(8,128)S(1)}, f32[1536,128]{1,0:T(8,128)S(1)}, u32[]{:S(2)}, u32[]{:S(2)}) collective-permute-start(f32[1536,128]{1,0:T(8,128)S(1)} %bitcast.17), channel_id=1, source_target_pairs={{0,16},{16,0},{32,48},{48,32},{64,80},{80,64},{96,112},{112,96},{1... | collective-permute-start | bytes 2359304 | tf_op jit(solution)/shard_map/ppermute | solution.py:382
  143.8 1.5 copy-start

commit v2 on v1

v2 whole, which is shorter than its diff:
```python
import functools
import math

import jax
import jax.numpy as jnp
import numpy as np
from jax import lax
from jax.experimental import pallas as pl
from jax.experimental.pallas import tpu as pltpu
from jax.sharding import PartitionSpec as P

FRESNEL = 40.0
f32 = jnp.float32
bf16 = jnp.bfloat16


def complex_block(matrix):
    return np.block([[matrix.real, matrix.imag], [-matrix.imag, matrix.real]])


def split_table(block):
    block = block.astype(np.float32)
    high = block.astype(jnp.bfloat16)
    low = (block - high.astype(np.float32)).astype(jnp.bfloat16)
    return np.stack([high, low])


def make_tables(width):
    index = np.arange(width)
    fourier = np.exp(-2j * np.pi / width * (index[:, None] * index[None, :] % width)) / np.sqrt(width)
    frequency = np.where(index < width // 2, index, index - width) / width
    chirp = np.exp(-1j * FRESNEL * frequency**2)
    spread = fourier.conj() @ (chirp[:, None] * fourier)
    forward = complex_block(fourier)
    step = complex_block(spread)
    steps = np.stack([split_table(step), split_table(step.T)])
    transforms = np.stack([split_table(forward), split_table(forward.T)])
    return steps, transforms


def split(values):
    high = values.astype(bf16)
    low = (values - high.astype(f32)).astype(bf16)
    return high, low


def mm(left, right):
    return jnp.dot(left, right, preferred_element_type=f32)


def times_right(planes, table):
    a_re, a_im, b_re, b_im = planes
    stacked = jnp.concatenate(
        [jnp.concatenate([a_re, a_im], axis=1), jnp.concatenate([b_re, b_im], axis=1)], axis=0
    )
    high, low = split(stacked)
    out = mm(high, table[0]) + mm(low, table[0]) + mm(high, table[1])
    w = a_re.shape[0]
    return out[:w, :w], out[:w, w:], out[w:, :w], out[w:, w:]


def times_left(planes, table):
    a_re, a_im, b_re, b_im = planes
    stacked = jnp.concatenate(
        [jnp.concatenate([a_re, b_re], axis=1), jnp.concatenate([a_im, b_im], axis=1)], axis=0
    )
    high, low = split(stacked)
    out = mm(table[0], high) + mm(table[0], low) + mm(table[1], high)
    w = a_re.shape[0]
    return out[:w, :w], out[w:, :w], out[:w, w:], out[w:, w:]


def cmul(planes, re, im):
    a_re, a_im, b_re, b_im = planes
    return (
        a_re * re - a_im * im,
        a_re * im + a_im * re,
        b_re * re - b_im * im,
        b_re * im + b_im * re,
    )


def cmul_conj(planes, re, im):
    a_re, a_im, b_re, b_im = planes
    return (
        a_re * re + a_im * im,
        a_im * re - a_re * im,
        b_re * re + b_im * im,
        b_im * re - b_re * im,
    )


def overlap(wave, grad):
    re = wave[0] * grad[0] + wave[1] * grad[1] + wave[2] * grad[2] + wave[3] * grad[3]
    im = wave[0] * grad[1] - wave[1] * grad[0] + wave[2] * grad[3] - wave[3] * grad[2]
    return re, im


RIGHT, LEFT = 0, 1


def load_sheet(tile, halo, sheet, sems, width):
    rows, cols = tile.shape[2:]
    top, rest, below_first, below_second, corner = halo
    half = rows // 2
    spots = [
        (tile, sheet, 0, rows, 0, cols),
        (top, sheet, 0, half, cols, width),
        (rest, sheet, half, half, cols, width),
        (below_first, sheet.at[pl.ds(0, 1)], rows, width, 0, cols),
        (below_second, sheet.at[pl.ds(1, 1)], rows, width, 0, cols),
        (corner, sheet, rows, width, cols, width),
    ]
    copies = [
        pltpu.make_async_copy(src, dst.at[:, :, pl.ds(r, h), pl.ds(c, w)], sems.at[i])
        for i, (src, dst, r, h, c, w) in enumerate(spots)
    ]
    for copy in copies:
        copy.start()
    return copies


def corner_of(pos_ref, slot, width):
    top = pos_ref[0, slot]
    left = pos_ref[1, slot]
    top8 = pl.multiple_of((top // 8) * 8, 8)
    left128 = pl.multiple_of((left // width) * width, width)
    return top8, left128, top - top8, left - left128


def cut_window(sheet, layer, plane, corner, width):
    top8, left128, drop_r, drop_c = corner
    wide = sheet[layer, plane, pl.ds(top8, width + 8), pl.ds(left128, 2 * width)]
    wide = pltpu.roll(wide, 2 * width - drop_c, 1)[:, :width]
    return pltpu.roll(wide, width + 8 - drop_r, 0)[:width]


def load4(ref, pair):
    return tuple(ref[pair * 4 + i] for i in range(4))


def store4(ref, pair, values):
    for i in range(4):
        ref[pair * 4 + i] = values[i]


def subtract_terms(slot, pos_ref, terms, sheet, width):
    top8, left128, drop_r, drop_c = corner_of(pos_ref, slot, width)
    for s in range(2):
        for c in range(2):
            wide = jnp.concatenate([terms[slot, s, c], jnp.zeros((8, width), f32)], axis=0)
            wide = pltpu.roll(wide, drop_r, 0)
            wide = jnp.concatenate([wide, jnp.zeros_like(wide)], axis=1)
            wide = pltpu.roll(wide, drop_c, 1)
            where = (s, c, pl.ds(top8, width + 8), pl.ds(left128, 2 * width))
            sheet[where] = sheet[where] - wide


def slots_kernel(
    count_ref, pos_ref, core_ref, tile, top, rest, below_first, below_second, corner,
    probe_in, pattern_in, step_in, transform_in,
    keep_out, give_out, term_out, right_top_out, right_rest_out, below_first_out, below_second_out,
    corner_out,
    sheet, outer, probe, patterns, steps, transforms, window, wave, far, inten, pgrad, terms,
    sem_in, sem_load, sem_term, sem_out,
):
    rows, cols = tile.shape[2:]
    width = probe.shape[-1]
    planes = probe.shape[0]
    pairs = planes // 4
    count = count_ref[0, 0]
    copies = load_sheet(tile, (top, rest, below_first, below_second, corner), sheet, sem_in, width)
    loads = [
        pltpu.make_async_copy(src, dst, sem_load.at[i])
        for i, (src, dst) in enumerate(
            [(probe_in, probe), (step_in, steps), (transform_in, transforms), (pattern_in, patterns)]
        )
    ]
    for copy in loads:
        copy.start()

    def save(slot):
        return pltpu.make_async_copy(terms.at[slot], term_out.at[slot], sem_term.at[slot])

    pgrad[...] = jnp.zeros_like(pgrad)
    outer[:, :, 0 : rows + width, cols : cols + width] = jnp.zeros((2, 2, rows + width, width), f32)
    outer[:, :, rows : rows + width, 0:cols] = jnp.zeros((2, 2, width, cols), f32)
    for copy in copies + loads:
        copy.wait()

    def visit(slot, carry):
        place = corner_of(pos_ref, slot, width)
        for s in range(2):
            for c in range(2):
                window[s, c] = cut_window(sheet, s, c, place, width)
        waves = [cmul(load4(probe, p), window[0, 0], window[0, 1]) for p in range(pairs)]
        waves = [times_right(v, steps[RIGHT]) for v in waves]
        waves = [times_left(v, steps[LEFT]) for v in waves]
        for p, v in enumerate(waves):
            store4(wave, p, v)
        waves = [cmul(v, window[1, 0], window[1, 1]) for v in waves]
        waves = [times_right(v, transforms[RIGHT]) for v in waves]
        waves = [times_left(v, transforms[LEFT]) for v in waves]
        total = -patterns[slot]
        for p, v in enumerate(waves):
            store4(far, p, v)
            total = total + (v[0] * v[0] + v[1] * v[1] + v[2] * v[2] + v[3] * v[3])
        inten[...] = total

        residual = inten[...]
        grads = [tuple(residual * x for x in load4(far, p)) for p in range(pairs)]
        grads = [times_right(v, transforms[LEFT]) for v in grads]
        grads = [times_left(v, transforms[RIGHT]) for v in grads]
        products = [overlap(load4(wave, p), v) for p, v in enumerate(grads)]
        terms[slot, 1, 0] = sum(t[0] for t in products)
        terms[slot, 1, 1] = sum(t[1] for t in products)
        grads = [cmul_conj(v, window[1, 0], window[1, 1]) for v in grads]
        grads = [times_right(v, steps[LEFT]) for v in grads]
        grads = [times_left(v, steps[RIGHT]) for v in grads]
        products = [overlap(load4(probe, p), v) for p, v in enumerate(grads)]
        terms[slot, 0, 0] = sum(t[0] for t in products)
        terms[slot, 0, 1] = sum(t[1] for t in products)
        grads = [cmul_conj(v, window[0, 0], window[0, 1]) for v in grads]
        for p, v in enumerate(grads):
            for i in range(4):
                pgrad[p * 4 + i] += v[i]
        save(slot).start()
        leaves = (pos_ref[0, slot] > rows - width) | (pos_ref[1, slot] > cols - width)

        @pl.when(leaves)
        def _():
            subtract_terms(slot, pos_ref, terms, outer, width)

        return carry

    def finish(slot, carry):
        save(slot).wait()
        return carry

    lax.fori_loop(0, count, visit, 0)
    half = planes // 2
    core = core_ref[0, 0]
    middle = rows // 2
    down, across = pl.ds(rows, width), pl.ds(cols, width)
    results = [
        (pgrad.at[pl.ds((1 - core) * half, half)], give_out),
        (pgrad.at[pl.ds(core * half, half)], keep_out),
        (outer.at[:, :, down, across], corner_out),
        (outer.at[:, :, pl.ds(middle, middle), across], right_rest_out),
        (outer.at[:, :, pl.ds(0, middle), across], right_top_out),
        (outer.at[pl.ds(0, 1), :, down, pl.ds(0, cols)], below_first_out),
        (outer.at[pl.ds(1, 1), :, down, pl.ds(0, cols)], below_second_out),
    ]
    stores = [
        pltpu.make_async_copy(src, dst, sem_out.at[i]) for i, (src, dst) in enumerate(results)
    ]
    for copy in stores:
        copy.start()
    lax.fori_loop(0, count, finish, 0)
    for copy in stores:
        copy.wait()


def load_terms(count, term_in, terms, sems):
    def fetch(slot):
        return pltpu.make_async_copy(term_in.at[slot], terms.at[slot], sems.at[slot])

    def begin(slot, carry):
        fetch(slot).start()
        return carry

    def finish(slot, carry):
        fetch(slot).wait()
        return carry

    lax.fori_loop(0, count, begin, 0)
    return lambda: lax.fori_loop(0, count, finish, 0)


def settle_kernel(
    count_ref, pos_ref, tile, term_in, left_top_in, left_rest_in, above_first_in, above_second_in, tile_out,
    sheet, terms, left, above, sem_term, sem_in, sem_out,
):
    width = above_first_in.shape[2]
    rows, cols = tile.shape[2:]
    middle = rows // 2
    count = count_ref[0, 0]
    inner = sheet.at[:, :, pl.ds(0, rows), pl.ds(0, cols)]
    sources = [
        (tile, inner),
        (left_top_in, left.at[:, :, pl.ds(0, middle)]),
        (left_rest_in, left.at[:, :, pl.ds(middle, middle)]),
        (above_first_in, above.at[pl.ds(0, 1)]),
        (above_second_in, above.at[pl.ds(1, 1)]),
    ]
    loads = [
        pltpu.make_async_copy(src, dst, sem_in.at[i]) for i, (src, dst) in enumerate(sources)
    ]
    for copy in loads:
        copy.start()
    wait = load_terms(count, term_in, terms, sem_term)
    for copy in loads:
        copy.wait()
    wait()
    sheet[:, :, 0:rows, 0:width] += left[...]
    sheet[:, :, 0:width, 0:cols] += above[...]

    def visit(slot, carry):
        subtract_terms(slot, pos_ref, terms, sheet, width)
        return carry

    lax.fori_loop(0, count, visit, 0)
    store = pltpu.make_async_copy(inner, tile_out, sem_out.at[0])
    store.start()
    store.wait()


VMEM = pl.BlockSpec(memory_space=pltpu.VMEM)
SMEM = pl.BlockSpec(memory_space=pltpu.SMEM)
ANY = pl.BlockSpec(memory_space=pl.ANY)
DMA = pltpu.SemaphoreType.DMA


def shape(*dims):
    return jax.ShapeDtypeStruct(dims, f32)


def params(mib):
    return pltpu.CompilerParams(vmem_limit_bytes=mib * 1024 * 1024)


def work(products):
    return pl.CostEstimate(
        flops=products * 2 * 256**3, bytes_accessed=8 * 1024 * 1024, transcendentals=0
    )


def run_slots(counts, positions, core, tile, halo, probe, patterns):
    planes, width = probe.shape[0], probe.shape[-1]
    rows, cols = tile.shape[2:]
    capacity = positions.shape[1]
    half = (planes // 2, width, width)
    stack = pltpu.VMEM(probe.shape, f32)
    steps, transforms = make_tables(width)
    return pl.pallas_call(
        slots_kernel,
        out_shape=[
            shape(*half),
            shape(*half),
            shape(capacity, 2, 2, width, width),
            shape(2, 2, rows // 2, width),
            shape(2, 2, rows // 2, width),
            shape(1, 2, width, cols),
            shape(1, 2, width, cols),
            shape(2, 2, width, width),
        ],
        in_specs=[SMEM, SMEM, SMEM] + [ANY] * 10,
        out_specs=[ANY] * 8,
        scratch_shapes=[
            pltpu.VMEM((2, 2, rows + width + 8, cols + 2 * width), f32),
            pltpu.VMEM((2, 2, rows + width + 8, cols + 2 * width), f32),
            stack,
            pltpu.VMEM(patterns.shape, f32),
            pltpu.VMEM(steps.shape, bf16),
            pltpu.VMEM(transforms.shape, bf16),
            pltpu.VMEM((2, 2, width, width), f32),
            stack,
            stack,
            pltpu.VMEM((width, width), f32),
            stack,
            pltpu.VMEM((capacity, 2, 2, width, width), f32),
            DMA((6,)),
            DMA((4,)),
            DMA((capacity,)),
            DMA((7,)),
        ],
        compiler_params=params(60),
        cost_estimate=work(4 * capacity * planes),
        name="slots",
    )(counts, positions, core, tile, *halo, probe, patterns, steps, transforms)


def settle(counts, positions, tile, terms, left, above):
    capacity, width = terms.shape[0], terms.shape[-1]
    rows, cols = tile.shape[2:]
    return pl.pallas_call(
        settle_kernel,
        out_shape=shape(*tile.shape),
        in_specs=[SMEM, SMEM] + [ANY] * 6,
        out_specs=ANY,
        scratch_shapes=[
            pltpu.VMEM((2, 2, rows + width + 8, cols + 2 * width), f32),
            pltpu.VMEM(terms.shape, f32),
            pltpu.VMEM((2, 2, rows, width), f32),
            pltpu.VMEM((2, 2, width, cols), f32),
            DMA((capacity,)),
            DMA((5,)),
            DMA((1,)),
        ],
        compiler_params=params(60),
        cost_estimate=work(4096),
        name="settle",
    )(counts, positions, tile, terms, *left, *above)


def core_groups(rows, cols, split):
    return [
        [r * cols + c for r in range(part, rows, split) for c in range(cols)]
        for part in range(split)
    ]


def orthogonal_kernel(
    scale, core_ref, probe_ref, mine, other, out_ref, total, stepped, sums, gram, coef, sem
):
    planes, width = probe_ref.shape[0], probe_ref.shape[-1]
    half = planes // 2
    core = core_ref[0, 0]
    loads = [
        pltpu.make_async_copy(mine, total.at[pl.ds(core * half, half)], sem.at[0]),
        pltpu.make_async_copy(other, total.at[pl.ds((1 - core) * half, half)], sem.at[1]),
    ]
    for copy in loads:
        copy.start()
    for copy in loads:
        copy.wait()
    modes = planes // 2
    sub = 8
    chunks = width // sub
    stepped[...] = probe_ref[...] - total[...] * scale

    block = 3
    sums[...] = jnp.zeros_like(sums)
    for jb in range(0, modes, block):
        for kb in range(jb, modes, block):
            pairs = [
                (j, k) for j in range(jb, jb + block) for k in range(kb, kb + block) if j <= k
            ]

            def accumulate(chunk, carried):
                rows = pl.ds(pl.multiple_of(chunk * sub, sub), sub)
                left = {j: (stepped[2 * j, rows], stepped[2 * j + 1, rows]) for j in range(jb, jb + block)}
                right = {k: (stepped[2 * k, rows], stepped[2 * k + 1, rows]) for k in range(kb, kb + block)}
                out = []
                for (j, k), (acc_re, acc_im) in zip(pairs, carried):
                    (l_re, l_im), (r_re, r_im) = left[j], right[k]
                    out.append(
                        (
                            acc_re + l_re * r_re + l_im * r_im,
                            acc_im + l_re * r_im - l_im * r_re,
                        )
                    )
                return out

            zero = jnp.zeros((sub, width), f32)
            result = lax.fori_loop(
                0, chunks, accumulate, [(zero, zero) for _ in pairs], unroll=4
            )
            for (j, k), (acc_re, acc_im) in zip(pairs, result):
                s_re = jnp.sum(acc_re, axis=0, keepdims=True)
                s_im = jnp.sum(acc_im, axis=0, keepdims=True)
                sums[0, j, k : k + 1] = s_re
                sums[1, j, k : k + 1] = s_im
                if j != k:
                    sums[0, k, j : j + 1] = s_re
                    sums[1, k, j : j + 1] = -s_im
    side = sums.shape[1]
    ones = jnp.ones((sub, width), f32)
    for part in range(2):
        for j in range(modes):
            row = lax.dot_general(
                ones, sums[part, j], (((1,), (1,)), ((), ())),
                precision=lax.Precision.HIGHEST, preferred_element_type=f32,
            )
            gram[part, j : j + 1, 0:side] = row[0:1]

    row_id = lax.broadcasted_iota(jnp.int32, (side, width), 0)
    lane_id = lax.broadcasted_iota(jnp.int32, (side, width), 1)
    valid = (row_id < modes) & (lane_id < modes)
    eye = jnp.where((lane_id == row_id + side) & (row_id < modes), 1.0, 0.0)
    work_re = jnp.where(valid, gram[0], 0.0) + eye
    work_im = jnp.where(valid, gram[1], 0.0)
    for k in range(modes - 1):
        row_re = work_re[k : k + 1]
        row_im = work_im[k : k + 1]
        inverse = 1.0 / work_re[k : k + 1, k : k + 1]
        f_re = jnp.where(row_id[:, :1] > k, work_re[:, k : k + 1] * inverse, 0.0)
        f_im = jnp.where(row_id[:, :1] > k, work_im[:, k : k + 1] * inverse, 0.0)
        work_re, work_im = (
            work_re - (f_re * row_re - f_im * row_im),
            work_im - (f_re * row_im + f_im * row_re),
        )
    place = 0
    for k in range(modes):
        for j in range(k):
            coef[place] = jnp.broadcast_to(work_re[k : k + 1, side + j : side + j + 1], (sub, width))
            coef[place + 1] = jnp.broadcast_to(work_im[k : k + 1, side + j : side + j + 1], (sub, width))
            place += 2

    def combine(chunk, carry):
        rows = pl.ds(pl.multiple_of(chunk * sub, sub), sub)
        values = [stepped[i, rows] for i in range(planes)]
        place = 0
        for k in range(modes):
            acc_re, acc_im = values[2 * k], values[2 * k + 1]
            for j in range(k):
                c_re, c_im = coef[place], coef[place + 1]
                place += 2
                acc_re = acc_re + (c_re * values[2 * j] + c_im * values[2 * j + 1])
                acc_im = acc_im + (c_re * values[2 * j + 1] - c_im * values[2 * j])
            out_ref[2 * k, rows] = acc_re
            out_ref[2 * k + 1, rows] = acc_im
        return carry

    lax.fori_loop(0, chunks, combine, 0)


def orthogonalize(core, probe, mine, other, divisor):
    planes, width = probe.shape[0], probe.shape[-1]
    modes = planes // 2
    side = 16
    return pl.pallas_call(
        functools.partial(orthogonal_kernel, 1.0 / divisor),
        out_shape=shape(*probe.shape),
        in_specs=[SMEM, VMEM, ANY, ANY],
        out_specs=VMEM,
        scratch_shapes=[
            pltpu.VMEM(probe.shape, f32),
            pltpu.VMEM(probe.shape, f32),
            pltpu.VMEM((2, side, side, width), f32),
            pltpu.VMEM((2, side, width), f32),
            pltpu.VMEM((modes * (modes - 1), 8, width), f32),
            DMA((2,)),
        ],
        compiler_params=params(32),
        name="orthogonalize",
    )(core, probe, mine, other)


def moved(shard, axes, pairs):
    return lax.ppermute(shard, axes, pairs)


def shifted(size, by):
    return [(i, i + by) for i in range(size) if 0 <= i + by < size]


def sum_share(keep, groups):
    members = len(groups[0])
    parts = keep.reshape(members, -1, keep.shape[-1])
    parts = lax.all_to_all(parts, ("row", "col"), 0, 0, axis_index_groups=groups)
    return jnp.sum(parts, axis=0)


def gather_shares(share, groups):
    members = len(groups[0])
    parts = jnp.broadcast_to(share[None], (members,) + share.shape)
    return lax.all_to_all(parts, ("row", "col"), 0, 0, axis_index_groups=groups)


def local(object_slices, probe, measured, positions, counts):
    rows, cols = lax.axis_size("row"), lax.axis_size("col")
    modes, width = probe.shape[0], probe.shape[-1]
    planes = probe.reshape(2 * modes, width, width)
    capacity = positions.shape[2]
    spots = positions[:, 0]
    core = (lax.axis_index("row") % 2).astype(jnp.int32).reshape(1, 1)
    left_one, right_one = shifted(cols, -1), shifted(cols, 1)
    up_one, down_one = shifted(rows, -1), shifted(rows, 1)
    swap = [(r, r ^ 1) for r in range(rows)]
    groups = core_groups(rows, cols, 2)

    middle = object_slices.shape[2] // 2
    top = moved(object_slices[:, :, :middle, :width], "col", left_one)
    rest = moved(object_slices[:, :, middle:, :width], "col", left_one)
    below = [moved(object_slices[s : s + 1, :, :width, :], "row", up_one) for s in range(2)]
    corner = moved(top[:, :, :width], "row", up_one)
    keep, give, terms, right_top, right_rest, *below_grads, corner_grad = run_slots(
        counts, spots, core, object_slices, (top, rest, *below, corner), planes, measured[0]
    )
    keep = keep + moved(give, "row", swap)
    left_rest = moved(right_rest, "col", right_one)
    right_top = right_top.at[:, :, :width].add(moved(corner_grad, "row", down_one))
    left_top = moved(right_top, "col", right_one)
    above = [moved(part, "row", down_one) for part in below_grads]
    share = sum_share(keep, groups)
    mine = gather_shares(share, groups).reshape(keep.shape)
    object_next = settle(counts, spots, object_slices, terms, (left_top, left_rest), above)
    mine, object_next = lax.optimization_barrier((mine, object_next))
    other = moved(mine, "row", swap)
    divisor = math.sqrt(rows * cols * capacity)
    probe_next = orthogonalize(core, planes, mine, other, divisor).reshape(probe.shape)
    return (object_next, probe_next)


def solution(mesh):
    return jax.shard_map(
        local,
        mesh=mesh,
        in_specs=(
            P(None, None, "row", "col"),
            P(),
            P("row", "col", None, None),
            P(None, "row", "col"),
            P("row", "col"),
        ),
        out_specs=(P(None, None, "row", "col"), P()),
        check_vma=False,
    )
```

time: 151 us -> 142 us (0.940); the launches traced: 151 us -> 139 us
  waiting for transfers between devices: 57.5 us -> 45.2 us
  starting transfers between devices: 52.9 us -> 59.3 us
  local copies, waits for them, and re-layouts: 9.33 us -> 4.36 us
  other arithmetic: 7.86 us -> 3.87 us
  Pallas kernels: 22.2 us -> 25 us
    all_to_all x2, waiting for transfers between devices: 31.2 us -> 13.2 us  [the longest x1 10 us: gather_shares(): return lax.all_to_all(parts, ('row', 'col'), 0, 0, axis_index_groups=groups)]
    ppermute x8 -> x12, starting transfers between devices: 18.7 us -> 31.8 us  [moved(): return lax.ppermute(shard, axes, pairs)]
    all_to_all x2, starting transfers between devices: 34.2 us -> 27.5 us  [the longest x1 21.5 us: sum_share(): lax.all_to_all(parts, ('row', 'col'), 0, 0, axis_index_groups=groups)]
    ppermute x8 -> x12, waiting for transfers between devices: 26.3 us -> 32.1 us  [moved(): return lax.ppermute(shard, axes, pairs)]
    scatter-add x3 -> x1, other arithmetic: 5.47 us -> 1.69 us  [local(): right_top.at[:, :, :width].add(moved(corner_grad, 'row', down_one))]
    pallas_call x1 -> x2, Pallas kernels: 16.2 us -> 18.9 us  [the longest x1 12.7 us: run_slots(): pl.pallas_call(slots_kernel, out_shape=[shape(*half), shape(*half), shape...]
    slice x3, local copies, waits for them, and re-layouts: 5.25 us -> 2.6 us  [the longest x1 1.3 us: local(): rest = moved(object_slices[:, :, middle:, :width], 'col', left_one)]
  transfers between devices with their start and end apart: 10 -> 14, of which waited for: 4 -> 6; matrix products, arithmetic and copies ran while one was open for 7% -> 4% of each run, Pallas kernels for 0% -> 4%
where the time goes in v2:
time: 142 us; the launch traced here: 139 us
  starting transfers between devices  59.3 us (42%)
  waiting for transfers between devices  45.2 us (32%)
  Pallas kernels  25 us (18%)
  local copies, waits for them, and re-layouts  4.36 us (3%)
  other arithmetic  3.87 us (3%)
  between operations  1.54 us (1%)
    ppermute x12, waiting for transfers between devices, moved(): return lax.ppermute(shard, axes, pairs)  32.1 us
    ppermute x12, starting transfers between devices, moved(): return lax.ppermute(shard, axes, pairs)  31.8 us
    all_to_all x1, starting transfers between devices, sum_share(): lax.all_to_all(parts, ('row', 'col'), 0, 0, axis_index_groups=groups)  21.5 us
    pallas_call x1, Pallas kernels, run_slots(): pl.pallas_call(slots_kernel, out_shape=[shape(*half), shape(*half), shape...  12.7 us
    all_to_all x1, waiting for transfers between devices, gather_shares(): return lax.all_to_all(parts, ('row', 'col'), 0, 0, axis_index_groups=groups)  10 us
    pallas_call x1, Pallas kernels, settle(): pl.pallas_call(settle_kernel, out_shape=shape(*tile.shape), in_specs=[SME...  6.11 us
    pallas_call x1, Pallas kernels, orthogonalize(): pl.pallas_call(functools.partial(orthogonal_kernel, 1.0 / divisor), out_s...  6.1 us
    all_to_all x1, starting transfers between devices, gather_shares(): return lax.all_to_all(parts, ('row', 'col'), 0, 0, axis_index_groups=groups)  6.01 us
  transfers between devices with their start and end apart: 14, of which 6 were waited for; matrix products, arithmetic and copies ran while one was open for 4% of the time, Pallas kernels for 4%

profile of v2, /device:TPU:1, one launch (start us, length us, event | category | flops | bytes accessed | tf_op | source)
XLA Modules:
  0.0 139.3 jit_solution(17980517053741543132)
XLA Ops:
  0.6 1.3 fusion.1
  1.9 1.3 collective-permute-start.1
  3.2 1.3 collective-permute-start
  4.5 1.3 fusion
  5.8 3.3 %collective-permute-start.3 = (f32[1,2,128,512]{3,2,1,0:T(8,128)S(1)}, f32[1,2,128,512]{3,2,1,0:T(8,128)S(1)}, u32[]{:S(2)}, u32[]{:S(2)}) collective-permute-start(f32[1,2,128,512]{3,2,1,0:T(8,128)S(1)} %get-tuple-element.34), channel_id=1, source_target_pairs={{16,0},{32,16},{48,32},{64,48},{80,64},{96,80},{112,96},{17,1},{33... | collective-permute-start | bytes 1572872 | tf_op jit(solution)/shard_map/ppermute | solution.py:541
  9.2 1.9 %collective-permute-start.2 = (f32[1,2,128,512]{3,2,1,0:T(8,128)S(1)}, f32[1,2,128,512]{3,2,1,0:T(8,128)}, u32[]{:S(2)}, u32[]{:S(2)}) collective-permute-start(f32[1,2,128,512]{3,2,1,0:T(8,128)S(1)} %get-tuple-element.35), channel_id=1, source_target_pairs={{16,0},{32,16},{48,32},{64,48},{80,64},{96,80},{112,96},{17,1},{33... | collective-permute-start | bytes 1572872 | tf_op jit(solution)/shard_map/ppermute | solution.py:541
  11.1 17.1 %collective-permute-done.top = f32[2,2,256,128]{3,2,1,0:T(8,128)S(1)} collective-permute-done((f32[2,2,256,128]{3,2,1,0:T(8,128)S(1)}, f32[2,2,256,128]{3,2,1,0:T(8,128)S(1)}, u32[]{:S(2)}, u32[]{:S(2)}) %collective-permute-start) | collective-permute-done | bytes 524320 | tf_op jit(solution)/shard_map/ppermute | solution.py:541
  28.2 0.0 copy-start.1
  28.3 3.7 %collective-permute-start.4 = (f32[2,2,128,128]{3,2,1,0:T(8,128)S(1)}, f32[2,2,128,128]{3,2,1,0:T(8,128)}, u32[]{:S(2)}, u32[]{:S(2)}) collective-permute-start(f32[2,2,128,128]{3,2,1,0:T(8,128)S(1)} %slice.50), channel_id=1, source_target_pairs={{16,0},{32,16},{48,32},{64,48},{80,64},{96,80},{112,96},{17,1},{33... | collective-permute-start | bytes 786440 | tf_op jit(solution)/shard_map/ppermute | solution.py:541
  32.6 0.0 collective-permute-done.1.rest
  32.6 0.0 copy-start.2
  32.6 0.0 collective-permute-done.3.below_second
  32.6 0.0 copy-start.3
  32.6 0.0 collective-permute-done.2.below_first
  32.6 5.2 %collective-permute-done.4.corner = f32[2,2,128,128]{3,2,1,0:T(8,128)} collective-permute-done((f32[2,2,128,128]{3,2,1,0:T(8,128)S(1)}, f32[2,2,128,128]{3,2,1,0:T(8,128)}, u32[]{:S(2)}, u32[]{:S(2)}) %collective-permute-start.4) | collective-permute-done | bytes 262176 | tf_op jit(solution)/shard_map/ppermute | solution.py:541
  37.8 0.0 copy-done.1
  37.9 0.0 copy-done.2
  37.9 0.0 copy-done.3
  37.9 12.7 %slots.1 = (f32[12,128,128]{2,1,0:T(8,128)}, f32[12,128,128]{2,1,0:T(8,128)}, f32[4,2,2,128,128]{4,3,2,1,0:T(8,128)}, f32[2,2,256,128]{3,2,1,0:T(8,128)}, f32[2,...) custom-call(s32[1,1]{1,0:T(1,128)S(6)} %copy.10.count_ref, ...), custom_call_target="tpu_custom_call" | custom-call | flops 12884901888 | bytes 8388608 | tf_op jit(solution)/shard_map/slots/pallas_call | solution.py:345
  50.6 0.1 collective-permute-start.5
  50.7 7.7 %collective-permute-start.6 = (f32[2,2,128,128]{3,2,1,0:T(8,128)}, f32[2,2,128,128]{3,2,1,0:T(8,128)S(1)}, u32[]{:S(2)}, u32[]{:S(2)}) collective-permute-start(f32[2,2,128,128]{3,2,1,0:T(8,128)} %get-tuple-element.28), channel_id=1, source_target_pairs={{0,16},{16,32},{32,48},{48,64},{64,80},{80,96},{96,112},{1,17},{17... | collective-permute-start | bytes 786440 | tf_op jit(solution)/shard_map/ppermute | solution.py:541
  58.4 0.0 collective-permute-done.5
  58.4 2.1 %add.15 = f32[12,128,128]{2,1,0:T(8,128)} add(f32[12,128,128]{2,1,0:T(8,128)} %get-tuple-element.24, f32[12,128,128]{2,1,0:T(8,128)S(1)} %collective-permute-done.5) | non-fusion elementwise | flops 196608 | bytes 2359296 | tf_op jit(solution)/shard_map/add | solution.py:581
  60.5 21.5 %all-to-all-start = ((f32[64,24,128]{2,1,0:T(8,128)}), f32[64,24,128]{2,1,0:T(8,128)S(1)}, u32[]{:S(2)}, u32[]{:S(2)}) async-start(f32[64,24,128]{2,1,0:T(8,128)} %bitcast.4), calls=%async_computation | async-start | bytes 1572864 | tf_op jit(solution)/shard_map/all_to_all | solution.py:551
  82.0 2.9 %collective-permute-start.8 = (f32[2,2,256,128]{3,2,1,0:T(8,128)}, f32[2,2,256,128]{3,2,1,0:T(8,128)S(1)}, u32[]{:S(2)}, u32[]{:S(2)}) collective-permute-start(f32[2,2,256,128]{3,2,1,0:T(8,128)} %get-tuple-element.29), channel_id=1, source_target_pairs={{0,1},{1,2},{2,3},{3,4},{4,5},{5,6},{6,7},{7,8},{8,9},{9,10},{10,1... | collective-permute-start | bytes 1572872 | tf_op jit(solution)/shard_map/ppermute | solution.py:541
  85.0 3.3 %collective-permute-start.9 = (f32[1,2,128,512]{3,2,1,0:T(8,128)}, f32[1,2,128,512]{3,2,1,0:T(8,128)S(1)}, u32[]{:S(2)}, u32[]{:S(2)}) collective-permute-start(f32[1,2,128,512]{3,2,1,0:T(8,128)} %get-tuple-element.30), channel_id=1, source_target_pairs={{0,16},{16,32},{32,48},{48,64},{64,80},{80,96},{96,112},{1,17},{17... | collective-permute-start | bytes 1572872 | tf_op jit(solution)/shard_map/ppermute | solution.py:541
  88.3 2.1 %collective-permute-start.10 = (f32[1,2,128,512]{3,2,1,0:T(8,128)}, f32[1,2,128,512]{3,2,1,0:T(8,128)S(1)}, u32[]{:S(2)}, u32[]{:S(2)}) collective-permute-start(f32[1,2,128,512]{3,2,1,0:T(8,128)} %get-tuple-element.31), channel_id=1, source_target_pairs={{0,16},{16,32},{32,48},{48,64},{64,80},{80,96},{96,112},{1,17},{17... | collective-permute-start | bytes 1572872 | tf_op jit(solution)/shard_map/ppermute | solution.py:541
  90.4 0.0 collective-permute-done.6
  90.4 1.7 %add_dynamic-update-slice_fusion = f32[2,2,256,128]{3,2,1,0:T(8,128)} fusion(f32[2,2,256,128]{3,2,1,0:T(8,128)} %get-tuple-element.27, f32[2,2,128,128]{3,2,1,0:T(8,128)S(1)} %collective-permute-done.6), kind=kLoop, calls=%fused_computation | loop fusion | flops 65536 | bytes 786432 | tf_op jit(solution)/shard_map/scatter-add | solution.py:583
  92.1 3.1 %collective-permute-start.7 = (f32[2,2,256,128]{3,2,1,0:T(8,128)}, f32[2,2,256,128]{3,2,1,0:T(8,128)S(1)}, u32[]{:S(2)}, u32[]{:S(2)}) collective-permute-start(f32[2,2,256,128]{3,2,1,0:T(8,128)} %add_dynamic-update-slice_fusion), channel_id=1, source_target_pairs={{0,1},{1,2},{2,3},{3,4},{4,5},{5,6},{6,7},{7,8},{8,9},{9,10},{10,1... | collective-permute-start | bytes 1572872 | tf_op jit(solution)/shard_map/ppermute | solution.py:541
  95.2 3.2 %all-to-all-done = f32[64,24,128]{2,1,0:T(8,128)S(1)} async-done(((f32[64,24,128]{2,1,0:T(8,128)}), f32[64,24,128]{2,1,0:T(8,128)S(1)}, u32[]{:S(2)}, u32[]{:S(2)}) %all-to-all-start) | async-done | bytes 786464 | tf_op jit(solution)/shard_map/all_to_all | solution.py:551
  98.4 0.1 reduce_sum.9
  98.5 0.9 broadcast_in_dim.2
  99.4 6.0 %all-to-all-start.1 = ((f32[64,24,128]{2,1,0:T(8,128)}), f32[64,24,128]{2,1,0:T(8,128)S(1)}, u32[]{:S(2)}, u32[]{:S(2)}) async-start(f32[64,24,128]{2,1,0:T(8,128)} %broadcast_in_dim.2), calls=%async_computation.1 | async-start | bytes 1572864 | tf_op jit(solution)/shard_map/all_to_all | solution.py:558
  105.4 0.0 collective-permute-done.8.left_rest_in
  105.4 0.0 copy-start.4
  105.4 0.0 collective-permute-done.9.above_first_in
  105.4 0.0 copy-start.5
  105.4 0.0 collective-permute-done.10.above_second_in
  105.5 0.0 copy-start.6
  105.5 7.8 %collective-permute-done.7.left_top_in = f32[2,2,256,128]{3,2,1,0:T(8,128)S(1)} collective-permute-done((f32[2,2,256,128]{3,2,1,0:T(8,128)}, f32[2,2,256,128]{3,2,1,0:T(8,128)S(1)}, u32[]{:S(2)}, u32[]{:S(2)}) %collective-permute-start.7) | collective-permute-done | bytes 524320 | tf_op jit(solution)/shard_map/ppermute | solution.py:541
  113.3 0.0 copy-done.6
  113.3 0.0 copy-start.7
  113.3 0.8 copy-done.7
  114.1 0.0 copy-done.4
  114.1 0.0 copy-done.5
  114.1 0.0 copy-start
  114.1 6.1 %settle.1 = f32[2,2,512,512]{3,2,1,0:T(8,128)} custom-call(s32[1,1]{1,0:T(1,128)S(6)} %copy.10.count_ref, s32[2,4]{1,0:T(2,128)} %bitcast.14, f32[2,2,512,512]{3,2,1,0:T(8,128)} %tile.3, f32[4,2,2,128,128]{4,3,2,1,0:T(8,128)} %get-tuple-element.26.term_in, f32[2,2,256,128]{3,2,1,0:T(8,128)} %copy-done.7, f32[2,2,256,128]{3,2,1,0:T(8,128)} %copy-done.4, ...), custom_call_target="tpu_custom_call" | custom-call | flops 137438953472 | bytes 8388608 | tf_op jit(solution)/shard_map/settle/pallas_call | solution.py:386
  120.2 10.0 %all-to-all-done.1 = f32[64,24,128]{2,1,0:T(8,128)S(1)} async-done(((f32[64,24,128]{2,1,0:T(8,128)}), f32[64,24,128]{2,1,0:T(8,128)S(1)}, u32[]{:S(2)}, u32[]{:S(2)}) %all-to-all-start.1) | async-done | bytes 786464 | tf_op jit(solution)/shard_map/all_to_all | solution.py:558
  130.2 1.1 collective-permute-start.11
  131.3 1.9 %collective-permute-done.11.other = f32[12,128,128]{2,1,0:T(8,128)S(1)} collective-permute-done((f32[12,128,128]{2,1,0:T(8,128)S(1)}, f32[12,128,128]{2,1,0:T(8,128)S(1)}, u32[]{:S(2)}, u32[]{:S(2)}) %collective-permute-start.11) | collective-permute-done | bytes 786464 | tf_op jit(solution)/shard_map/ppermute | solution.py:541
  133.2 0.0 copy-done
  133.2 6.1 %orthogonalize.1 = f32[24,128,128]{2,1,0:T(8,128)} custom-call(s32[1,1]{1,0:T(1,128)} %bitcast.1.core_ref, f32[24,128,128]{2,1,0:T(8,128)S(1)} %bitcast.10, f32[12,128,128]{2,1,0:T(8,128)S(1)} %bitcast.8, f32[12,128,128]{2,1,0:T(8,128)S(1)} %collective-permute-done.11.other), custom_call_target="tpu_custom_call" | custom-call | tf_op jit(solution)/shard_map/orthogonalize/pallas_call | solution.py:522
  (1 shorter events, 0.0 us)
Async XLA Ops:
  1.9 30.7 %collective-permute-start.1 = (f32[2,2,256,128]{3,2,1,0:T(8,128)S(1)}, f32[2,2,256,128]{3,2,1,0:T(8,128)S(1)}, u32[]{:S(2)}, u32[]{:S(2)}) collective-permute-start(f32[2,2,256,128]{3,2,1,0:T(8,128)S(1)} %get-tuple-element.36), channel_id=1, source_target_pairs={{1,0},{2,1},{3,2},{4,3},{5,4},{6,5},{7,6},{8,7},{9,8},{10,9},{11,1... | collective-permute-start | bytes 1572872 | tf_op jit(solution)/shard_map/ppermute | solution.py:541
  3.2 25.0 %collective-permute-start = (f32[2,2,256,128]{3,2,1,0:T(8,128)S(1)}, f32[2,2,256,128]{3,2,1,0:T(8,128)S(1)}, u32[]{:S(2)}, u32[]{:S(2)}) collective-permute-start(f32[2,2,256,128]{3,2,1,0:T(8,128)S(1)} %get-tuple-element.37), channel_id=1, source_target_pairs={{1,0},{2,1},{3,2},{4,3},{5,4},{6,5},{7,6},{8,7},{9,8},{10,9},{11,1... | collective-permute-start | bytes 1572872 | tf_op jit(solution)/shard_map/ppermute | solution.py:541
  5.8 26.8 %collective-permute-start.3 = (f32[1,2,128,512]{3,2,1,0:T(8,128)S(1)}, f32[1,2,128,512]{3,2,1,0:T(8,128)S(1)}, u32[]{:S(2)}, u32[]{:S(2)}) collective-permute-start(f32[1,2,128,512]{3,2,1,0:T(8,128)S(1)} %get-tuple-element.34), channel_id=1, source_target_pairs={{16,0},{32,16},{48,32},{64,48},{80,64},{96,80},{112,96},{17,1},{33... | collective-permute-start | bytes 1572872 | tf_op jit(solution)/shard_map/ppermute | solution.py:541
  9.2 23.5 %collective-permute-start.2 = (f32[1,2,128,512]{3,2,1,0:T(8,128)S(1)}, f32[1,2,128,512]{3,2,1,0:T(8,128)}, u32[]{:S(2)}, u32[]{:S(2)}) collective-permute-start(f32[1,2,128,512]{3,2,1,0:T(8,128)S(1)} %get-tuple-element.35), channel_id=1, source_target_pairs={{16,0},{32,16},{48,32},{64,48},{80,64},{96,80},{112,96},{17,1},{33... | collective-permute-start | bytes 1572872 | tf_op jit(solution)/shard_map/ppermute | solution.py:541
  28.2 9.6 %copy-start.1 = (f32[2,2,256,128]{3,2,1,0:T(8,128)}, f32[2,2,256,128]{3,2,1,0:T(8,128)S(1)}, u32[]{:S(2)}) copy-start(f32[2,2,256,128]{3,2,1,0:T(8,128)S(1)} %collective-permute-done.top) | copy-start | bytes 1572868
  28.3 9.6 %collective-permute-start.4 = (f32[2,2,128,128]{3,2,1,0:T(8,128)S(1)}, f32[2,2,128,128]{3,2,1,0:T(8,128)}, u32[]{:S(2)}, u32[]{:S(2)}) collective-permute-start(f32[2,2,128,128]{3,2,1,0:T(8,128)S(1)} %slice.50), channel_id=1, source_target_pairs={{16,0},{32,16},{48,32},{64,48},{80,64},{96,80},{112,96},{17,1},{33... | collective-permute-start | bytes 786440 | tf_op jit(solution)/shard_map/ppermute | solution.py:541
  32.6 5.2 %copy-start.2 = (f32[2,2,256,128]{3,2,1,0:T(8,128)}, f32[2,2,256,128]{3,2,1,0:T(8,128)S(1)}, u32[]{:S(2)}) copy-start(f32[2,2,256,128]{3,2,1,0:T(8,128)S(1)} %collective-permute-done.1.rest) | copy-start | bytes 1572868
  32.6 5.2 %copy-start.3 = (f32[1,2,128,512]{3,2,1,0:T(8,128)}, f32[1,2,128,512]{3,2,1,0:T(8,128)S(1)}, u32[]{:S(2)}) copy-start(f32[1,2,128,512]{3,2,1,0:T(8,128)S(1)} %collective-permute-done.3.below_second) | copy-start | bytes 1572868
  50.6 7.8 %collective-permute-start.5 = (f32[12,128,128]{2,1,0:T(8,128)}, f32[12,128,128]{2,1,0:T(8,128)S(1)}, u32[]{:S(2)}, u32[]{:S(2)}) collective-permute-start(f32[12,128,128]{2,1,0:T(8,128)} %get-tuple-element.25), channel_id=1, source_target_pairs={{0,16},{16,0},{32,48},{48,32},{64,80},{80,64},{96,112},{112,96},{1... | collective-permute-start | bytes 2359304 | tf_op jit(solution)/shard_map/ppermute | solution.py:541
  50.7 39.7 %collective-permute-start.6 = (f32[2,2,128,128]{3,2,1,0:T(8,128)}, f32[2,2,128,128]{3,2,1,0:T(8,128)S(1)}, u32[]{:S(2)}, u32[]{:S(2)}) collective-permute-start(f32[2,2,128,128]{3,2,1,0:T(8,128)} %get-tuple-element.28), channel_id=1, source_target_pairs={{0,16},{16,32},{32,48},{48,64},{64,80},{80,96},{96,112},{1,17},{17... | collective-permute-start | bytes 786440 | tf_op jit(solution)/shard_map/ppermute | solution.py:541
  60.5 37.9 %all-to-all-start = ((f32[64,24,128]{2,1,0:T(8,128)}), f32[64,24,128]{2,1,0:T(8,128)S(1)}, u32[]{:S(2)}, u32[]{:S(2)}) async-start(f32[64,24,128]{2,1,0:T(8,128)} %bitcast.4), calls=%async_computation | async-start | bytes 1572864 | tf_op jit(solution)/shard_map/all_to_all | solution.py:551
  82.0 23.4 %collective-permute-start.8 = (f32[2,2,256,128]{3,2,1,0:T(8,128)}, f32[2,2,256,128]{3,2,1,0:T(8,128)S(1)}, u32[]{:S(2)}, u32[]{:S(2)}) collective-permute-start(f32[2,2,256,128]{3,2,1,0:T(8,128)} %get-tuple-element.29), channel_id=1, source_target_pairs={{0,1},{1,2},{2,3},{3,4},{4,5},{5,6},{6,7},{7,8},{8,9},{9,10},{10,1... | collective-permute-start | bytes 1572872 | tf_op jit(solution)/shard_map/ppermute | solution.py:541
  85.0 20.4 %collective-permute-start.9 = (f32[1,2,128,512]{3,2,1,0:T(8,128)}, f32[1,2,128,512]{3,2,1,0:T(8,128)S(1)}, u32[]{:S(2)}, u32[]{:S(2)}) collective-permute-start(f32[1,2,128,512]{3,2,1,0:T(8,128)} %get-tuple-element.30), channel_id=1, source_target_pairs={{0,16},{16,32},{32,48},{48,64},{64,80},{80,96},{96,112},{1,17},{17... | collective-permute-start | bytes 1572872 | tf_op jit(solution)/shard_map/ppermute | solution.py:541
  88.3 17.1 %collective-permute-start.10 = (f32[1,2,128,512]{3,2,1,0:T(8,128)}, f32[1,2,128,512]{3,2,1,0:T(8,128)S(1)}, u32[]{:S(2)}, u32[]{:S(2)}) collective-permute-start(f32[1,2,128,512]{3,2,1,0:T(8,128)} %get-tuple-element.31), channel_id=1, source_target_pairs={{0,16},{16,32},{32,48},{48,64},{64,80},{80,96},{96,112},{1,17},{17... | collective-permute-start | bytes 1572872 | tf_op jit(solution)/shard_map/ppermute | solution.py:541
  92.1 21.1 %collective-permute-start.7 = (f32[2,2,256,128]{3,2,1,0:T(8,128)}, f32[2,2,256,128]{3,2,1,0:T(8,128)S(1)}, u32[]{:S(2)}, u32[]{:S(2)}) collective-permute-start(f32[2,2,256,128]{3,2,1,0:T(8,128)} %add_dynamic-update-slice_fusion), channel_id=1, source_target_pairs={{0,1},{1,2},{2,3},{3,4},{4,5},{5,6},{6,7},{7,8},{8,9},{9,10},{10,1... | collective-permute-start | bytes 1572872 | tf_op jit(solution)/shard_map/ppermute | solution.py:541
  99.4 30.8 %all-to-all-start.1 = ((f32[64,24,128]{2,1,0:T(8,128)}), f32[64,24,128]{2,1,0:T(8,128)S(1)}, u32[]{:S(2)}, u32[]{:S(2)}) async-start(f32[64,24,128]{2,1,0:T(8,128)} %broadcast_in_dim.2), calls=%async_computation.1 | async-start | bytes 1572864 | tf_op jit(solution)/shard_map/all_to_all | solution.py:558
  105.4 8.7 %copy-start.4 = (f32[2,2,256,128]{3,2,1,0:T(8,128)}, f32[2,2,256,128]{3,2,1,0:T(8,128)S(1)}, u32[]{:S(2)}) copy-start(f32[2,2,256,128]{3,2,1,0:T(8,128)S(1)} %collective-permute-done.8.left_rest_in) | copy-start | bytes 1572868
  105.4 8.6 %copy-start.5 = (f32[1,2,128,512]{3,2,1,0:T(8,128)}, f32[1,2,128,512]{3,2,1,0:T(8,128)S(1)}, u32[]{:S(2)}) copy-start(f32[1,2,128,512]{3,2,1,0:T(8,128)S(1)} %collective-permute-done.9.above_first_in) | copy-start | bytes 1572868
  105.5 7.8 %copy-start.6 = (f32[1,2,128,512]{3,2,1,0:T(8,128)}, f32[1,2,128,512]{3,2,1,0:T(8,128)S(1)}, u32[]{:S(2)}) copy-start(f32[1,2,128,512]{3,2,1,0:T(8,128)S(1)} %collective-permute-done.10.above_second_in) | copy-start | bytes 1572868
  113.3 0.8 copy-start.7
  114.1 19.1 %copy-start = (f32[12,2,128,128]{3,2,1,0:T(8,128)S(1)}, f32[12,2,128,128]{3,2,1,0:T(8,128)}, u32[]{:S(2)}) copy-start(f32[12,2,128,128]{3,2,1,0:T(8,128)} %param.10) | copy-start | bytes 4718596
  130.2 3.0 %collective-permute-start.11 = (f32[12,128,128]{2,1,0:T(8,128)S(1)}, f32[12,128,128]{2,1,0:T(8,128)S(1)}, u32[]{:S(2)}, u32[]{:S(2)}) collective-permute-start(f32[12,128,128]{2,1,0:T(8,128)S(1)} %bitcast.7), channel_id=1, source_target_pairs={{0,16},{16,0},{32,48},{48,32},{64,80},{80,64},{96,112},{112,96},{1... | collective-permute-start | bytes 2359304 | tf_op jit(solution)/shard_map/ppermute | solution.py:541

commit v3 on v2

--- a/solution.py
+++ b/solution.py
@@ -99,25 +99,33 @@
 RIGHT, LEFT = 0, 1
 
 
-def load_sheet(tile, halo, sheet, sems, width):
-    rows, cols = tile.shape[2:]
-    top, rest, below_first, below_second, corner = halo
-    half = rows // 2
-    spots = [
-        (tile, sheet, 0, rows, 0, cols),
-        (top, sheet, 0, half, cols, width),
-        (rest, sheet, half, half, cols, width),
-        (below_first, sheet.at[pl.ds(0, 1)], rows, width, 0, cols),
-        (below_second, sheet.at[pl.ds(1, 1)], rows, width, 0, cols),
-        (corner, sheet, rows, width, cols, width),
-    ]
-    copies = [
-        pltpu.make_async_copy(src, dst.at[:, :, pl.ds(r, h), pl.ds(c, w)], sems.at[i])
-        for i, (src, dst, r, h, c, w) in enumerate(spots)
-    ]
+def start_all(pairs, sems):
+    copies = [pltpu.make_async_copy(src, dst, sems.at[i]) for i, (src, dst) in enumerate(pairs)]
     for copy in copies:
         copy.start()
     return copies
+
+
+def near_sheet(tile, below, sheet, width):
+    rows, cols = tile.shape[2:]
+    down, across = pl.ds(rows, width), pl.ds(0, cols)
+    return [(tile, sheet.at[:, :, pl.ds(0, rows), across])] + [
+        (part, sheet.at[pl.ds(s, 1), :, down, across]) for s, part in enumerate(below)
+    ]
+
+
+def far_sheet(tile, right, below, corner, sheet, width):
+    rows, cols = tile.shape[2:]
+    down, across, last = pl.ds(rows, width), pl.ds(cols, width), pl.ds(cols - width, width)
+    return (
+        [(tile.at[:, :, :, last], sheet.at[:, :, pl.ds(0, rows), last])]
+        + [(right, sheet.at[:, :, pl.ds(0, rows), across])]
+        + [
+            (part.at[:, :, :, last], sheet.at[pl.ds(s, 1), :, down, last])
+            for s, part in enumerate(below)
+        ]
+        + [(corner, sheet.at[:, :, down, across])]
+    )
 
 
 def corner_of(pos_ref, slot, width):
@@ -156,39 +164,17 @@
             sheet[where] = sheet[where] - wide
 
 
-def slots_kernel(
-    count_ref, pos_ref, core_ref, tile, top, rest, below_first, below_second, corner,
-    probe_in, pattern_in, step_in, transform_in,
-    keep_out, give_out, term_out, right_top_out, right_rest_out, below_first_out, below_second_out,
-    corner_out,
-    sheet, outer, probe, patterns, steps, transforms, window, wave, far, inten, pgrad, terms,
-    sem_in, sem_load, sem_term, sem_out,
+def visit_slots(
+    chosen, count, pos_ref, leaves, term_out, sheet, outer, probe, patterns, steps, transforms,
+    window, wave, far, inten, pgrad, terms, sem_term,
 ):
-    rows, cols = tile.shape[2:]
     width = probe.shape[-1]
-    planes = probe.shape[0]
-    pairs = planes // 4
-    count = count_ref[0, 0]
-    copies = load_sheet(tile, (top, rest, below_first, below_second, corner), sheet, sem_in, width)
-    loads = [
-        pltpu.make_async_copy(src, dst, sem_load.at[i])
-        for i, (src, dst) in enumerate(
-            [(probe_in, probe), (step_in, steps), (transform_in, transforms), (pattern_in, patterns)]
-        )
-    ]
-    for copy in loads:
-        copy.start()
+    pairs = probe.shape[0] // 4
 
     def save(slot):
         return pltpu.make_async_copy(terms.at[slot], term_out.at[slot], sem_term.at[slot])
 
-    pgrad[...] = jnp.zeros_like(pgrad)
-    outer[:, :, 0 : rows + width, cols : cols + width] = jnp.zeros((2, 2, rows + width, width), f32)
-    outer[:, :, rows : rows + width, 0:cols] = jnp.zeros((2, 2, width, cols), f32)
-    for copy in copies + loads:
-        copy.wait()
-
-    def visit(slot, carry):
+    def process(slot):
         place = corner_of(pos_ref, slot, width)
         for s in range(2):
             for c in range(2):
@@ -225,38 +211,96 @@
             for i in range(4):
                 pgrad[p * 4 + i] += v[i]
         save(slot).start()
-        leaves = (pos_ref[0, slot] > rows - width) | (pos_ref[1, slot] > cols - width)
-
-        @pl.when(leaves)
+
+        @pl.when(leaves(slot))
         def _():
             subtract_terms(slot, pos_ref, terms, outer, width)
 
+    def visit(slot, carry):
+        pl.when(chosen(slot))(lambda: process(slot))
         return carry
 
     def finish(slot, carry):
-        save(slot).wait()
+        pl.when(chosen(slot))(lambda: save(slot).wait())
         return carry
 
     lax.fori_loop(0, count, visit, 0)
+    return lambda: lax.fori_loop(0, count, finish, 0)
+
+
+def near_kernel(
+    count_ref, pos_ref, tile, below_first, below_second, probe_in, pattern_in, step_in,
+    transform_in,
+    pgrad_out, term_out, below_out,
+    sheet, outer, probe, patterns, steps, transforms, window, wave, far, inten, pgrad, terms,
+    sem_in, sem_term, sem_out,
+):
+    width = probe.shape[-1]
+    rows, cols = tile.shape[2:]
+    loads = start_all(
+        near_sheet(tile, (below_first, below_second), sheet, width)
+        + [(probe_in, probe), (step_in, steps), (transform_in, transforms), (pattern_in, patterns)],
+        sem_in,
+    )
+    outside = outer.at[:, :, pl.ds(rows, width), pl.ds(0, cols)]
+    pgrad[...] = jnp.zeros_like(pgrad)
+    outside[...] = jnp.zeros((2, 2, width, cols), f32)
+    for copy in loads:
+        copy.wait()
+    wait_terms = visit_slots(
+        lambda slot: pos_ref[1, slot] <= cols - width, count_ref[0, 0], pos_ref,
+        lambda slot: pos_ref[0, slot] > rows - width,
+        term_out, sheet, outer, probe, patterns, steps, transforms, window, wave, far, inten,
+        pgrad, terms, sem_term,
+    )
+    stores = start_all([(pgrad, pgrad_out), (outside, below_out)], sem_out)
+    wait_terms()
+    for copy in stores:
+        copy.wait()
+
+
+def far_kernel(
+    count_ref, pos_ref, core_ref, tile, right, below_first, below_second, corner, probe_in,
+    pattern_in, step_in, transform_in, pgrad_in, below_in, term_in,
+    keep_out, give_out, right_top_out, right_rest_out, below_first_out, below_second_out,
+    corner_out, term_out,
+    sheet, outer, probe, patterns, steps, transforms, window, wave, far, inten, pgrad, terms,
+    sem_in, sem_term, sem_out,
+):
+    width = probe.shape[-1]
+    planes = probe.shape[0]
+    rows, cols = tile.shape[2:]
+    down, across, inner = pl.ds(rows, width), pl.ds(cols, width), pl.ds(0, cols)
+    loads = start_all(
+        far_sheet(tile, right, (below_first, below_second), corner, sheet, width)
+        + [(probe_in, probe), (step_in, steps), (transform_in, transforms), (pattern_in, patterns)]
+        + [(pgrad_in, pgrad), (below_in, outer.at[:, :, down, inner])],
+        sem_in,
+    )
+    outer[:, :, 0 : rows + width, cols : cols + width] = jnp.zeros((2, 2, rows + width, width), f32)
+    for copy in loads:
+        copy.wait()
+    wait_terms = visit_slots(
+        lambda slot: pos_ref[1, slot] > cols - width, count_ref[0, 0], pos_ref,
+        lambda slot: pos_ref[1, slot] > cols - width,
+        term_out, sheet, outer, probe, patterns, steps, transforms, window, wave, far, inten,
+        pgrad, terms, sem_term,
+    )
     half = planes // 2
     core = core_ref[0, 0]
-    middle = rows // 2
-    down, across = pl.ds(rows, width), pl.ds(cols, width)
-    results = [
-        (pgrad.at[pl.ds((1 - core) * half, half)], give_out),
-        (pgrad.at[pl.ds(core * half, half)], keep_out),
-        (outer.at[:, :, down, across], corner_out),
-        (outer.at[:, :, pl.ds(middle, middle), across], right_rest_out),
-        (outer.at[:, :, pl.ds(0, middle), across], right_top_out),
-        (outer.at[pl.ds(0, 1), :, down, pl.ds(0, cols)], below_first_out),
-        (outer.at[pl.ds(1, 1), :, down, pl.ds(0, cols)], below_second_out),
-    ]
-    stores = [
-        pltpu.make_async_copy(src, dst, sem_out.at[i]) for i, (src, dst) in enumerate(results)
-    ]
-    for copy in stores:
-        copy.start()
-    lax.fori_loop(0, count, finish, 0)
+    stores = start_all(
+        [
+            (pgrad.at[pl.ds((1 - core) * half, half)], give_out),
+            (pgrad.at[pl.ds(core * half, half)], keep_out),
+            (outer.at[:, :, down, across], corner_out),
+            (outer.at[:, :, pl.ds(width, rows - width), across], right_rest_out),
+            (outer.at[:, :, pl.ds(0, width), across], right_top_out),
+            (outer.at[pl.ds(0, 1), :, down, inner], below_first_out),
+            (outer.at[pl.ds(1, 1), :, down, inner], below_second_out),
+        ],
+        sem_out,
+    )
+    wait_terms()
     for copy in stores:
         copy.wait()
 
@@ -278,20 +322,21 @@
 
 
 def settle_kernel(
-    count_ref, pos_ref, tile, term_in, left_top_in, left_rest_in, above_first_in, above_second_in, tile_out,
-    sheet, terms, left, above, sem_term, sem_in, sem_out,
+    count_ref, pos_ref, tile, term_in, left_top_in, left_rest_in, above_first_in, above_second_in, corner_in,
+    tile_out,
+    sheet, terms, left, above, corner, sem_term, sem_in, sem_out,
 ):
     width = above_first_in.shape[2]
     rows, cols = tile.shape[2:]
-    middle = rows // 2
     count = count_ref[0, 0]
     inner = sheet.at[:, :, pl.ds(0, rows), pl.ds(0, cols)]
     sources = [
         (tile, inner),
-        (left_top_in, left.at[:, :, pl.ds(0, middle)]),
-        (left_rest_in, left.at[:, :, pl.ds(middle, middle)]),
+        (left_top_in, left.at[:, :, pl.ds(0, width)]),
+        (left_rest_in, left.at[:, :, pl.ds(width, rows - width)]),
         (above_first_in, above.at[pl.ds(0, 1)]),
         (above_second_in, above.at[pl.ds(1, 1)]),
+        (corner_in, corner),
     ]
     loads = [
         pltpu.make_async_copy(src, dst, sem_in.at[i]) for i, (src, dst) in enumerate(sources)
@@ -304,6 +349,7 @@
     wait()
     sheet[:, :, 0:rows, 0:width] += left[...]
     sheet[:, :, 0:width, 0:cols] += above[...]
+    sheet[:, :, 0:width, 0:width] += corner[...]
 
     def visit(slot, carry):
         subtract_terms(slot, pos_ref, terms, sheet, width)
@@ -335,72 +381,98 @@
     )
 
 
-def run_slots(counts, positions, core, tile, halo, probe, patterns):
+def slot_scratch(rows, cols, capacity, probe, steps, transforms, loads, stores):
+    width = probe.shape[-1]
+    stack = pltpu.VMEM(probe.shape, f32)
+    field = pltpu.VMEM((2, 2, rows + width + 8, cols + 2 * width), f32)
+    return [
+        field,
+        field,
+        stack,
+        pltpu.VMEM((capacity, width, width), f32),
+        pltpu.VMEM(steps.shape, bf16),
+        pltpu.VMEM(transforms.shape, bf16),
+        pltpu.VMEM((2, 2, width, width), f32),
+        stack,
+        stack,
+        pltpu.VMEM((width, width), f32),
+        stack,
+        pltpu.VMEM((capacity, 2, 2, width, width), f32),
+        DMA((loads,)),
+        DMA((capacity,)),
+        DMA((stores,)),
+    ]
+
+
+def near_slots(counts, positions, tile, below, probe, patterns, tables, products):
+    width = probe.shape[-1]
+    rows, cols = tile.shape[2:]
+    capacity = positions.shape[1]
+    return pl.pallas_call(
+        near_kernel,
+        out_shape=[
+            shape(*probe.shape),
+            shape(capacity, 2, 2, width, width),
+            shape(2, 2, width, cols),
+        ],
+        in_specs=[SMEM, SMEM] + [ANY] * 7,
+        out_specs=[ANY] * 3,
+        scratch_shapes=slot_scratch(rows, cols, capacity, probe, *tables, 7, 2),
+        compiler_params=params(60),
+        cost_estimate=work(products),
+        name="near_slots",
+    )(counts, positions, tile, *below, probe, patterns, *tables)
+
+
+def far_slots(counts, positions, core, tile, halo, probe, patterns, tables, sums):
     planes, width = probe.shape[0], probe.shape[-1]
     rows, cols = tile.shape[2:]
     capacity = positions.shape[1]
-    half = (planes // 2, width, width)
-    stack = pltpu.VMEM(probe.shape, f32)
-    steps, transforms = make_tables(width)
+    half = shape(planes // 2, width, width)
     return pl.pallas_call(
-        slots_kernel,
+        far_kernel,
         out_shape=[
-            shape(*half),
-            shape(*half),
-            shape(capacity, 2, 2, width, width),
-            shape(2, 2, rows // 2, width),
-            shape(2, 2, rows // 2, width),
+            half,
+            half,
+            shape(2, 2, width, width),
+            shape(2, 2, rows - width, width),
             shape(1, 2, width, cols),
             shape(1, 2, width, cols),
             shape(2, 2, width, width),
+            shape(capacity, 2, 2, width, width),
         ],
-        in_specs=[SMEM, SMEM, SMEM] + [ANY] * 10,
+        in_specs=[SMEM, SMEM, SMEM] + [ANY] * 12,
         out_specs=[ANY] * 8,
-        scratch_shapes=[
-            pltpu.VMEM((2, 2, rows + width + 8, cols + 2 * width), f32),
-            pltpu.VMEM((2, 2, rows + width + 8, cols + 2 * width), f32),
-            stack,
-            pltpu.VMEM(patterns.shape, f32),
-            pltpu.VMEM(steps.shape, bf16),
-            pltpu.VMEM(transforms.shape, bf16),
-            pltpu.VMEM((2, 2, width, width), f32),
-            stack,
-            stack,
-            pltpu.VMEM((width, width), f32),
-            stack,
-            pltpu.VMEM((capacity, 2, 2, width, width), f32),
-            DMA((6,)),
-            DMA((4,)),
-            DMA((capacity,)),
-            DMA((7,)),
-        ],
+        scratch_shapes=slot_scratch(rows, cols, capacity, probe, *tables, 11, 7),
+        input_output_aliases={14: 7},
         compiler_params=params(60),
         cost_estimate=work(4 * capacity * planes),
-        name="slots",
-    )(counts, positions, core, tile, *halo, probe, patterns, steps, transforms)
-
-
-def settle(counts, positions, tile, terms, left, above):
+        name="far_slots",
+    )(counts, positions, core, tile, *halo, probe, patterns, *tables, *sums)
+
+
+def settle(counts, positions, tile, terms, left, above, corner):
     capacity, width = terms.shape[0], terms.shape[-1]
     rows, cols = tile.shape[2:]
     return pl.pallas_call(
         settle_kernel,
         out_shape=shape(*tile.shape),
-        in_specs=[SMEM, SMEM] + [ANY] * 6,
+        in_specs=[SMEM, SMEM] + [ANY] * 7,
         out_specs=ANY,
         scratch_shapes=[
             pltpu.VMEM((2, 2, rows + width + 8, cols + 2 * width), f32),
             pltpu.VMEM(terms.shape, f32),
             pltpu.VMEM((2, 2, rows, width), f32),
             pltpu.VMEM((2, 2, width, cols), f32),
+            pltpu.VMEM(corner.shape, f32),
             DMA((capacity,)),
-            DMA((5,)),
+            DMA((6,)),
             DMA((1,)),
         ],
         compiler_params=params(60),
         cost_estimate=work(4096),
         name="settle",
-    )(counts, positions, tile, terms, *left, *above)
+    )(counts, positions, tile, terms, *left, *above, corner)
 
 
 def core_groups(rows, cols, split):
@@ -545,6 +617,15 @@
     return [(i, i + by) for i in range(size) if 0 <= i + by < size]
 
 
+def shifted_both(rows, cols, by):
+    return [
+        (r * cols + c, (r + by) * cols + c + by)
+        for r in range(rows)
+        for c in range(cols)
+        if 0 <= r + by < rows and 0 <= c + by < cols
+    ]
+
+
 def sum_share(keep, groups):
     members = len(groups[0])
     parts = keep.reshape(members, -1, keep.shape[-1])
@@ -570,22 +651,25 @@
     swap = [(r, r ^ 1) for r in range(rows)]
     groups = core_groups(rows, cols, 2)
 
-    middle = object_slices.shape[2] // 2
-    top = moved(object_slices[:, :, :middle, :width], "col", left_one)
-    rest = moved(object_slices[:, :, middle:, :width], "col", left_one)
+    right = moved(object_slices[:, :, :, :width], "col", left_one)
     below = [moved(object_slices[s : s + 1, :, :width, :], "row", up_one) for s in range(2)]
-    corner = moved(top[:, :, :width], "row", up_one)
-    keep, give, terms, right_top, right_rest, *below_grads, corner_grad = run_slots(
-        counts, spots, core, object_slices, (top, rest, *below, corner), planes, measured[0]
+    corner = moved(object_slices[:, :, :width, :width], ("row", "col"), shifted_both(rows, cols, -1))
+    tables = [jnp.asarray(t) for t in make_tables(width)]
+    probe_sum, terms, below_sum = near_slots(
+        counts, spots, object_slices, below, planes, measured[0], tables, 1
+    )
+    keep, give, right_top, right_rest, *below_grads, corner_grad, terms = far_slots(
+        counts, spots, core, object_slices, (right, *below, corner), planes, measured[0],
+        tables, (probe_sum, below_sum, terms),
     )
     keep = keep + moved(give, "row", swap)
     left_rest = moved(right_rest, "col", right_one)
-    right_top = right_top.at[:, :, :width].add(moved(corner_grad, "row", down_one))
+    from_corner = moved(corner_grad, ("row", "col"), shifted_both(rows, cols, 1))
     left_top = moved(right_top, "col", right_one)
     above = [moved(part, "row", down_one) for part in below_grads]
     share = sum_share(keep, groups)
     mine = gather_shares(share, groups).reshape(keep.shape)
-    object_next = settle(counts, spots, object_slices, terms, (left_top, left_rest), above)
+    object_next = settle(counts, spots, object_slices, terms, (left_top, left_rest), above, from_corner)
     mine, object_next = lax.optimization_barrier((mine, object_next))
     other = moved(mine, "row", swap)
     divisor = math.sqrt(rows * cols * capacity)

time: 142 us -> 131 us (0.923)
  waiting for transfers between devices: 45.2 us -> 23.5 us
  Pallas kernels: 25 us -> 36.8 us
  local copies, waits for them, and re-layouts: 4.36 us -> 6.98 us
  other arithmetic: 3.87 us -> 2.18 us
  starting transfers between devices: 59.3 us -> 57.8 us
    ppermute x12 -> x11, waiting for transfers between devices: 32.1 us -> 12.3 us  [moved(): return lax.ppermute(shard, axes, pairs)]
    pallas_call x1 -> x2, Pallas kernels: 12.7 us -> 24.2 us  [the longest x1 18.1 us: near_slots(): pl.pallas_call(near_kernel, out_shape=[shape(*probe.shape), shape(capacit...]
    all_to_all x1, waiting for transfers between devices: 10 us -> 5.22 us  [gather_shares(): return lax.all_to_all(parts, ('row', 'col'), 0, 0, axis_index_groups=groups)]
    all_to_all x1, waiting for transfers between devices: 3.16 us -> 5.93 us  [sum_share(): lax.all_to_all(parts, ('row', 'col'), 0, 0, axis_index_groups=groups)]
    ppermute x12 -> x11, starting transfers between devices: 31.8 us -> 29.2 us  [moved(): return lax.ppermute(shard, axes, pairs)]
    all_to_all x1, starting transfers between devices: 21.5 us -> 24 us  [sum_share(): lax.all_to_all(parts, ('row', 'col'), 0, 0, axis_index_groups=groups)]
    scatter-add x1 -> x0, other arithmetic: 1.69 us -> none  [local(): right_top.at[:, :, :width].add(moved(corner_grad, 'row', down_one))]
    unnamed x16 -> x12, local copies, waits for them, and re-layouts: 0.83 us -> 2.49 us
  transfers between devices with their start and end apart: 14 -> 13, of which waited for: 6 -> 6; matrix products, arithmetic and copies ran while one was open for 4% -> 4% of each run, Pallas kernels for 4% -> 19%
where the time goes in v3:
time: 131 us; the launch traced here: 129 us
  starting transfers between devices  57.8 us (44%)
  Pallas kernels  36.8 us (28%)
  waiting for transfers between devices  23.5 us (18%)
  local copies, waits for them, and re-layouts  6.98 us (5%)
  other arithmetic  2.18 us (2%)
  between operations  1.65 us (1%)
    ppermute x11, starting transfers between devices, moved(): return lax.ppermute(shard, axes, pairs)  29.2 us
    all_to_all x1, starting transfers between devices, sum_share(): lax.all_to_all(parts, ('row', 'col'), 0, 0, axis_index_groups=groups)  24 us
    pallas_call x1, Pallas kernels, near_slots(): pl.pallas_call(near_kernel, out_shape=[shape(*probe.shape), shape(capacit...  18.1 us
    ppermute x11, waiting for transfers between devices, moved(): return lax.ppermute(shard, axes, pairs)  12.3 us
    pallas_call x1, Pallas kernels, settle(): pl.pallas_call(settle_kernel, out_shape=shape(*tile.shape), in_specs=[SME...  6.47 us
    pallas_call x1, Pallas kernels, far_slots(): pl.pallas_call(far_kernel, out_shape=[half, half, shape(2, 2, width, widt...  6.17 us
    pallas_call x1, Pallas kernels, orthogonalize(): pl.pallas_call(functools.partial(orthogonal_kernel, 1.0 / divisor), out_s...  6.1 us
    all_to_all x1, waiting for transfers between devices, sum_share(): lax.all_to_all(parts, ('row', 'col'), 0, 0, axis_index_groups=groups)  5.93 us
  transfers between devices with their start and end apart: 13, of which 6 were waited for; matrix products, arithmetic and copies ran while one was open for 4% of the time, Pallas kernels for 19%

profile of v3, /device:TPU:1, one launch (start us, length us, event | category | flops | bytes accessed | tf_op | source)
XLA Modules:
  0.0 128.9 jit_solution(11846251507985044760)
XLA Ops:
  0.6 1.3 %slice.12 = f32[2,2,512,128]{3,2,1,0:T(8,128)S(1)} slice(f32[2,2,512,512]{3,2,1,0:T(8,128)} %tile.5), slice={[0:2], [0:2], [0:512], [0:128]} | slice | bytes 2097152 | tf_op jit(solution)/shard_map/slice | solution.py:654
  1.9 1.3 %collective-permute-start = (f32[2,2,512,128]{3,2,1,0:T(8,128)S(1)}, f32[2,2,512,128]{3,2,1,0:T(8,128)}, u32[]{:S(2)}, u32[]{:S(2)}) collective-permute-start(f32[2,2,512,128]{3,2,1,0:T(8,128)S(1)} %slice.12), channel_id=1, source_target_pairs={{1,0},{2,1},{3,2},{4,3},{5,4},{6,5},{7,6},{8,7},{9,8},{10,9},{11,1... | collective-permute-start | bytes 3145736 | tf_op jit(solution)/shard_map/ppermute | solution.py:613
  3.2 1.3 fusion
  4.5 3.3 %collective-permute-start.2 = (f32[1,2,128,512]{3,2,1,0:T(8,128)S(1)}, f32[1,2,128,512]{3,2,1,0:T(8,128)S(1)}, u32[]{:S(2)}, u32[]{:S(2)}) collective-permute-start(f32[1,2,128,512]{3,2,1,0:T(8,128)S(1)} %get-tuple-element.28), channel_id=1, source_target_pairs={{16,0},{32,16},{48,32},{64,48},{80,64},{96,80},{112,96},{17,1},{33... | collective-permute-start | bytes 1572872 | tf_op jit(solution)/shard_map/ppermute | solution.py:613
  7.9 1.9 %collective-permute-start.1 = (f32[1,2,128,512]{3,2,1,0:T(8,128)S(1)}, f32[1,2,128,512]{3,2,1,0:T(8,128)S(1)}, u32[]{:S(2)}, u32[]{:S(2)}) collective-permute-start(f32[1,2,128,512]{3,2,1,0:T(8,128)S(1)} %get-tuple-element.29), channel_id=1, source_target_pairs={{16,0},{32,16},{48,32},{64,48},{80,64},{96,80},{112,96},{17,1},{33... | collective-permute-start | bytes 1572872 | tf_op jit(solution)/shard_map/ppermute | solution.py:613
  9.8 1.0 slice.15
  10.8 1.3 %collective-permute-start.3 = (f32[2,2,128,128]{3,2,1,0:T(8,128)S(1)}, f32[2,2,128,128]{3,2,1,0:T(8,128)}, u32[]{:S(2)}, u32[]{:S(2)}) collective-permute-start(f32[2,2,128,128]{3,2,1,0:T(8,128)S(1)} %slice.15), channel_id=1, source_target_pairs={{17,0},{18,1},{19,2},{20,3},{21,4},{22,5},{23,6},{24,7},{25,8},{26... | collective-permute-start | bytes 786440 | tf_op jit(solution)/shard_map/ppermute | solution.py:613
  12.7 4.0 %collective-permute-done.2.below_second = f32[1,2,128,512]{3,2,1,0:T(8,128)S(1)} collective-permute-done((f32[1,2,128,512]{3,2,1,0:T(8,128)S(1)}, f32[1,2,128,512]{3,2,1,0:T(8,128)S(1)}, u32[]{:S(2)}, u32[]{:S(2)}) %collective-permute-start.2) | collective-permute-done | bytes 524320 | tf_op jit(solution)/shard_map/ppermute | solution.py:613
  16.7 0.0 copy-start.1
  16.7 5.6 %collective-permute-done.1.below_first = f32[1,2,128,512]{3,2,1,0:T(8,128)S(1)} collective-permute-done((f32[1,2,128,512]{3,2,1,0:T(8,128)S(1)}, f32[1,2,128,512]{3,2,1,0:T(8,128)S(1)}, u32[]{:S(2)}, u32[]{:S(2)}) %collective-permute-start.1) | collective-permute-done | bytes 524320 | tf_op jit(solution)/shard_map/ppermute | solution.py:613
  22.3 0.0 copy-start.2
  22.3 0.0 copy-done.1
  22.3 0.8 copy-done.2
  23.1 18.1 %near_slots.1 = (f32[24,128,128]{2,1,0:T(8,128)}, f32[4,2,2,128,128]{4,3,2,1,0:T(8,128)}, f32[2,2,128,512]{3,2,1,0:T(8,128)}) custom-call(s32[1,1]{1,0:T(1,128)S(6)} %copy.11.count_ref, s32[2,4]{1,0:T(2,128)} %bitcast.15, f32[2,2,512,512]{3,2,1,0:T(8,128)} %tile.5, f32[1,2,128,512]{3,2,1,0:T(8,128)} %copy-done.2, f32[1,2,128,512]{3,2,1,0:T(8,128)} %copy-done.1, ...), custom_call_target="tpu_custom_call" | custom-call | flops 33554432 | bytes 8388608 | tf_op jit(solution)/shard_map/near_slots/pallas_call | solution.py:411
  41.2 0.0 collective-permute-done.3.corner
  41.2 0.0 collective-permute-done.right
  41.2 6.2 %far_slots.1 = (f32[12,128,128]{2,1,0:T(8,128)}, f32[12,128,128]{2,1,0:T(8,128)}, f32[2,2,128,128]{3,2,1,0:T(8,128)}, f32[2,2,384,128]{3,2,1,0:T(8,128)}, f32[1,...) custom-call(s32[1,1]{1,0:T(1,128)S(6)} %copy.11.count_ref, ...), custom_call_target="tpu_custom_call", output_to_operand_aliasing={{7}: (14, {})} | custom-call | flops 12884901888 | bytes 8388608 | tf_op jit(solution)/shard_map/far_slots/pallas_call | solution.py:432
  47.4 1.8 %collective-permute-start.4 = (f32[12,128,128]{2,1,0:T(8,128)}, f32[12,128,128]{2,1,0:T(8,128)S(1)}, u32[]{:S(2)}, u32[]{:S(2)}) collective-permute-start(f32[12,128,128]{2,1,0:T(8,128)} %get-tuple-element.19), channel_id=1, source_target_pairs={{0,16},{16,0},{32,48},{48,32},{64,80},{80,64},{96,112},{112,96},{1... | collective-permute-start | bytes 2359304 | tf_op jit(solution)/shard_map/ppermute | solution.py:613
  49.2 1.3 %collective-permute-start.6 = (f32[2,2,384,128]{3,2,1,0:T(8,128)}, f32[2,2,384,128]{3,2,1,0:T(8,128)S(1)}, u32[]{:S(2)}, u32[]{:S(2)}) collective-permute-start(f32[2,2,384,128]{3,2,1,0:T(8,128)} %get-tuple-element.22), channel_id=1, source_target_pairs={{0,1},{1,2},{2,3},{3,4},{4,5},{5,6},{6,7},{7,8},{8,9},{9,10},{10,1... | collective-permute-start | bytes 2359304 | tf_op jit(solution)/shard_map/ppermute | solution.py:613
  50.5 0.8 collective-permute-done.4
  51.3 2.1 %add.8 = f32[12,128,128]{2,1,0:T(8,128)} add(f32[12,128,128]{2,1,0:T(8,128)} %get-tuple-element.18, f32[12,128,128]{2,1,0:T(8,128)S(1)} %collective-permute-done.4) | non-fusion elementwise | flops 196608 | bytes 2359296 | tf_op jit(solution)/shard_map/add | solution.py:665
  53.4 24.0 %all-to-all-start = ((f32[64,24,128]{2,1,0:T(8,128)}), f32[64,24,128]{2,1,0:T(8,128)S(1)}, u32[]{:S(2)}, u32[]{:S(2)}) async-start(f32[64,24,128]{2,1,0:T(8,128)} %bitcast.4), calls=%async_computation | async-start | bytes 1572864 | tf_op jit(solution)/shard_map/all_to_all | solution.py:632
  77.4 4.1 %collective-permute-start.7 = (f32[1,2,128,512]{3,2,1,0:T(8,128)}, f32[1,2,128,512]{3,2,1,0:T(8,128)S(1)}, u32[]{:S(2)}, u32[]{:S(2)}) collective-permute-start(f32[1,2,128,512]{3,2,1,0:T(8,128)} %get-tuple-element.23), channel_id=1, source_target_pairs={{0,16},{16,32},{32,48},{48,64},{64,80},{80,96},{96,112},{1,17},{17... | collective-permute-start | bytes 1572872 | tf_op jit(solution)/shard_map/ppermute | solution.py:613
  81.6 1.9 %collective-permute-start.8 = (f32[1,2,128,512]{3,2,1,0:T(8,128)}, f32[1,2,128,512]{3,2,1,0:T(8,128)}, u32[]{:S(2)}, u32[]{:S(2)}) collective-permute-start(f32[1,2,128,512]{3,2,1,0:T(8,128)} %get-tuple-element.24), channel_id=1, source_target_pairs={{0,16},{16,32},{32,48},{48,64},{64,80},{80,96},{96,112},{1,17},{17... | collective-permute-start | bytes 1572872 | tf_op jit(solution)/shard_map/ppermute | solution.py:613
  83.5 3.1 %collective-permute-start.5 = (f32[2,2,128,128]{3,2,1,0:T(8,128)}, f32[2,2,128,128]{3,2,1,0:T(8,128)S(1)}, u32[]{:S(2)}, u32[]{:S(2)}) collective-permute-start(f32[2,2,128,128]{3,2,1,0:T(8,128)} %get-tuple-element.21), channel_id=1, source_target_pairs={{0,1},{1,2},{2,3},{3,4},{4,5},{5,6},{6,7},{7,8},{8,9},{9,10},{10,1... | collective-permute-start | bytes 786440 | tf_op jit(solution)/shard_map/ppermute | solution.py:613
  86.6 5.4 %collective-permute-start.9 = (f32[2,2,128,128]{3,2,1,0:T(8,128)}, f32[2,2,128,128]{3,2,1,0:T(8,128)}, u32[]{:S(2)}, u32[]{:S(2)}) collective-permute-start(f32[2,2,128,128]{3,2,1,0:T(8,128)} %get-tuple-element.25), channel_id=1, source_target_pairs={{0,17},{1,18},{2,19},{3,20},{4,21},{5,22},{6,23},{7,24},{8,25},{9,... | collective-permute-start | bytes 786440 | tf_op jit(solution)/shard_map/ppermute | solution.py:613
  92.0 5.9 %all-to-all-done = f32[64,24,128]{2,1,0:T(8,128)S(1)} async-done(((f32[64,24,128]{2,1,0:T(8,128)}), f32[64,24,128]{2,1,0:T(8,128)S(1)}, u32[]{:S(2)}, u32[]{:S(2)}) %all-to-all-start) | async-done | bytes 786464 | tf_op jit(solution)/shard_map/all_to_all | solution.py:632
  98.0 0.1 reduce_sum.9
  98.1 0.9 broadcast_in_dim.2
  99.0 4.6 %all-to-all-start.1 = ((f32[64,24,128]{2,1,0:T(8,128)}), f32[64,24,128]{2,1,0:T(8,128)S(1)}, u32[]{:S(2)}, u32[]{:S(2)}) async-start(f32[64,24,128]{2,1,0:T(8,128)} %broadcast_in_dim.2), calls=%async_computation.1 | async-start | bytes 1572864 | tf_op jit(solution)/shard_map/all_to_all | solution.py:639
  103.6 0.0 collective-permute-done.5.left_top_in
  103.6 0.0 copy-start.5
  103.7 0.0 collective-permute-done.9.corner_in
  103.7 0.0 collective-permute-done.7.above_first_in
  103.7 0.0 copy-start.4
  103.7 0.0 collective-permute-done.8.above_second_in
  103.7 0.0 collective-permute-done.6.left_rest_in
  103.7 0.8 copy-done.4
  104.5 0.0 copy-start.3
  104.5 0.0 copy-done.5
  104.5 0.9 copy-done.3
  105.4 0.0 copy-start
  105.4 6.5 %settle.1 = f32[2,2,512,512]{3,2,1,0:T(8,128)} custom-call(s32[1,1]{1,0:T(1,128)S(6)} %copy.11.count_ref, s32[2,4]{1,0:T(2,128)} %bitcast.17, f32[2,2,512,512]{3,2,1,0:T(8,128)} %tile.5, f32[4,2,2,128,128]{4,3,2,1,0:T(8,128)} %get-tuple-element.20.term_in, f32[2,2,128,128]{3,2,1,0:T(8,128)} %copy-done.5, f32[2,2,384,128]{3,2,1,0:T(8,128)} %copy-done.3, ...), custom_call_target="tpu_custom_call" | custom-call | flops 137438953472 | bytes 8388608 | tf_op jit(solution)/shard_map/settle/pallas_call | solution.py:457
  111.9 5.2 %all-to-all-done.1 = f32[64,24,128]{2,1,0:T(8,128)S(1)} async-done(((f32[64,24,128]{2,1,0:T(8,128)}), f32[64,24,128]{2,1,0:T(8,128)S(1)}, u32[]{:S(2)}, u32[]{:S(2)}) %all-to-all-start.1) | async-done | bytes 786464 | tf_op jit(solution)/shard_map/all_to_all | solution.py:639
  117.1 3.6 %collective-permute-start.10 = (f32[12,128,128]{2,1,0:T(8,128)S(1)}, f32[12,128,128]{2,1,0:T(8,128)S(1)}, u32[]{:S(2)}, u32[]{:S(2)}) collective-permute-start(f32[12,128,128]{2,1,0:T(8,128)S(1)} %bitcast.10), channel_id=1, source_target_pairs={{0,16},{16,0},{32,48},{48,32},{64,80},{80,64},{96,112},{112,96},{1... | collective-permute-start | bytes 2359304 | tf_op jit(solution)/shard_map/ppermute | solution.py:613
  120.7 1.9 %collective-permute-done.10.other = f32[12,128,128]{2,1,0:T(8,128)S(1)} collective-permute-done((f32[12,128,128]{2,1,0:T(8,128)S(1)}, f32[12,128,128]{2,1,0:T(8,128)S(1)}, u32[]{:S(2)}, u32[]{:S(2)}) %collective-permute-start.10) | collective-permute-done | bytes 786464 | tf_op jit(solution)/shard_map/ppermute | solution.py:613
  122.6 0.0 copy-done
  122.6 6.1 %orthogonalize.1 = f32[24,128,128]{2,1,0:T(8,128)} custom-call(s32[1,1]{1,0:T(1,128)} %bitcast.1.core_ref, f32[24,128,128]{2,1,0:T(8,128)S(1)} %bitcast.9, f32[12,128,128]{2,1,0:T(8,128)S(1)} %bitcast.11, f32[12,128,128]{2,1,0:T(8,128)S(1)} %collective-permute-done.10.other), custom_call_target="tpu_custom_call" | custom-call | tf_op jit(solution)/shard_map/orthogonalize/pallas_call | solution.py:594
Async XLA Ops:
  1.9 39.2 %collective-permute-start = (f32[2,2,512,128]{3,2,1,0:T(8,128)S(1)}, f32[2,2,512,128]{3,2,1,0:T(8,128)}, u32[]{:S(2)}, u32[]{:S(2)}) collective-permute-start(f32[2,2,512,128]{3,2,1,0:T(8,128)S(1)} %slice.12), channel_id=1, source_target_pairs={{1,0},{2,1},{3,2},{4,3},{5,4},{6,5},{7,6},{8,7},{9,8},{10,9},{11,1... | collective-permute-start | bytes 3145736 | tf_op jit(solution)/shard_map/ppermute | solution.py:613
  4.5 12.2 %collective-permute-start.2 = (f32[1,2,128,512]{3,2,1,0:T(8,128)S(1)}, f32[1,2,128,512]{3,2,1,0:T(8,128)S(1)}, u32[]{:S(2)}, u32[]{:S(2)}) collective-permute-start(f32[1,2,128,512]{3,2,1,0:T(8,128)S(1)} %get-tuple-element.28), channel_id=1, source_target_pairs={{16,0},{32,16},{48,32},{64,48},{80,64},{96,80},{112,96},{17,1},{33... | collective-permute-start | bytes 1572872 | tf_op jit(solution)/shard_map/ppermute | solution.py:613
  7.9 14.5 %collective-permute-start.1 = (f32[1,2,128,512]{3,2,1,0:T(8,128)S(1)}, f32[1,2,128,512]{3,2,1,0:T(8,128)S(1)}, u32[]{:S(2)}, u32[]{:S(2)}) collective-permute-start(f32[1,2,128,512]{3,2,1,0:T(8,128)S(1)} %get-tuple-element.29), channel_id=1, source_target_pairs={{16,0},{32,16},{48,32},{64,48},{80,64},{96,80},{112,96},{17,1},{33... | collective-permute-start | bytes 1572872 | tf_op jit(solution)/shard_map/ppermute | solution.py:613
  10.8 30.4 %collective-permute-start.3 = (f32[2,2,128,128]{3,2,1,0:T(8,128)S(1)}, f32[2,2,128,128]{3,2,1,0:T(8,128)}, u32[]{:S(2)}, u32[]{:S(2)}) collective-permute-start(f32[2,2,128,128]{3,2,1,0:T(8,128)S(1)} %slice.15), channel_id=1, source_target_pairs={{17,0},{18,1},{19,2},{20,3},{21,4},{22,5},{23,6},{24,7},{25,8},{26... | collective-permute-start | bytes 786440 | tf_op jit(solution)/shard_map/ppermute | solution.py:613
  16.7 5.6 %copy-start.1 = (f32[1,2,128,512]{3,2,1,0:T(8,128)}, f32[1,2,128,512]{3,2,1,0:T(8,128)S(1)}, u32[]{:S(2)}) copy-start(f32[1,2,128,512]{3,2,1,0:T(8,128)S(1)} %collective-permute-done.2.below_second) | copy-start | bytes 1572868
  22.3 0.8 copy-start.2
  47.4 3.9 %collective-permute-start.4 = (f32[12,128,128]{2,1,0:T(8,128)}, f32[12,128,128]{2,1,0:T(8,128)S(1)}, u32[]{:S(2)}, u32[]{:S(2)}) collective-permute-start(f32[12,128,128]{2,1,0:T(8,128)} %get-tuple-element.19), channel_id=1, source_target_pairs={{0,16},{16,0},{32,48},{48,32},{64,80},{80,64},{96,112},{112,96},{1... | collective-permute-start | bytes 2359304 | tf_op jit(solution)/shard_map/ppermute | solution.py:613
  49.2 54.5 %collective-permute-start.6 = (f32[2,2,384,128]{3,2,1,0:T(8,128)}, f32[2,2,384,128]{3,2,1,0:T(8,128)S(1)}, u32[]{:S(2)}, u32[]{:S(2)}) collective-permute-start(f32[2,2,384,128]{3,2,1,0:T(8,128)} %get-tuple-element.22), channel_id=1, source_target_pairs={{0,1},{1,2},{2,3},{3,4},{4,5},{5,6},{6,7},{7,8},{8,9},{9,10},{10,1... | collective-permute-start | bytes 2359304 | tf_op jit(solution)/shard_map/ppermute | solution.py:613
  53.4 44.6 %all-to-all-start = ((f32[64,24,128]{2,1,0:T(8,128)}), f32[64,24,128]{2,1,0:T(8,128)S(1)}, u32[]{:S(2)}, u32[]{:S(2)}) async-start(f32[64,24,128]{2,1,0:T(8,128)} %bitcast.4), calls=%async_computation | async-start | bytes 1572864 | tf_op jit(solution)/shard_map/all_to_all | solution.py:632
  77.4 26.3 %collective-permute-start.7 = (f32[1,2,128,512]{3,2,1,0:T(8,128)}, f32[1,2,128,512]{3,2,1,0:T(8,128)S(1)}, u32[]{:S(2)}, u32[]{:S(2)}) collective-permute-start(f32[1,2,128,512]{3,2,1,0:T(8,128)} %get-tuple-element.23), channel_id=1, source_target_pairs={{0,16},{16,32},{32,48},{48,64},{64,80},{80,96},{96,112},{1,17},{17... | collective-permute-start | bytes 1572872 | tf_op jit(solution)/shard_map/ppermute | solution.py:613
  81.6 22.1 %collective-permute-start.8 = (f32[1,2,128,512]{3,2,1,0:T(8,128)}, f32[1,2,128,512]{3,2,1,0:T(8,128)}, u32[]{:S(2)}, u32[]{:S(2)}) collective-permute-start(f32[1,2,128,512]{3,2,1,0:T(8,128)} %get-tuple-element.24), channel_id=1, source_target_pairs={{0,16},{16,32},{32,48},{48,64},{64,80},{80,96},{96,112},{1,17},{17... | collective-permute-start | bytes 1572872 | tf_op jit(solution)/shard_map/ppermute | solution.py:613
  83.5 20.2 %collective-permute-start.5 = (f32[2,2,128,128]{3,2,1,0:T(8,128)}, f32[2,2,128,128]{3,2,1,0:T(8,128)S(1)}, u32[]{:S(2)}, u32[]{:S(2)}) collective-permute-start(f32[2,2,128,128]{3,2,1,0:T(8,128)} %get-tuple-element.21), channel_id=1, source_target_pairs={{0,1},{1,2},{2,3},{3,4},{4,5},{5,6},{6,7},{7,8},{8,9},{9,10},{10,1... | collective-permute-start | bytes 786440 | tf_op jit(solution)/shard_map/ppermute | solution.py:613
  86.6 17.1 %collective-permute-start.9 = (f32[2,2,128,128]{3,2,1,0:T(8,128)}, f32[2,2,128,128]{3,2,1,0:T(8,128)}, u32[]{:S(2)}, u32[]{:S(2)}) collective-permute-start(f32[2,2,128,128]{3,2,1,0:T(8,128)} %get-tuple-element.25), channel_id=1, source_target_pairs={{0,17},{1,18},{2,19},{3,20},{4,21},{5,22},{6,23},{7,24},{8,25},{9,... | collective-permute-start | bytes 786440 | tf_op jit(solution)/shard_map/ppermute | solution.py:613
  99.0 18.1 %all-to-all-start.1 = ((f32[64,24,128]{2,1,0:T(8,128)}), f32[64,24,128]{2,1,0:T(8,128)S(1)}, u32[]{:S(2)}, u32[]{:S(2)}) async-start(f32[64,24,128]{2,1,0:T(8,128)} %broadcast_in_dim.2), calls=%async_computation.1 | async-start | bytes 1572864 | tf_op jit(solution)/shard_map/all_to_all | solution.py:639
  103.6 0.9 copy-start.5
  103.7 0.9 copy-start.4
  104.5 0.9 copy-start.3
  105.4 17.2 %copy-start = (f32[12,2,128,128]{3,2,1,0:T(8,128)S(1)}, f32[12,2,128,128]{3,2,1,0:T(8,128)}, u32[]{:S(2)}) copy-start(f32[12,2,128,128]{3,2,1,0:T(8,128)} %param.8) | copy-start | bytes 4718596
  117.1 5.5 %collective-permute-start.10 = (f32[12,128,128]{2,1,0:T(8,128)S(1)}, f32[12,128,128]{2,1,0:T(8,128)S(1)}, u32[]{:S(2)}, u32[]{:S(2)}) collective-permute-start(f32[12,128,128]{2,1,0:T(8,128)S(1)} %bitcast.10), channel_id=1, source_target_pairs={{0,16},{16,0},{32,48},{48,32},{64,80},{80,64},{96,112},{112,96},{1... | collective-permute-start | bytes 2359304 | tf_op jit(solution)/shard_map/ppermute | solution.py:613

commit v4 on v3

--- a/solution.py
+++ b/solution.py
@@ -65,7 +65,9 @@
         [jnp.concatenate([a_re, b_re], axis=1), jnp.concatenate([a_im, b_im], axis=1)], axis=0
     )
     high, low = split(stacked)
-    out = mm(table[0], high) + mm(table[0], low) + mm(table[1], high)
+    both = mm(jnp.concatenate([table[0], table[1]], axis=0), high)
+    side = stacked.shape[0]
+    out = both[:side] + both[side:] + mm(table[0], low)
     w = a_re.shape[0]
     return out[:w, :w], out[w:, :w], out[:w, w:], out[w:, w:]
 
@@ -119,7 +121,7 @@
     down, across, last = pl.ds(rows, width), pl.ds(cols, width), pl.ds(cols - width, width)
     return (
         [(tile.at[:, :, :, last], sheet.at[:, :, pl.ds(0, rows), last])]
-        + [(right, sheet.at[:, :, pl.ds(0, rows), across])]
+        + [(part, sheet.at[:, :, pl.ds(r, part.shape[2]), across]) for r, part in right]
         + [
             (part.at[:, :, :, last], sheet.at[pl.ds(s, 1), :, down, last])
             for s, part in enumerate(below)
@@ -260,7 +262,7 @@
 
 
 def far_kernel(
-    count_ref, pos_ref, core_ref, tile, right, below_first, below_second, corner, probe_in,
+    count_ref, pos_ref, core_ref, tile, top, middle, bottom, below_first, below_second, corner, probe_in,
     pattern_in, step_in, transform_in, pgrad_in, below_in, term_in,
     keep_out, give_out, right_top_out, right_rest_out, below_first_out, below_second_out,
     corner_out, term_out,
@@ -271,6 +273,7 @@
     planes = probe.shape[0]
     rows, cols = tile.shape[2:]
     down, across, inner = pl.ds(rows, width), pl.ds(cols, width), pl.ds(0, cols)
+    right = [(0, top), (top.shape[2], middle), (rows - bottom.shape[2], bottom)]
     loads = start_all(
         far_sheet(tile, right, (below_first, below_second), corner, sheet, width)
         + [(probe_in, probe), (step_in, steps), (transform_in, transforms), (pattern_in, patterns)]
@@ -441,10 +444,10 @@
             shape(2, 2, width, width),
             shape(capacity, 2, 2, width, width),
         ],
-        in_specs=[SMEM, SMEM, SMEM] + [ANY] * 12,
+        in_specs=[SMEM, SMEM, SMEM] + [ANY] * 14,
         out_specs=[ANY] * 8,
-        scratch_shapes=slot_scratch(rows, cols, capacity, probe, *tables, 11, 7),
-        input_output_aliases={14: 7},
+        scratch_shapes=slot_scratch(rows, cols, capacity, probe, *tables, 13, 7),
+        input_output_aliases={16: 7},
         compiler_params=params(60),
         cost_estimate=work(4 * capacity * planes),
         name="far_slots",
@@ -526,7 +529,7 @@
 
             zero = jnp.zeros((sub, width), f32)
             result = lax.fori_loop(
-                0, chunks, accumulate, [(zero, zero) for _ in pairs], unroll=4
+                0, chunks, accumulate, [(zero, zero) for _ in pairs], unroll=16
             )
             for (j, k), (acc_re, acc_im) in zip(pairs, result):
                 s_re = jnp.sum(acc_re, axis=0, keepdims=True)
@@ -651,15 +654,21 @@
     swap = [(r, r ^ 1) for r in range(rows)]
     groups = core_groups(rows, cols, 2)
 
-    right = moved(object_slices[:, :, :, :width], "col", left_one)
+    edge = object_slices[:, :, :, :width]
+    first = width + 32
+    second = (first + edge.shape[2]) // 2
+    right = [
+        moved(edge[:, :, begin:end], "col", left_one)
+        for begin, end in ((0, first), (first, second), (second, edge.shape[2]))
+    ]
     below = [moved(object_slices[s : s + 1, :, :width, :], "row", up_one) for s in range(2)]
-    corner = moved(object_slices[:, :, :width, :width], ("row", "col"), shifted_both(rows, cols, -1))
+    corner = moved(right[0][:, :, :width], "row", up_one)
     tables = [jnp.asarray(t) for t in make_tables(width)]
     probe_sum, terms, below_sum = near_slots(
         counts, spots, object_slices, below, planes, measured[0], tables, 1
     )
     keep, give, right_top, right_rest, *below_grads, corner_grad, terms = far_slots(
-        counts, spots, core, object_slices, (right, *below, corner), planes, measured[0],
+        counts, spots, core, object_slices, (*right, *below, corner), planes, measured[0],
         tables, (probe_sum, below_sum, terms),
     )
     keep = keep + moved(give, "row", swap)

time: 131 us -> 131 us (level); the launches traced: 129 us -> 133 us
  starting transfers between devices: 57.8 us -> 62.5 us
    ppermute x11 -> x13, waiting for transfers between devices: 12.3 us -> 8.24 us  [moved(): return lax.ppermute(shard, axes, pairs)]
    all_to_all x1, starting transfers between devices: 4.64 us -> 8.24 us  [gather_shares(): return lax.all_to_all(parts, ('row', 'col'), 0, 0, axis_index_groups=groups)]
    all_to_all x1, waiting for transfers between devices: 5.93 us -> 8.86 us  [sum_share(): lax.all_to_all(parts, ('row', 'col'), 0, 0, axis_index_groups=groups)]
    ppermute x11 -> x13, starting transfers between devices: 29.2 us -> 30.4 us  [moved(): return lax.ppermute(shard, axes, pairs)]
  transfers between devices with their start and end apart: 13 -> 15, of which waited for: 6 -> 5; matrix products, arithmetic and copies ran while one was open for 4% -> 4% of each run, Pallas kernels for 19% -> 18%
where the time goes in v4:
time: 131 us; the launch traced here: 133 us
  starting transfers between devices  62.5 us (48%)
  Pallas kernels  36.1 us (28%)
  waiting for transfers between devices  23.5 us (18%)
  local copies, waits for them, and re-layouts  6.93 us (5%)
  other arithmetic  2.18 us (2%)
  between operations  1.74 us (1%)
    ppermute x13, starting transfers between devices, moved(): return lax.ppermute(shard, axes, pairs)  30.4 us
    all_to_all x1, starting transfers between devices, sum_share(): lax.all_to_all(parts, ('row', 'col'), 0, 0, axis_index_groups=groups)  23.8 us
    pallas_call x1, Pallas kernels, near_slots(): pl.pallas_call(near_kernel, out_shape=[shape(*probe.shape), shape(capacit...  17.7 us
    all_to_all x1, waiting for transfers between devices, sum_share(): lax.all_to_all(parts, ('row', 'col'), 0, 0, axis_index_groups=groups)  8.86 us
    all_to_all x1, starting transfers between devices, gather_shares(): return lax.all_to_all(parts, ('row', 'col'), 0, 0, axis_index_groups=groups)  8.24 us
    ppermute x13, waiting for transfers between devices, moved(): return lax.ppermute(shard, axes, pairs)  8.24 us
    pallas_call x1, Pallas kernels, settle(): pl.pallas_call(settle_kernel, out_shape=shape(*tile.shape), in_specs=[SME...  6.47 us
    all_to_all x1, waiting for transfers between devices, gather_shares(): return lax.all_to_all(parts, ('row', 'col'), 0, 0, axis_index_groups=groups)  6.45 us
  transfers between devices with their start and end apart: 15, of which 5 were waited for; matrix products, arithmetic and copies ran while one was open for 4% of the time, Pallas kernels for 18%

profile of v4, /device:TPU:1, one launch (start us, length us, event | category | flops | bytes accessed | tf_op | source)
XLA Modules:
  0.0 133.0 jit_solution(12285454382571540535)
XLA Ops:
  0.6 1.0 slice.22
  1.6 1.3 collective-permute-start
  2.9 1.3 fusion
  4.2 3.3 %collective-permute-start.4 = (f32[1,2,128,512]{3,2,1,0:T(8,128)S(1)}, f32[1,2,128,512]{3,2,1,0:T(8,128)S(1)}, u32[]{:S(2)}, u32[]{:S(2)}) collective-permute-start(f32[1,2,128,512]{3,2,1,0:T(8,128)S(1)} %get-tuple-element.28), channel_id=1, source_target_pairs={{16,0},{32,16},{48,32},{64,48},{80,64},{96,80},{112,96},{17,1},{33... | collective-permute-start | bytes 1572872 | tf_op jit(solution)/shard_map/ppermute | solution.py:616
  7.6 1.9 %collective-permute-start.3 = (f32[1,2,128,512]{3,2,1,0:T(8,128)S(1)}, f32[1,2,128,512]{3,2,1,0:T(8,128)S(1)}, u32[]{:S(2)}, u32[]{:S(2)}) collective-permute-start(f32[1,2,128,512]{3,2,1,0:T(8,128)S(1)} %get-tuple-element.29), channel_id=1, source_target_pairs={{16,0},{32,16},{48,32},{64,48},{80,64},{96,80},{112,96},{17,1},{33... | collective-permute-start | bytes 1572872 | tf_op jit(solution)/shard_map/ppermute | solution.py:616
  9.5 1.2 fusion.1
  10.7 1.3 collective-permute-start.2
  12.0 1.3 collective-permute-start.1
  13.3 0.0 collective-permute-done.top
  13.3 0.0 copy-start.3
  13.3 2.9 %collective-permute-start.5 = (f32[2,2,128,128]{3,2,1,0:T(8,128)S(1)}, f32[2,2,128,128]{3,2,1,0:T(8,128)}, u32[]{:S(2)}, u32[]{:S(2)}) collective-permute-start(f32[2,2,128,128]{3,2,1,0:T(8,128)S(1)} %slice.28), channel_id=1, source_target_pairs={{16,0},{32,16},{48,32},{64,48},{80,64},{96,80},{112,96},{17,1},{33... | collective-permute-start | bytes 786440 | tf_op jit(solution)/shard_map/ppermute | solution.py:616
  16.8 0.0 collective-permute-done.4.below_second
  16.9 0.0 copy-start.1
  16.9 5.2 %collective-permute-done.3.below_first = f32[1,2,128,512]{3,2,1,0:T(8,128)S(1)} collective-permute-done((f32[1,2,128,512]{3,2,1,0:T(8,128)S(1)}, f32[1,2,128,512]{3,2,1,0:T(8,128)S(1)}, u32[]{:S(2)}, u32[]{:S(2)}) %collective-permute-start.3) | collective-permute-done | bytes 524320 | tf_op jit(solution)/shard_map/ppermute | solution.py:616
  22.0 0.0 copy-start.2
  22.0 0.0 copy-done.1
  22.0 0.8 copy-done.2
  22.8 17.7 %near_slots.1 = (f32[24,128,128]{2,1,0:T(8,128)}, f32[4,2,2,128,128]{4,3,2,1,0:T(8,128)}, f32[2,2,128,512]{3,2,1,0:T(8,128)}) custom-call(s32[1,1]{1,0:T(1,128)S(6)} %copy.11.count_ref, s32[2,4]{1,0:T(2,128)} %bitcast.15, f32[2,2,512,512]{3,2,1,0:T(8,128)} %tile.5, f32[1,2,128,512]{3,2,1,0:T(8,128)} %copy-done.2, f32[1,2,128,512]{3,2,1,0:T(8,128)} %copy-done.1, ...), custom_call_target="tpu_custom_call" | custom-call | flops 33554432 | bytes 8388608 | tf_op jit(solution)/shard_map/near_slots/pallas_call | solution.py:414
  40.5 0.0 copy-done.3
  40.5 0.0 collective-permute-done.2.bottom
  40.5 0.0 collective-permute-done.1.middle
  40.5 0.0 collective-permute-done.5.corner
  40.5 6.2 %far_slots.1 = (f32[12,128,128]{2,1,0:T(8,128)}, f32[12,128,128]{2,1,0:T(8,128)}, f32[2,2,128,128]{3,2,1,0:T(8,128)}, f32[2,2,384,128]{3,2,1,0:T(8,128)}, f32[1,...) custom-call(s32[1,1]{1,0:T(1,128)S(6)} %copy.11.count_ref, ...), custom_call_target="tpu_custom_call", output_to_operand_aliasing={{7}: (16, {})} | custom-call | flops 12884901888 | bytes 8388608 | tf_op jit(solution)/shard_map/far_slots/pallas_call | solution.py:435
  46.8 0.1 collective-permute-start.6
  46.9 1.3 %collective-permute-start.8 = (f32[2,2,384,128]{3,2,1,0:T(8,128)}, f32[2,2,384,128]{3,2,1,0:T(8,128)S(1)}, u32[]{:S(2)}, u32[]{:S(2)}) collective-permute-start(f32[2,2,384,128]{3,2,1,0:T(8,128)} %get-tuple-element.22), channel_id=1, source_target_pairs={{0,1},{1,2},{2,3},{3,4},{4,5},{5,6},{6,7},{7,8},{8,9},{9,10},{10,1... | collective-permute-start | bytes 2359304 | tf_op jit(solution)/shard_map/ppermute | solution.py:616
  48.2 1.1 collective-permute-done.6
  49.3 2.1 %add.8 = f32[12,128,128]{2,1,0:T(8,128)} add(f32[12,128,128]{2,1,0:T(8,128)} %get-tuple-element.18, f32[12,128,128]{2,1,0:T(8,128)S(1)} %collective-permute-done.6) | non-fusion elementwise | flops 196608 | bytes 2359296 | tf_op jit(solution)/shard_map/add | solution.py:674
  51.4 23.8 %all-to-all-start = ((f32[64,24,128]{2,1,0:T(8,128)}), f32[64,24,128]{2,1,0:T(8,128)S(1)}, u32[]{:S(2)}, u32[]{:S(2)}) async-start(f32[64,24,128]{2,1,0:T(8,128)} %bitcast.4), calls=%async_computation | async-start | bytes 1572864 | tf_op jit(solution)/shard_map/all_to_all | solution.py:635
  75.3 4.1 %collective-permute-start.9 = (f32[1,2,128,512]{3,2,1,0:T(8,128)}, f32[1,2,128,512]{3,2,1,0:T(8,128)S(1)}, u32[]{:S(2)}, u32[]{:S(2)}) collective-permute-start(f32[1,2,128,512]{3,2,1,0:T(8,128)} %get-tuple-element.23), channel_id=1, source_target_pairs={{0,16},{16,32},{32,48},{48,64},{64,80},{80,96},{96,112},{1,17},{17... | collective-permute-start | bytes 1572872 | tf_op jit(solution)/shard_map/ppermute | solution.py:616
  79.4 1.9 %collective-permute-start.10 = (f32[1,2,128,512]{3,2,1,0:T(8,128)}, f32[1,2,128,512]{3,2,1,0:T(8,128)}, u32[]{:S(2)}, u32[]{:S(2)}) collective-permute-start(f32[1,2,128,512]{3,2,1,0:T(8,128)} %get-tuple-element.24), channel_id=1, source_target_pairs={{0,16},{16,32},{32,48},{48,64},{64,80},{80,96},{96,112},{1,17},{17... | collective-permute-start | bytes 1572872 | tf_op jit(solution)/shard_map/ppermute | solution.py:616
  81.3 3.1 %collective-permute-start.7 = (f32[2,2,128,128]{3,2,1,0:T(8,128)}, f32[2,2,128,128]{3,2,1,0:T(8,128)S(1)}, u32[]{:S(2)}, u32[]{:S(2)}) collective-permute-start(f32[2,2,128,128]{3,2,1,0:T(8,128)} %get-tuple-element.21), channel_id=1, source_target_pairs={{0,1},{1,2},{2,3},{3,4},{4,5},{5,6},{6,7},{7,8},{8,9},{9,10},{10,1... | collective-permute-start | bytes 786440 | tf_op jit(solution)/shard_map/ppermute | solution.py:616
  84.4 5.4 %collective-permute-start.11 = (f32[2,2,128,128]{3,2,1,0:T(8,128)}, f32[2,2,128,128]{3,2,1,0:T(8,128)}, u32[]{:S(2)}, u32[]{:S(2)}) collective-permute-start(f32[2,2,128,128]{3,2,1,0:T(8,128)} %get-tuple-element.25), channel_id=1, source_target_pairs={{0,17},{1,18},{2,19},{3,20},{4,21},{5,22},{6,23},{7,24},{8,25},{9,... | collective-permute-start | bytes 786440 | tf_op jit(solution)/shard_map/ppermute | solution.py:616
  89.9 8.9 %all-to-all-done = f32[64,24,128]{2,1,0:T(8,128)S(1)} async-done(((f32[64,24,128]{2,1,0:T(8,128)}), f32[64,24,128]{2,1,0:T(8,128)S(1)}, u32[]{:S(2)}, u32[]{:S(2)}) %all-to-all-start) | async-done | bytes 786464 | tf_op jit(solution)/shard_map/all_to_all | solution.py:635
  98.7 0.1 reduce_sum.9
  98.8 0.9 broadcast_in_dim.2
  99.8 8.2 %all-to-all-start.1 = ((f32[64,24,128]{2,1,0:T(8,128)}), f32[64,24,128]{2,1,0:T(8,128)S(1)}, u32[]{:S(2)}, u32[]{:S(2)}) async-start(f32[64,24,128]{2,1,0:T(8,128)} %broadcast_in_dim.2), calls=%async_computation.1 | async-start | bytes 1572864 | tf_op jit(solution)/shard_map/all_to_all | solution.py:642
  108.0 0.0 collective-permute-done.7.left_top_in
  108.0 0.0 copy-start.6
  108.0 0.0 collective-permute-done.11.corner_in
  108.0 0.0 collective-permute-done.9.above_first_in
  108.0 0.0 copy-start.5
  108.1 0.0 collective-permute-done.10.above_second_in
  108.1 0.0 collective-permute-done.8.left_rest_in
  108.1 0.8 copy-done.5
  108.9 0.0 copy-start.4
  108.9 0.0 copy-done.6
  108.9 0.9 copy-done.4
  109.8 0.0 copy-start
  109.8 6.5 %settle.1 = f32[2,2,512,512]{3,2,1,0:T(8,128)} custom-call(s32[1,1]{1,0:T(1,128)S(6)} %copy.11.count_ref, s32[2,4]{1,0:T(2,128)} %bitcast.17, f32[2,2,512,512]{3,2,1,0:T(8,128)} %tile.5, f32[4,2,2,128,128]{4,3,2,1,0:T(8,128)} %get-tuple-element.20.term_in, f32[2,2,128,128]{3,2,1,0:T(8,128)} %copy-done.6, f32[2,2,384,128]{3,2,1,0:T(8,128)} %copy-done.4, ...), custom_call_target="tpu_custom_call" | custom-call | flops 137438953472 | bytes 8388608 | tf_op jit(solution)/shard_map/settle/pallas_call | solution.py:460
  116.3 6.4 %all-to-all-done.1 = f32[64,24,128]{2,1,0:T(8,128)S(1)} async-done(((f32[64,24,128]{2,1,0:T(8,128)}), f32[64,24,128]{2,1,0:T(8,128)S(1)}, u32[]{:S(2)}, u32[]{:S(2)}) %all-to-all-start.1) | async-done | bytes 786464 | tf_op jit(solution)/shard_map/all_to_all | solution.py:642
  122.7 2.4 %collective-permute-start.12 = (f32[12,128,128]{2,1,0:T(8,128)S(1)}, f32[12,128,128]{2,1,0:T(8,128)S(1)}, u32[]{:S(2)}, u32[]{:S(2)}) collective-permute-start(f32[12,128,128]{2,1,0:T(8,128)S(1)} %bitcast.10), channel_id=1, source_target_pairs={{0,16},{16,0},{32,48},{48,32},{64,80},{80,64},{96,112},{112,96},{1... | collective-permute-start | bytes 2359304 | tf_op jit(solution)/shard_map/ppermute | solution.py:616
  125.1 1.9 %collective-permute-done.12.other = f32[12,128,128]{2,1,0:T(8,128)S(1)} collective-permute-done((f32[12,128,128]{2,1,0:T(8,128)S(1)}, f32[12,128,128]{2,1,0:T(8,128)S(1)}, u32[]{:S(2)}, u32[]{:S(2)}) %collective-permute-start.12) | collective-permute-done | bytes 786464 | tf_op jit(solution)/shard_map/ppermute | solution.py:616
  127.0 0.0 copy-done
  127.0 5.8 %orthogonalize.1 = f32[24,128,128]{2,1,0:T(8,128)} custom-call(s32[1,1]{1,0:T(1,128)} %bitcast.1.core_ref, f32[24,128,128]{2,1,0:T(8,128)S(1)} %bitcast.9, f32[12,128,128]{2,1,0:T(8,128)S(1)} %bitcast.11, f32[12,128,128]{2,1,0:T(8,128)S(1)} %collective-permute-done.12.other), custom_call_target="tpu_custom_call" | custom-call | tf_op jit(solution)/shard_map/orthogonalize/pallas_call | solution.py:597
  (1 shorter events, 0.0 us)
Async XLA Ops:
  1.6 11.6 %collective-permute-start = (f32[2,2,160,128]{3,2,1,0:T(8,128)S(1)}, f32[2,2,160,128]{3,2,1,0:T(8,128)S(1)}, u32[]{:S(2)}, u32[]{:S(2)}) collective-permute-start(f32[2,2,160,128]{3,2,1,0:T(8,128)S(1)} %slice.22), channel_id=1, source_target_pairs={{1,0},{2,1},{3,2},{4,3},{5,4},{6,5},{7,6},{8,7},{9,8},{10,9},{11,1... | collective-permute-start | bytes 983048 | tf_op jit(solution)/shard_map/ppermute | solution.py:616
  4.2 12.6 %collective-permute-start.4 = (f32[1,2,128,512]{3,2,1,0:T(8,128)S(1)}, f32[1,2,128,512]{3,2,1,0:T(8,128)S(1)}, u32[]{:S(2)}, u32[]{:S(2)}) collective-permute-start(f32[1,2,128,512]{3,2,1,0:T(8,128)S(1)} %get-tuple-element.28), channel_id=1, source_target_pairs={{16,0},{32,16},{48,32},{64,48},{80,64},{96,80},{112,96},{17,1},{33... | collective-permute-start | bytes 1572872 | tf_op jit(solution)/shard_map/ppermute | solution.py:616
  7.6 14.5 %collective-permute-start.3 = (f32[1,2,128,512]{3,2,1,0:T(8,128)S(1)}, f32[1,2,128,512]{3,2,1,0:T(8,128)S(1)}, u32[]{:S(2)}, u32[]{:S(2)}) collective-permute-start(f32[1,2,128,512]{3,2,1,0:T(8,128)S(1)} %get-tuple-element.29), channel_id=1, source_target_pairs={{16,0},{32,16},{48,32},{64,48},{80,64},{96,80},{112,96},{17,1},{33... | collective-permute-start | bytes 1572872 | tf_op jit(solution)/shard_map/ppermute | solution.py:616
  10.7 29.8 %collective-permute-start.2 = (f32[2,2,176,128]{3,2,1,0:T(8,128)S(1)}, f32[2,2,176,128]{3,2,1,0:T(8,128)}, u32[]{:S(2)}, u32[]{:S(2)}) collective-permute-start(f32[2,2,176,128]{3,2,1,0:T(8,128)S(1)} %get-tuple-element.30), channel_id=1, source_target_pairs={{1,0},{2,1},{3,2},{4,3},{5,4},{6,5},{7,6},{8,7},{9,8},{10,9},{11,1... | collective-permute-start | bytes 1081352 | tf_op jit(solution)/shard_map/ppermute | solution.py:616
  12.0 28.6 %collective-permute-start.1 = (f32[2,2,176,128]{3,2,1,0:T(8,128)S(1)}, f32[2,2,176,128]{3,2,1,0:T(8,128)}, u32[]{:S(2)}, u32[]{:S(2)}) collective-permute-start(f32[2,2,176,128]{3,2,1,0:T(8,128)S(1)} %get-tuple-element.31), channel_id=1, source_target_pairs={{1,0},{2,1},{3,2},{4,3},{5,4},{6,5},{7,6},{8,7},{9,8},{10,9},{11,1... | collective-permute-start | bytes 1081352 | tf_op jit(solution)/shard_map/ppermute | solution.py:616
  13.3 27.2 %copy-start.3 = (f32[2,2,160,128]{3,2,1,0:T(8,128)}, f32[2,2,160,128]{3,2,1,0:T(8,128)S(1)}, u32[]{:S(2)}) copy-start(f32[2,2,160,128]{3,2,1,0:T(8,128)S(1)} %collective-permute-done.top) | copy-start | bytes 983044
  13.3 27.2 %collective-permute-start.5 = (f32[2,2,128,128]{3,2,1,0:T(8,128)S(1)}, f32[2,2,128,128]{3,2,1,0:T(8,128)}, u32[]{:S(2)}, u32[]{:S(2)}) collective-permute-start(f32[2,2,128,128]{3,2,1,0:T(8,128)S(1)} %slice.28), channel_id=1, source_target_pairs={{16,0},{32,16},{48,32},{64,48},{80,64},{96,80},{112,96},{17,1},{33... | collective-permute-start | bytes 786440 | tf_op jit(solution)/shard_map/ppermute | solution.py:616
  16.9 5.2 %copy-start.1 = (f32[1,2,128,512]{3,2,1,0:T(8,128)}, f32[1,2,128,512]{3,2,1,0:T(8,128)S(1)}, u32[]{:S(2)}) copy-start(f32[1,2,128,512]{3,2,1,0:T(8,128)S(1)} %collective-permute-done.4.below_second) | copy-start | bytes 1572868
  22.0 0.8 copy-start.2
  46.8 2.6 %collective-permute-start.6 = (f32[12,128,128]{2,1,0:T(8,128)}, f32[12,128,128]{2,1,0:T(8,128)S(1)}, u32[]{:S(2)}, u32[]{:S(2)}) collective-permute-start(f32[12,128,128]{2,1,0:T(8,128)} %get-tuple-element.19), channel_id=1, source_target_pairs={{0,16},{16,0},{32,48},{48,32},{64,80},{80,64},{96,112},{112,96},{1... | collective-permute-start | bytes 2359304 | tf_op jit(solution)/shard_map/ppermute | solution.py:616
  46.9 61.2 %collective-permute-start.8 = (f32[2,2,384,128]{3,2,1,0:T(8,128)}, f32[2,2,384,128]{3,2,1,0:T(8,128)S(1)}, u32[]{:S(2)}, u32[]{:S(2)}) collective-permute-start(f32[2,2,384,128]{3,2,1,0:T(8,128)} %get-tuple-element.22), channel_id=1, source_target_pairs={{0,1},{1,2},{2,3},{3,4},{4,5},{5,6},{6,7},{7,8},{8,9},{9,10},{10,1... | collective-permute-start | bytes 2359304 | tf_op jit(solution)/shard_map/ppermute | solution.py:616
  51.4 47.3 %all-to-all-start = ((f32[64,24,128]{2,1,0:T(8,128)}), f32[64,24,128]{2,1,0:T(8,128)S(1)}, u32[]{:S(2)}, u32[]{:S(2)}) async-start(f32[64,24,128]{2,1,0:T(8,128)} %bitcast.4), calls=%async_computation | async-start | bytes 1572864 | tf_op jit(solution)/shard_map/all_to_all | solution.py:635
  75.3 32.8 %collective-permute-start.9 = (f32[1,2,128,512]{3,2,1,0:T(8,128)}, f32[1,2,128,512]{3,2,1,0:T(8,128)S(1)}, u32[]{:S(2)}, u32[]{:S(2)}) collective-permute-start(f32[1,2,128,512]{3,2,1,0:T(8,128)} %get-tuple-element.23), channel_id=1, source_target_pairs={{0,16},{16,32},{32,48},{48,64},{64,80},{80,96},{96,112},{1,17},{17... | collective-permute-start | bytes 1572872 | tf_op jit(solution)/shard_map/ppermute | solution.py:616
  79.4 28.7 %collective-permute-start.10 = (f32[1,2,128,512]{3,2,1,0:T(8,128)}, f32[1,2,128,512]{3,2,1,0:T(8,128)}, u32[]{:S(2)}, u32[]{:S(2)}) collective-permute-start(f32[1,2,128,512]{3,2,1,0:T(8,128)} %get-tuple-element.24), channel_id=1, source_target_pairs={{0,16},{16,32},{32,48},{48,64},{64,80},{80,96},{96,112},{1,17},{17... | collective-permute-start | bytes 1572872 | tf_op jit(solution)/shard_map/ppermute | solution.py:616
  81.3 26.7 %collective-permute-start.7 = (f32[2,2,128,128]{3,2,1,0:T(8,128)}, f32[2,2,128,128]{3,2,1,0:T(8,128)S(1)}, u32[]{:S(2)}, u32[]{:S(2)}) collective-permute-start(f32[2,2,128,128]{3,2,1,0:T(8,128)} %get-tuple-element.21), channel_id=1, source_target_pairs={{0,1},{1,2},{2,3},{3,4},{4,5},{5,6},{6,7},{7,8},{8,9},{9,10},{10,1... | collective-permute-start | bytes 786440 | tf_op jit(solution)/shard_map/ppermute | solution.py:616
  84.4 23.6 %collective-permute-start.11 = (f32[2,2,128,128]{3,2,1,0:T(8,128)}, f32[2,2,128,128]{3,2,1,0:T(8,128)}, u32[]{:S(2)}, u32[]{:S(2)}) collective-permute-start(f32[2,2,128,128]{3,2,1,0:T(8,128)} %get-tuple-element.25), channel_id=1, source_target_pairs={{0,17},{1,18},{2,19},{3,20},{4,21},{5,22},{6,23},{7,24},{8,25},{9,... | collective-permute-start | bytes 786440 | tf_op jit(solution)/shard_map/ppermute | solution.py:616
  99.8 23.0 %all-to-all-start.1 = ((f32[64,24,128]{2,1,0:T(8,128)}), f32[64,24,128]{2,1,0:T(8,128)S(1)}, u32[]{:S(2)}, u32[]{:S(2)}) async-start(f32[64,24,128]{2,1,0:T(8,128)} %broadcast_in_dim.2), calls=%async_computation.1 | async-start | bytes 1572864 | tf_op jit(solution)/shard_map/all_to_all | solution.py:642
  108.0 0.9 copy-start.6
  108.0 0.9 copy-start.5
  108.9 0.9 copy-start.4
  109.8 17.2 %copy-start = (f32[12,2,128,128]{3,2,1,0:T(8,128)S(1)}, f32[12,2,128,128]{3,2,1,0:T(8,128)}, u32[]{:S(2)}) copy-start(f32[12,2,128,128]{3,2,1,0:T(8,128)} %param.8) | copy-start | bytes 4718596
  122.7 4.3 %collective-permute-start.12 = (f32[12,128,128]{2,1,0:T(8,128)S(1)}, f32[12,128,128]{2,1,0:T(8,128)S(1)}, u32[]{:S(2)}, u32[]{:S(2)}) collective-permute-start(f32[12,128,128]{2,1,0:T(8,128)S(1)} %bitcast.10), channel_id=1, source_target_pairs={{0,16},{16,0},{32,48},{48,32},{64,80},{80,64},{96,112},{112,96},{1... | collective-permute-start | bytes 2359304 | tf_op jit(solution)/shard_map/ppermute | solution.py:616

commit v5 on v4

--- a/solution.py
+++ b/solution.py
@@ -324,44 +324,56 @@
     return lambda: lax.fori_loop(0, count, finish, 0)
 
 
-def settle_kernel(
-    count_ref, pos_ref, tile, term_in, left_top_in, left_rest_in, above_first_in, above_second_in, corner_in,
-    tile_out,
-    sheet, terms, left, above, corner, sem_term, sem_in, sem_out,
-):
-    width = above_first_in.shape[2]
+def inside_kernel(count_ref, pos_ref, tile, term_in, tile_out, sheet, terms, sem_term, sems):
+    width = terms.shape[-1]
     rows, cols = tile.shape[2:]
     count = count_ref[0, 0]
     inner = sheet.at[:, :, pl.ds(0, rows), pl.ds(0, cols)]
-    sources = [
-        (tile, inner),
-        (left_top_in, left.at[:, :, pl.ds(0, width)]),
-        (left_rest_in, left.at[:, :, pl.ds(width, rows - width)]),
-        (above_first_in, above.at[pl.ds(0, 1)]),
-        (above_second_in, above.at[pl.ds(1, 1)]),
-        (corner_in, corner),
-    ]
-    loads = [
-        pltpu.make_async_copy(src, dst, sem_in.at[i]) for i, (src, dst) in enumerate(sources)
-    ]
-    for copy in loads:
-        copy.start()
+    load = pltpu.make_async_copy(tile, inner, sems.at[0])
+    load.start()
     wait = load_terms(count, term_in, terms, sem_term)
-    for copy in loads:
-        copy.wait()
+    load.wait()
     wait()
-    sheet[:, :, 0:rows, 0:width] += left[...]
-    sheet[:, :, 0:width, 0:cols] += above[...]
-    sheet[:, :, 0:width, 0:width] += corner[...]
 
     def visit(slot, carry):
         subtract_terms(slot, pos_ref, terms, sheet, width)
         return carry
 
     lax.fori_loop(0, count, visit, 0)
-    store = pltpu.make_async_copy(inner, tile_out, sem_out.at[0])
+    store = pltpu.make_async_copy(inner, tile_out, sems.at[1])
     store.start()
     store.wait()
+
+
+def settle_kernel(
+    partial, left_top_in, left_rest_in, above_first_in, above_second_in, corner_in, tile_out,
+    side, head, left, above, corner, sem_in, sem_out,
+):
+    width = corner_in.shape[-1]
+    rows, cols = partial.shape[2:]
+    edge, rest = pl.ds(0, width), pl.ds(width, cols - width)
+    loads = start_all(
+        [
+            (partial.at[:, :, :, edge], side),
+            (partial.at[:, :, edge, rest], head),
+            (left_top_in, left.at[:, :, pl.ds(0, width)]),
+            (left_rest_in, left.at[:, :, pl.ds(width, rows - width)]),
+            (above_first_in, above.at[pl.ds(0, 1)]),
+            (above_second_in, above.at[pl.ds(1, 1)]),
+            (corner_in, corner),
+        ],
+        sem_in,
+    )
+    for copy in loads:
+        copy.wait()
+    side[...] += left[...]
+    side[:, :, 0:width] += above[:, :, :, 0:width] + corner[...]
+    head[...] += above[:, :, :, width:cols]
+    stores = start_all(
+        [(side, tile_out.at[:, :, :, edge]), (head, tile_out.at[:, :, edge, rest])], sem_out
+    )
+    for copy in stores:
+        copy.wait()
 
 
 VMEM = pl.BlockSpec(memory_space=pltpu.VMEM)
@@ -454,28 +466,48 @@
     )(counts, positions, core, tile, *halo, probe, patterns, *tables, *sums)
 
 
-def settle(counts, positions, tile, terms, left, above, corner):
+def inside(counts, positions, tile, terms):
     capacity, width = terms.shape[0], terms.shape[-1]
     rows, cols = tile.shape[2:]
     return pl.pallas_call(
-        settle_kernel,
+        inside_kernel,
         out_shape=shape(*tile.shape),
-        in_specs=[SMEM, SMEM] + [ANY] * 7,
+        in_specs=[SMEM, SMEM, ANY, ANY],
         out_specs=ANY,
         scratch_shapes=[
             pltpu.VMEM((2, 2, rows + width + 8, cols + 2 * width), f32),
             pltpu.VMEM(terms.shape, f32),
+            DMA((capacity,)),
+            DMA((2,)),
+        ],
+        compiler_params=params(60),
+        cost_estimate=work(8),
+        name="inside",
+    )(counts, positions, tile, terms)
+
+
+def settle(partial, left, above, corner):
+    width = corner.shape[-1]
+    rows, cols = partial.shape[2:]
+    return pl.pallas_call(
+        settle_kernel,
+        out_shape=shape(*partial.shape),
+        in_specs=[ANY] * 6,
+        out_specs=ANY,
+        scratch_shapes=[
+            pltpu.VMEM((2, 2, rows, width), f32),
+            pltpu.VMEM((2, 2, width, cols - width), f32),
             pltpu.VMEM((2, 2, rows, width), f32),
             pltpu.VMEM((2, 2, width, cols), f32),
             pltpu.VMEM(corner.shape, f32),
-            DMA((capacity,)),
-            DMA((6,)),
-            DMA((1,)),
+            DMA((7,)),
+            DMA((2,)),
         ],
+        input_output_aliases={0: 0},
         compiler_params=params(60),
         cost_estimate=work(4096),
         name="settle",
-    )(counts, positions, tile, terms, *left, *above, corner)
+    )(partial, *left, *above, corner)
 
 
 def core_groups(rows, cols, split):
@@ -678,7 +710,8 @@
     above = [moved(part, "row", down_one) for part in below_grads]
     share = sum_share(keep, groups)
     mine = gather_shares(share, groups).reshape(keep.shape)
-    object_next = settle(counts, spots, object_slices, terms, (left_top, left_rest), above, from_corner)
+    partial = inside(counts, spots, object_slices, terms)
+    object_next = settle(partial, (left_top, left_rest), above, from_corner)
     mine, object_next = lax.optimization_barrier((mine, object_next))
     other = moved(mine, "row", swap)
     divisor = math.sqrt(rows * cols * capacity)

time: 131 us -> 130 us (level); the launches traced: 133 us -> 128 us
  waiting for transfers between devices: 23.5 us -> 18.2 us
  Pallas kernels: 36.1 us -> 38.8 us
  starting transfers between devices: 62.5 us -> 60.6 us
    all_to_all x1, waiting for transfers between devices: 8.86 us -> 1.64 us  [sum_share(): lax.all_to_all(parts, ('row', 'col'), 0, 0, axis_index_groups=groups)]
    all_to_all x1, starting transfers between devices: 8.24 us -> 5.25 us  [gather_shares(): return lax.all_to_all(parts, ('row', 'col'), 0, 0, axis_index_groups=groups)]
    pallas_call x1 -> x2, Pallas kernels: 6.47 us -> 8.99 us  [the longest x1 5.38 us: inside(): pl.pallas_call(inside_kernel, out_shape=shape(*tile.shape), in_specs=[SME...]
    all_to_all x1, waiting for transfers between devices: 6.45 us -> 8.34 us  [gather_shares(): return lax.all_to_all(parts, ('row', 'col'), 0, 0, axis_index_groups=groups)]
  transfers between devices with their start and end apart: 15 -> 15, of which waited for: 5 -> 5; matrix products, arithmetic and copies ran while one was open for 4% -> 4% of each run, Pallas kernels for 18% -> 21%
where the time goes in v5:
time: 130 us; the launch traced here: 128 us
  starting transfers between devices  60.6 us (47%)
  Pallas kernels  38.8 us (30%)
  waiting for transfers between devices  18.2 us (14%)
  local copies, waits for them, and re-layouts  6.76 us (5%)
  other arithmetic  2.18 us (2%)
  between operations  1.75 us (1%)
    ppermute x13, starting transfers between devices, moved(): return lax.ppermute(shard, axes, pairs)  31.3 us
    all_to_all x1, starting transfers between devices, sum_share(): lax.all_to_all(parts, ('row', 'col'), 0, 0, axis_index_groups=groups)  24.1 us
    pallas_call x1, Pallas kernels, near_slots(): pl.pallas_call(near_kernel, out_shape=[shape(*probe.shape), shape(capacit...  17.7 us
    all_to_all x1, waiting for transfers between devices, gather_shares(): return lax.all_to_all(parts, ('row', 'col'), 0, 0, axis_index_groups=groups)  8.34 us
    ppermute x13, waiting for transfers between devices, moved(): return lax.ppermute(shard, axes, pairs)  8.24 us
    pallas_call x1, Pallas kernels, far_slots(): pl.pallas_call(far_kernel, out_shape=[half, half, shape(2, 2, width, widt...  6.24 us
    pallas_call x1, Pallas kernels, orthogonalize(): pl.pallas_call(functools.partial(orthogonal_kernel, 1.0 / divisor), out_s...  5.79 us
    pallas_call x1, Pallas kernels, inside(): pl.pallas_call(inside_kernel, out_shape=shape(*tile.shape), in_specs=[SME...  5.38 us
  transfers between devices with their start and end apart: 15, of which 5 were waited for; matrix products, arithmetic and copies ran while one was open for 4% of the time, Pallas kernels for 21%

profile of v5, /device:TPU:1, one launch (start us, length us, event | category | flops | bytes accessed | tf_op | source)
XLA Modules:
  0.0 128.3 jit_solution(14560848897720247471)
XLA Ops:
  0.6 1.0 slice.22
  1.6 1.3 %collective-permute-start = (f32[2,2,160,128]{3,2,1,0:T(8,128)S(1)}, f32[2,2,160,128]{3,2,1,0:T(8,128)S(1)}, u32[]{:S(2)}, u32[]{:S(2)}) collective-permute-start(f32[2,2,160,128]{3,2,1,0:T(8,128)S(1)} %slice.22), channel_id=1, source_target_pairs={{1,0},{2,1},{3,2},{4,3},{5,4},{6,5},{7,6},{8,7},{9,8},{10,9},{11,1... | collective-permute-start | bytes 983048 | tf_op jit(solution)/shard_map/ppermute | solution.py:648
  2.9 1.3 fusion
  4.2 3.3 %collective-permute-start.4 = (f32[1,2,128,512]{3,2,1,0:T(8,128)S(1)}, f32[1,2,128,512]{3,2,1,0:T(8,128)S(1)}, u32[]{:S(2)}, u32[]{:S(2)}) collective-permute-start(f32[1,2,128,512]{3,2,1,0:T(8,128)S(1)} %get-tuple-element.28), channel_id=1, source_target_pairs={{16,0},{32,16},{48,32},{64,48},{80,64},{96,80},{112,96},{17,1},{33... | collective-permute-start | bytes 1572872 | tf_op jit(solution)/shard_map/ppermute | solution.py:648
  7.6 1.9 %collective-permute-start.3 = (f32[1,2,128,512]{3,2,1,0:T(8,128)S(1)}, f32[1,2,128,512]{3,2,1,0:T(8,128)S(1)}, u32[]{:S(2)}, u32[]{:S(2)}) collective-permute-start(f32[1,2,128,512]{3,2,1,0:T(8,128)S(1)} %get-tuple-element.29), channel_id=1, source_target_pairs={{16,0},{32,16},{48,32},{64,48},{80,64},{96,80},{112,96},{17,1},{33... | collective-permute-start | bytes 1572872 | tf_op jit(solution)/shard_map/ppermute | solution.py:648
  9.5 1.2 fusion.1
  10.7 1.3 %collective-permute-start.2 = (f32[2,2,176,128]{3,2,1,0:T(8,128)S(1)}, f32[2,2,176,128]{3,2,1,0:T(8,128)}, u32[]{:S(2)}, u32[]{:S(2)}) collective-permute-start(f32[2,2,176,128]{3,2,1,0:T(8,128)S(1)} %get-tuple-element.30), channel_id=1, source_target_pairs={{1,0},{2,1},{3,2},{4,3},{5,4},{6,5},{7,6},{8,7},{9,8},{10,9},{11,1... | collective-permute-start | bytes 1081352 | tf_op jit(solution)/shard_map/ppermute | solution.py:648
  12.0 1.3 %collective-permute-start.1 = (f32[2,2,176,128]{3,2,1,0:T(8,128)S(1)}, f32[2,2,176,128]{3,2,1,0:T(8,128)}, u32[]{:S(2)}, u32[]{:S(2)}) collective-permute-start(f32[2,2,176,128]{3,2,1,0:T(8,128)S(1)} %get-tuple-element.31), channel_id=1, source_target_pairs={{1,0},{2,1},{3,2},{4,3},{5,4},{6,5},{7,6},{8,7},{9,8},{10,9},{11,1... | collective-permute-start | bytes 1081352 | tf_op jit(solution)/shard_map/ppermute | solution.py:648
  13.3 0.0 collective-permute-done.top
  13.3 0.0 copy-start.3
  13.3 2.9 %collective-permute-start.5 = (f32[2,2,128,128]{3,2,1,0:T(8,128)S(1)}, f32[2,2,128,128]{3,2,1,0:T(8,128)}, u32[]{:S(2)}, u32[]{:S(2)}) collective-permute-start(f32[2,2,128,128]{3,2,1,0:T(8,128)S(1)} %slice.28), channel_id=1, source_target_pairs={{16,0},{32,16},{48,32},{64,48},{80,64},{96,80},{112,96},{17,1},{33... | collective-permute-start | bytes 786440 | tf_op jit(solution)/shard_map/ppermute | solution.py:648
  16.8 0.0 collective-permute-done.4.below_second
  16.9 0.0 copy-start.1
  16.9 5.2 %collective-permute-done.3.below_first = f32[1,2,128,512]{3,2,1,0:T(8,128)S(1)} collective-permute-done((f32[1,2,128,512]{3,2,1,0:T(8,128)S(1)}, f32[1,2,128,512]{3,2,1,0:T(8,128)S(1)}, u32[]{:S(2)}, u32[]{:S(2)}) %collective-permute-start.3) | collective-permute-done | bytes 524320 | tf_op jit(solution)/shard_map/ppermute | solution.py:648
  22.0 0.0 copy-start.2
  22.0 0.0 copy-done.1
  22.0 0.8 copy-done.2
  22.8 17.7 %near_slots.1 = (f32[24,128,128]{2,1,0:T(8,128)}, f32[4,2,2,128,128]{4,3,2,1,0:T(8,128)}, f32[2,2,128,512]{3,2,1,0:T(8,128)}) custom-call(s32[1,1]{1,0:T(1,128)S(6)} %copy.13.count_ref, s32[2,4]{1,0:T(2,128)} %bitcast.15, f32[2,2,512,512]{3,2,1,0:T(8,128)} %tile.5, f32[1,2,128,512]{3,2,1,0:T(8,128)} %copy-done.2, f32[1,2,128,512]{3,2,1,0:T(8,128)} %copy-done.1, ...), custom_call_target="tpu_custom_call" | custom-call | flops 33554432 | bytes 8388608 | tf_op jit(solution)/shard_map/near_slots/pallas_call | solution.py:426
  40.6 0.0 copy-done.3
  40.6 0.0 collective-permute-done.2.bottom
  40.6 0.0 collective-permute-done.1.middle
  40.6 0.0 collective-permute-done.5.corner
  40.6 6.2 %far_slots.1 = (f32[12,128,128]{2,1,0:T(8,128)}, f32[12,128,128]{2,1,0:T(8,128)}, f32[2,2,128,128]{3,2,1,0:T(8,128)}, f32[2,2,384,128]{3,2,1,0:T(8,128)}, f32[1,...) custom-call(s32[1,1]{1,0:T(1,128)S(6)} %copy.13.count_ref, ...), custom_call_target="tpu_custom_call", output_to_operand_aliasing={{7}: (16, {})} | custom-call | flops 12884901888 | bytes 8388608 | tf_op jit(solution)/shard_map/far_slots/pallas_call | solution.py:447
  46.9 0.1 collective-permute-start.6
  47.0 1.3 %collective-permute-start.8 = (f32[2,2,384,128]{3,2,1,0:T(8,128)}, f32[2,2,384,128]{3,2,1,0:T(8,128)S(1)}, u32[]{:S(2)}, u32[]{:S(2)}) collective-permute-start(f32[2,2,384,128]{3,2,1,0:T(8,128)} %get-tuple-element.22), channel_id=1, source_target_pairs={{0,1},{1,2},{2,3},{3,4},{4,5},{5,6},{6,7},{7,8},{8,9},{9,10},{10,1... | collective-permute-start | bytes 2359304 | tf_op jit(solution)/shard_map/ppermute | solution.py:648
  48.3 1.1 collective-permute-done.6
  49.4 2.1 %add.8 = f32[12,128,128]{2,1,0:T(8,128)} add(f32[12,128,128]{2,1,0:T(8,128)} %get-tuple-element.18, f32[12,128,128]{2,1,0:T(8,128)S(1)} %collective-permute-done.6) | non-fusion elementwise | flops 196608 | bytes 2359296 | tf_op jit(solution)/shard_map/add | solution.py:706
  51.5 24.1 %all-to-all-start = ((f32[64,24,128]{2,1,0:T(8,128)}), f32[64,24,128]{2,1,0:T(8,128)S(1)}, u32[]{:S(2)}, u32[]{:S(2)}) async-start(f32[64,24,128]{2,1,0:T(8,128)} %bitcast.4), calls=%async_computation | async-start | bytes 1572864 | tf_op jit(solution)/shard_map/all_to_all | solution.py:667
  75.7 3.9 %collective-permute-start.9 = (f32[1,2,128,512]{3,2,1,0:T(8,128)}, f32[1,2,128,512]{3,2,1,0:T(8,128)}, u32[]{:S(2)}, u32[]{:S(2)}) collective-permute-start(f32[1,2,128,512]{3,2,1,0:T(8,128)} %get-tuple-element.23), channel_id=1, source_target_pairs={{0,16},{16,32},{32,48},{48,64},{64,80},{80,96},{96,112},{1,17},{17... | collective-permute-start | bytes 1572872 | tf_op jit(solution)/shard_map/ppermute | solution.py:648
  79.5 1.9 %collective-permute-start.10 = (f32[1,2,128,512]{3,2,1,0:T(8,128)}, f32[1,2,128,512]{3,2,1,0:T(8,128)}, u32[]{:S(2)}, u32[]{:S(2)}) collective-permute-start(f32[1,2,128,512]{3,2,1,0:T(8,128)} %get-tuple-element.24), channel_id=1, source_target_pairs={{0,16},{16,32},{32,48},{48,64},{64,80},{80,96},{96,112},{1,17},{17... | collective-permute-start | bytes 1572872 | tf_op jit(solution)/shard_map/ppermute | solution.py:648
  81.5 3.1 %collective-permute-start.7 = (f32[2,2,128,128]{3,2,1,0:T(8,128)}, f32[2,2,128,128]{3,2,1,0:T(8,128)S(1)}, u32[]{:S(2)}, u32[]{:S(2)}) collective-permute-start(f32[2,2,128,128]{3,2,1,0:T(8,128)} %get-tuple-element.21), channel_id=1, source_target_pairs={{0,1},{1,2},{2,3},{3,4},{4,5},{5,6},{6,7},{7,8},{8,9},{9,10},{10,1... | collective-permute-start | bytes 786440 | tf_op jit(solution)/shard_map/ppermute | solution.py:648
  84.6 5.5 %collective-permute-start.11 = (f32[2,2,128,128]{3,2,1,0:T(8,128)}, f32[2,2,128,128]{3,2,1,0:T(8,128)}, u32[]{:S(2)}, u32[]{:S(2)}) collective-permute-start(f32[2,2,128,128]{3,2,1,0:T(8,128)} %get-tuple-element.25), channel_id=1, source_target_pairs={{0,17},{1,18},{2,19},{3,20},{4,21},{5,22},{6,23},{7,24},{8,25},{9,... | collective-permute-start | bytes 786440 | tf_op jit(solution)/shard_map/ppermute | solution.py:648
  90.0 5.4 %inside.1.partial = f32[2,2,512,512]{3,2,1,0:T(8,128)} custom-call(s32[1,1]{1,0:T(1,128)S(6)} %copy.13.count_ref, s32[2,4]{1,0:T(2,128)} %bitcast.17, f32[2,2,512,512]{3,2,1,0:T(8,128)} %tile.5, f32[4,2,2,128,128]{4,3,2,1,0:T(8,128)} %get-tuple-element.20.term_in), custom_call_target="tpu_custom_call" | custom-call | flops 268435456 | bytes 8388608 | tf_op jit(solution)/shard_map/inside/pallas_call | solution.py:472
  95.4 1.6 %all-to-all-done = f32[64,24,128]{2,1,0:T(8,128)S(1)} async-done(((f32[64,24,128]{2,1,0:T(8,128)}), f32[64,24,128]{2,1,0:T(8,128)S(1)}, u32[]{:S(2)}, u32[]{:S(2)}) %all-to-all-start) | async-done | bytes 786464 | tf_op jit(solution)/shard_map/all_to_all | solution.py:667
  97.0 0.1 reduce_sum.9
  97.1 0.9 broadcast_in_dim.2
  98.1 5.2 %all-to-all-start.1 = ((f32[64,24,128]{2,1,0:T(8,128)}), f32[64,24,128]{2,1,0:T(8,128)S(1)}, u32[]{:S(2)}, u32[]{:S(2)}) async-start(f32[64,24,128]{2,1,0:T(8,128)} %broadcast_in_dim.2), calls=%async_computation.1 | async-start | bytes 1572864 | tf_op jit(solution)/shard_map/all_to_all | solution.py:674
  103.3 0.0 copy-start
  103.3 0.0 collective-permute-done.7.left_top_in
  103.3 0.0 copy-start.5
  103.4 0.0 collective-permute-done.11.corner_in
  103.4 0.0 collective-permute-done.9.above_first_in
  103.4 0.0 collective-permute-done.10.above_second_in
  103.4 0.0 collective-permute-done.8.left_rest_in
  103.4 0.7 copy-done.5
  104.1 0.0 copy-start.4
  104.1 0.9 copy-done.4
  104.9 3.6 %settle.1 = f32[2,2,512,512]{3,2,1,0:T(8,128)} custom-call(f32[2,2,512,512]{3,2,1,0:T(8,128)} %inside.1.partial, f32[2,2,128,128]{3,2,1,0:T(8,128)} %copy-done.5, f32[2,2,384,128]{3,2,1,0:T(8,128)} %copy-done.4, f32[1,2,128,512]{3,2,1,0:T(8,128)} %collective-permute-done.9.above_first_in, ...), custom_call_target="tpu_custom_call", output_to_operand_aliasing={{}: (0, {})} | custom-call | flops 137438953472 | bytes 8388608 | tf_op jit(solution)/shard_map/settle/pallas_call | solution.py:492
  108.6 8.3 %all-to-all-done.1 = f32[64,24,128]{2,1,0:T(8,128)S(1)} async-done(((f32[64,24,128]{2,1,0:T(8,128)}), f32[64,24,128]{2,1,0:T(8,128)S(1)}, u32[]{:S(2)}, u32[]{:S(2)}) %all-to-all-start.1) | async-done | bytes 786464 | tf_op jit(solution)/shard_map/all_to_all | solution.py:674
  116.9 3.5 %collective-permute-start.12 = (f32[12,128,128]{2,1,0:T(8,128)S(1)}, f32[12,128,128]{2,1,0:T(8,128)S(1)}, u32[]{:S(2)}, u32[]{:S(2)}) collective-permute-start(f32[12,128,128]{2,1,0:T(8,128)S(1)} %bitcast.10), channel_id=1, source_target_pairs={{0,16},{16,0},{32,48},{48,32},{64,80},{80,64},{96,112},{112,96},{1... | collective-permute-start | bytes 2359304 | tf_op jit(solution)/shard_map/ppermute | solution.py:648
  120.4 1.9 %collective-permute-done.12.other = f32[12,128,128]{2,1,0:T(8,128)S(1)} collective-permute-done((f32[12,128,128]{2,1,0:T(8,128)S(1)}, f32[12,128,128]{2,1,0:T(8,128)S(1)}, u32[]{:S(2)}, u32[]{:S(2)}) %collective-permute-start.12) | collective-permute-done | bytes 786464 | tf_op jit(solution)/shard_map/ppermute | solution.py:648
  122.3 0.0 copy-done
  122.3 5.8 %orthogonalize.1 = f32[24,128,128]{2,1,0:T(8,128)} custom-call(s32[1,1]{1,0:T(1,128)} %bitcast.1.core_ref, f32[24,128,128]{2,1,0:T(8,128)S(1)} %bitcast.9, f32[12,128,128]{2,1,0:T(8,128)S(1)} %bitcast.11, f32[12,128,128]{2,1,0:T(8,128)S(1)} %collective-permute-done.12.other), custom_call_target="tpu_custom_call" | custom-call | tf_op jit(solution)/shard_map/orthogonalize/pallas_call | solution.py:629
  (1 shorter events, 0.0 us)
Async XLA Ops:
  1.6 11.6 %collective-permute-start = (f32[2,2,160,128]{3,2,1,0:T(8,128)S(1)}, f32[2,2,160,128]{3,2,1,0:T(8,128)S(1)}, u32[]{:S(2)}, u32[]{:S(2)}) collective-permute-start(f32[2,2,160,128]{3,2,1,0:T(8,128)S(1)} %slice.22), channel_id=1, source_target_pairs={{1,0},{2,1},{3,2},{4,3},{5,4},{6,5},{7,6},{8,7},{9,8},{10,9},{11,1... | collective-permute-start | bytes 983048 | tf_op jit(solution)/shard_map/ppermute | solution.py:648
  4.2 12.6 %collective-permute-start.4 = (f32[1,2,128,512]{3,2,1,0:T(8,128)S(1)}, f32[1,2,128,512]{3,2,1,0:T(8,128)S(1)}, u32[]{:S(2)}, u32[]{:S(2)}) collective-permute-start(f32[1,2,128,512]{3,2,1,0:T(8,128)S(1)} %get-tuple-element.28), channel_id=1, source_target_pairs={{16,0},{32,16},{48,32},{64,48},{80,64},{96,80},{112,96},{17,1},{33... | collective-permute-start | bytes 1572872 | tf_op jit(solution)/shard_map/ppermute | solution.py:648
  7.6 14.5 %collective-permute-start.3 = (f32[1,2,128,512]{3,2,1,0:T(8,128)S(1)}, f32[1,2,128,512]{3,2,1,0:T(8,128)S(1)}, u32[]{:S(2)}, u32[]{:S(2)}) collective-permute-start(f32[1,2,128,512]{3,2,1,0:T(8,128)S(1)} %get-tuple-element.29), channel_id=1, source_target_pairs={{16,0},{32,16},{48,32},{64,48},{80,64},{96,80},{112,96},{17,1},{33... | collective-permute-start | bytes 1572872 | tf_op jit(solution)/shard_map/ppermute | solution.py:648
  10.7 29.9 %collective-permute-start.2 = (f32[2,2,176,128]{3,2,1,0:T(8,128)S(1)}, f32[2,2,176,128]{3,2,1,0:T(8,128)}, u32[]{:S(2)}, u32[]{:S(2)}) collective-permute-start(f32[2,2,176,128]{3,2,1,0:T(8,128)S(1)} %get-tuple-element.30), channel_id=1, source_target_pairs={{1,0},{2,1},{3,2},{4,3},{5,4},{6,5},{7,6},{8,7},{9,8},{10,9},{11,1... | collective-permute-start | bytes 1081352 | tf_op jit(solution)/shard_map/ppermute | solution.py:648
  12.0 28.6 %collective-permute-start.1 = (f32[2,2,176,128]{3,2,1,0:T(8,128)S(1)}, f32[2,2,176,128]{3,2,1,0:T(8,128)}, u32[]{:S(2)}, u32[]{:S(2)}) collective-permute-start(f32[2,2,176,128]{3,2,1,0:T(8,128)S(1)} %get-tuple-element.31), channel_id=1, source_target_pairs={{1,0},{2,1},{3,2},{4,3},{5,4},{6,5},{7,6},{8,7},{9,8},{10,9},{11,1... | collective-permute-start | bytes 1081352 | tf_op jit(solution)/shard_map/ppermute | solution.py:648
  13.3 27.3 %copy-start.3 = (f32[2,2,160,128]{3,2,1,0:T(8,128)}, f32[2,2,160,128]{3,2,1,0:T(8,128)S(1)}, u32[]{:S(2)}) copy-start(f32[2,2,160,128]{3,2,1,0:T(8,128)S(1)} %collective-permute-done.top) | copy-start | bytes 983044
  13.3 27.3 %collective-permute-start.5 = (f32[2,2,128,128]{3,2,1,0:T(8,128)S(1)}, f32[2,2,128,128]{3,2,1,0:T(8,128)}, u32[]{:S(2)}, u32[]{:S(2)}) collective-permute-start(f32[2,2,128,128]{3,2,1,0:T(8,128)S(1)} %slice.28), channel_id=1, source_target_pairs={{16,0},{32,16},{48,32},{64,48},{80,64},{96,80},{112,96},{17,1},{33... | collective-permute-start | bytes 786440 | tf_op jit(solution)/shard_map/ppermute | solution.py:648
  16.9 5.2 %copy-start.1 = (f32[1,2,128,512]{3,2,1,0:T(8,128)}, f32[1,2,128,512]{3,2,1,0:T(8,128)S(1)}, u32[]{:S(2)}) copy-start(f32[1,2,128,512]{3,2,1,0:T(8,128)S(1)} %collective-permute-done.4.below_second) | copy-start | bytes 1572868
  22.0 0.8 copy-start.2
  46.9 2.6 %collective-permute-start.6 = (f32[12,128,128]{2,1,0:T(8,128)}, f32[12,128,128]{2,1,0:T(8,128)S(1)}, u32[]{:S(2)}, u32[]{:S(2)}) collective-permute-start(f32[12,128,128]{2,1,0:T(8,128)} %get-tuple-element.19), channel_id=1, source_target_pairs={{0,16},{16,0},{32,48},{48,32},{64,80},{80,64},{96,112},{112,96},{1... | collective-permute-start | bytes 2359304 | tf_op jit(solution)/shard_map/ppermute | solution.py:648
  47.0 56.4 %collective-permute-start.8 = (f32[2,2,384,128]{3,2,1,0:T(8,128)}, f32[2,2,384,128]{3,2,1,0:T(8,128)S(1)}, u32[]{:S(2)}, u32[]{:S(2)}) collective-permute-start(f32[2,2,384,128]{3,2,1,0:T(8,128)} %get-tuple-element.22), channel_id=1, source_target_pairs={{0,1},{1,2},{2,3},{3,4},{4,5},{5,6},{6,7},{7,8},{8,9},{9,10},{10,1... | collective-permute-start | bytes 2359304 | tf_op jit(solution)/shard_map/ppermute | solution.py:648
  51.5 45.5 %all-to-all-start = ((f32[64,24,128]{2,1,0:T(8,128)}), f32[64,24,128]{2,1,0:T(8,128)S(1)}, u32[]{:S(2)}, u32[]{:S(2)}) async-start(f32[64,24,128]{2,1,0:T(8,128)} %bitcast.4), calls=%async_computation | async-start | bytes 1572864 | tf_op jit(solution)/shard_map/all_to_all | solution.py:667
  75.7 27.7 %collective-permute-start.9 = (f32[1,2,128,512]{3,2,1,0:T(8,128)}, f32[1,2,128,512]{3,2,1,0:T(8,128)}, u32[]{:S(2)}, u32[]{:S(2)}) collective-permute-start(f32[1,2,128,512]{3,2,1,0:T(8,128)} %get-tuple-element.23), channel_id=1, source_target_pairs={{0,16},{16,32},{32,48},{48,64},{64,80},{80,96},{96,112},{1,17},{17... | collective-permute-start | bytes 1572872 | tf_op jit(solution)/shard_map/ppermute | solution.py:648
  79.5 23.9 %collective-permute-start.10 = (f32[1,2,128,512]{3,2,1,0:T(8,128)}, f32[1,2,128,512]{3,2,1,0:T(8,128)}, u32[]{:S(2)}, u32[]{:S(2)}) collective-permute-start(f32[1,2,128,512]{3,2,1,0:T(8,128)} %get-tuple-element.24), channel_id=1, source_target_pairs={{0,16},{16,32},{32,48},{48,64},{64,80},{80,96},{96,112},{1,17},{17... | collective-permute-start | bytes 1572872 | tf_op jit(solution)/shard_map/ppermute | solution.py:648
  81.5 21.9 %collective-permute-start.7 = (f32[2,2,128,128]{3,2,1,0:T(8,128)}, f32[2,2,128,128]{3,2,1,0:T(8,128)S(1)}, u32[]{:S(2)}, u32[]{:S(2)}) collective-permute-start(f32[2,2,128,128]{3,2,1,0:T(8,128)} %get-tuple-element.21), channel_id=1, source_target_pairs={{0,1},{1,2},{2,3},{3,4},{4,5},{5,6},{6,7},{7,8},{8,9},{9,10},{10,1... | collective-permute-start | bytes 786440 | tf_op jit(solution)/shard_map/ppermute | solution.py:648
  84.6 18.8 %collective-permute-start.11 = (f32[2,2,128,128]{3,2,1,0:T(8,128)}, f32[2,2,128,128]{3,2,1,0:T(8,128)}, u32[]{:S(2)}, u32[]{:S(2)}) collective-permute-start(f32[2,2,128,128]{3,2,1,0:T(8,128)} %get-tuple-element.25), channel_id=1, source_target_pairs={{0,17},{1,18},{2,19},{3,20},{4,21},{5,22},{6,23},{7,24},{8,25},{9,... | collective-permute-start | bytes 786440 | tf_op jit(solution)/shard_map/ppermute | solution.py:648
  98.1 18.8 %all-to-all-start.1 = ((f32[64,24,128]{2,1,0:T(8,128)}), f32[64,24,128]{2,1,0:T(8,128)S(1)}, u32[]{:S(2)}, u32[]{:S(2)}) async-start(f32[64,24,128]{2,1,0:T(8,128)} %broadcast_in_dim.2), calls=%async_computation.1 | async-start | bytes 1572864 | tf_op jit(solution)/shard_map/all_to_all | solution.py:674
  103.3 19.0 %copy-start = (f32[12,2,128,128]{3,2,1,0:T(8,128)S(1)}, f32[12,2,128,128]{3,2,1,0:T(8,128)}, u32[]{:S(2)}) copy-start(f32[12,2,128,128]{3,2,1,0:T(8,128)} %param.8) | copy-start | bytes 4718596
  103.3 0.7 copy-start.5
  104.1 0.9 copy-start.4
  116.9 5.4 %collective-permute-start.12 = (f32[12,128,128]{2,1,0:T(8,128)S(1)}, f32[12,128,128]{2,1,0:T(8,128)S(1)}, u32[]{:S(2)}, u32[]{:S(2)}) collective-permute-start(f32[12,128,128]{2,1,0:T(8,128)S(1)} %bitcast.10), channel_id=1, source_target_pairs={{0,16},{16,0},{32,48},{48,32},{64,80},{80,64},{96,112},{112,96},{1... | collective-permute-start | bytes 2359304 | tf_op jit(solution)/shard_map/ppermute | solution.py:648

commit v6 on v5

--- a/solution.py
+++ b/solution.py
@@ -274,15 +274,37 @@
     rows, cols = tile.shape[2:]
     down, across, inner = pl.ds(rows, width), pl.ds(cols, width), pl.ds(0, cols)
     right = [(0, top), (top.shape[2], middle), (rows - bottom.shape[2], bottom)]
-    loads = start_all(
-        far_sheet(tile, right, (below_first, below_second), corner, sheet, width)
-        + [(probe_in, probe), (step_in, steps), (transform_in, transforms), (pattern_in, patterns)]
-        + [(pgrad_in, pgrad), (below_in, outer.at[:, :, down, inner])],
-        sem_in,
-    )
+    count = count_ref[0, 0]
+    reaching = [
+        ((slot < count) & (pos_ref[1, slot] > cols - width)).astype(jnp.int32)
+        for slot in range(pos_ref.shape[1])
+    ]
+    needed = sum(reaching) > 0
+    sums = [(pgrad_in, pgrad), (below_in, outer.at[:, :, down, inner])]
+    inputs = far_sheet(tile, right, (below_first, below_second), corner, sheet, width) + [
+        (probe_in, probe), (step_in, steps), (transform_in, transforms), (pattern_in, patterns)
+    ]
+    loads = [
+        pltpu.make_async_copy(src, dst, sem_in.at[i]) for i, (src, dst) in enumerate(sums + inputs)
+    ]
+    kept, optional = loads[: len(sums)], loads[len(sums) :]
+
+    @pl.when(needed)
+    def _():
+        for copy in optional:
+            copy.start()
+
+    for copy in kept:
+        copy.start()
     outer[:, :, 0 : rows + width, cols : cols + width] = jnp.zeros((2, 2, rows + width, width), f32)
-    for copy in loads:
+    for copy in kept:
         copy.wait()
+
+    @pl.when(needed)
+    def _():
+        for copy in optional:
+            copy.wait()
+
     wait_terms = visit_slots(
         lambda slot: pos_ref[1, slot] > cols - width, count_ref[0, 0], pos_ref,
         lambda slot: pos_ref[1, slot] > cols - width,

time: 130 us -> 130 us (level)
  Pallas kernels: 38.8 us -> 51.4 us
  starting transfers between devices: 60.6 us -> 49.2 us
    all_to_all x1, starting transfers between devices: 24.1 us -> 10.5 us  [sum_share(): lax.all_to_all(parts, ('row', 'col'), 0, 0, axis_index_groups=groups)]
    pallas_call x1, Pallas kernels: 6.24 us -> 12.6 us  [far_slots(): pl.pallas_call(far_kernel, out_shape=[half, half, shape(2, 2, width, widt...]
    pallas_call x1, Pallas kernels: 17.7 us -> 23.5 us  [near_slots(): pl.pallas_call(near_kernel, out_shape=[shape(*probe.shape), shape(capacit...]
    all_to_all x1, starting transfers between devices: 5.25 us -> 8.43 us  [gather_shares(): return lax.all_to_all(parts, ('row', 'col'), 0, 0, axis_index_groups=groups)]
    all_to_all x1, waiting for transfers between devices: 1.64 us -> 0.01 us  [sum_share(): lax.all_to_all(parts, ('row', 'col'), 0, 0, axis_index_groups=groups)]
  transfers between devices with their start and end apart: 15 -> 15, of which waited for: 5 -> 4; matrix products, arithmetic and copies ran while one was open for 4% -> 4% of each run, Pallas kernels for 21% -> 26%
where the time goes in v6:
time: 130 us; the launch traced here: 129 us
  Pallas kernels  51.4 us (40%)
  starting transfers between devices  49.2 us (38%)
  waiting for transfers between devices  17.6 us (14%)
  local copies, waits for them, and re-layouts  6.76 us (5%)
  other arithmetic  2.18 us (2%)
  between operations  1.76 us (1%)
    ppermute x13, starting transfers between devices, moved(): return lax.ppermute(shard, axes, pairs)  30.3 us
    pallas_call x1, Pallas kernels, near_slots(): pl.pallas_call(near_kernel, out_shape=[shape(*probe.shape), shape(capacit...  23.5 us
    pallas_call x1, Pallas kernels, far_slots(): pl.pallas_call(far_kernel, out_shape=[half, half, shape(2, 2, width, widt...  12.6 us
    all_to_all x1, starting transfers between devices, sum_share(): lax.all_to_all(parts, ('row', 'col'), 0, 0, axis_index_groups=groups)  10.5 us
    all_to_all x1, waiting for transfers between devices, gather_shares(): return lax.all_to_all(parts, ('row', 'col'), 0, 0, axis_index_groups=groups)  9.32 us
    all_to_all x1, starting transfers between devices, gather_shares(): return lax.all_to_all(parts, ('row', 'col'), 0, 0, axis_index_groups=groups)  8.43 us
    ppermute x13, waiting for transfers between devices, moved(): return lax.ppermute(shard, axes, pairs)  8.24 us
    pallas_call x1, Pallas kernels, inside(): pl.pallas_call(inside_kernel, out_shape=shape(*tile.shape), in_specs=[SME...  5.88 us
  transfers between devices with their start and end apart: 15, of which 4 were waited for; matrix products, arithmetic and copies ran while one was open for 4% of the time, Pallas kernels for 26%

profile of v6, /device:TPU:1, one launch (start us, length us, event | category | flops | bytes accessed | tf_op | source)
XLA Modules:
  0.0 128.9 jit_solution(7477812684462840690)
XLA Ops:
  0.6 1.0 slice.22
  1.6 1.3 %collective-permute-start = (f32[2,2,160,128]{3,2,1,0:T(8,128)S(1)}, f32[2,2,160,128]{3,2,1,0:T(8,128)S(1)}, u32[]{:S(2)}, u32[]{:S(2)}) collective-permute-start(f32[2,2,160,128]{3,2,1,0:T(8,128)S(1)} %slice.22), channel_id=1, source_target_pairs={{1,0},{2,1},{3,2},{4,3},{5,4},{6,5},{7,6},{8,7},{9,8},{10,9},{11,1... | collective-permute-start | bytes 983048 | tf_op jit(solution)/shard_map/ppermute | solution.py:670
  2.9 1.3 fusion
  4.2 3.3 %collective-permute-start.4 = (f32[1,2,128,512]{3,2,1,0:T(8,128)S(1)}, f32[1,2,128,512]{3,2,1,0:T(8,128)S(1)}, u32[]{:S(2)}, u32[]{:S(2)}) collective-permute-start(f32[1,2,128,512]{3,2,1,0:T(8,128)S(1)} %get-tuple-element.28), channel_id=1, source_target_pairs={{16,0},{32,16},{48,32},{64,48},{80,64},{96,80},{112,96},{17,1},{33... | collective-permute-start | bytes 1572872 | tf_op jit(solution)/shard_map/ppermute | solution.py:670
  7.6 1.9 %collective-permute-start.3 = (f32[1,2,128,512]{3,2,1,0:T(8,128)S(1)}, f32[1,2,128,512]{3,2,1,0:T(8,128)S(1)}, u32[]{:S(2)}, u32[]{:S(2)}) collective-permute-start(f32[1,2,128,512]{3,2,1,0:T(8,128)S(1)} %get-tuple-element.29), channel_id=1, source_target_pairs={{16,0},{32,16},{48,32},{64,48},{80,64},{96,80},{112,96},{17,1},{33... | collective-permute-start | bytes 1572872 | tf_op jit(solution)/shard_map/ppermute | solution.py:670
  9.5 1.2 fusion.1
  10.7 1.3 %collective-permute-start.2 = (f32[2,2,176,128]{3,2,1,0:T(8,128)S(1)}, f32[2,2,176,128]{3,2,1,0:T(8,128)}, u32[]{:S(2)}, u32[]{:S(2)}) collective-permute-start(f32[2,2,176,128]{3,2,1,0:T(8,128)S(1)} %get-tuple-element.30), channel_id=1, source_target_pairs={{1,0},{2,1},{3,2},{4,3},{5,4},{6,5},{7,6},{8,7},{9,8},{10,9},{11,1... | collective-permute-start | bytes 1081352 | tf_op jit(solution)/shard_map/ppermute | solution.py:670
  12.0 1.3 %collective-permute-start.1 = (f32[2,2,176,128]{3,2,1,0:T(8,128)S(1)}, f32[2,2,176,128]{3,2,1,0:T(8,128)}, u32[]{:S(2)}, u32[]{:S(2)}) collective-permute-start(f32[2,2,176,128]{3,2,1,0:T(8,128)S(1)} %get-tuple-element.31), channel_id=1, source_target_pairs={{1,0},{2,1},{3,2},{4,3},{5,4},{6,5},{7,6},{8,7},{9,8},{10,9},{11,1... | collective-permute-start | bytes 1081352 | tf_op jit(solution)/shard_map/ppermute | solution.py:670
  13.3 0.0 collective-permute-done.top
  13.3 0.0 copy-start.3
  13.3 2.9 %collective-permute-start.5 = (f32[2,2,128,128]{3,2,1,0:T(8,128)S(1)}, f32[2,2,128,128]{3,2,1,0:T(8,128)}, u32[]{:S(2)}, u32[]{:S(2)}) collective-permute-start(f32[2,2,128,128]{3,2,1,0:T(8,128)S(1)} %slice.28), channel_id=1, source_target_pairs={{16,0},{32,16},{48,32},{64,48},{80,64},{96,80},{112,96},{17,1},{33... | collective-permute-start | bytes 786440 | tf_op jit(solution)/shard_map/ppermute | solution.py:670
  16.8 0.0 collective-permute-done.4.below_second
  16.9 0.0 copy-start.1
  16.9 5.2 %collective-permute-done.3.below_first = f32[1,2,128,512]{3,2,1,0:T(8,128)S(1)} collective-permute-done((f32[1,2,128,512]{3,2,1,0:T(8,128)S(1)}, f32[1,2,128,512]{3,2,1,0:T(8,128)S(1)}, u32[]{:S(2)}, u32[]{:S(2)}) %collective-permute-start.3) | collective-permute-done | bytes 524320 | tf_op jit(solution)/shard_map/ppermute | solution.py:670
  22.0 0.0 copy-start.2
  22.0 0.0 copy-done.1
  22.0 0.8 copy-done.2
  22.8 23.5 %near_slots.1 = (f32[24,128,128]{2,1,0:T(8,128)}, f32[4,2,2,128,128]{4,3,2,1,0:T(8,128)}, f32[2,2,128,512]{3,2,1,0:T(8,128)}) custom-call(s32[1,1]{1,0:T(1,128)S(6)} %copy.13.count_ref, s32[2,4]{1,0:T(2,128)} %bitcast.15, f32[2,2,512,512]{3,2,1,0:T(8,128)} %tile.5, f32[1,2,128,512]{3,2,1,0:T(8,128)} %copy-done.2, f32[1,2,128,512]{3,2,1,0:T(8,128)} %copy-done.1, ...), custom_call_target="tpu_custom_call" | custom-call | flops 33554432 | bytes 8388608 | tf_op jit(solution)/shard_map/near_slots/pallas_call | solution.py:448
  46.4 0.0 copy-done.3
  46.4 0.0 collective-permute-done.2.bottom
  46.4 0.0 collective-permute-done.1.middle
  46.4 0.0 collective-permute-done.5.corner
  46.4 12.6 %far_slots.1 = (f32[12,128,128]{2,1,0:T(8,128)}, f32[12,128,128]{2,1,0:T(8,128)}, f32[2,2,128,128]{3,2,1,0:T(8,128)}, f32[2,2,384,128]{3,2,1,0:T(8,128)}, f32[1,...) custom-call(s32[1,1]{1,0:T(1,128)S(6)} %copy.13.count_ref, ...), custom_call_target="tpu_custom_call", output_to_operand_aliasing={{7}: (16, {})} | custom-call | flops 12884901888 | bytes 8388608 | tf_op jit(solution)/shard_map/far_slots/pallas_call | solution.py:469
  59.1 0.1 collective-permute-start.6
  59.1 1.3 %collective-permute-start.8 = (f32[2,2,384,128]{3,2,1,0:T(8,128)}, f32[2,2,384,128]{3,2,1,0:T(8,128)S(1)}, u32[]{:S(2)}, u32[]{:S(2)}) collective-permute-start(f32[2,2,384,128]{3,2,1,0:T(8,128)} %get-tuple-element.22), channel_id=1, source_target_pairs={{0,1},{1,2},{2,3},{3,4},{4,5},{5,6},{6,7},{7,8},{8,9},{9,10},{10,1... | collective-permute-start | bytes 2359304 | tf_op jit(solution)/shard_map/ppermute | solution.py:670
  60.5 1.1 collective-permute-done.6
  61.6 2.1 %add.8 = f32[12,128,128]{2,1,0:T(8,128)} add(f32[12,128,128]{2,1,0:T(8,128)} %get-tuple-element.18, f32[12,128,128]{2,1,0:T(8,128)S(1)} %collective-permute-done.6) | non-fusion elementwise | flops 196608 | bytes 2359296 | tf_op jit(solution)/shard_map/add | solution.py:728
  63.7 10.5 %all-to-all-start = ((f32[64,24,128]{2,1,0:T(8,128)}), f32[64,24,128]{2,1,0:T(8,128)S(1)}, u32[]{:S(2)}, u32[]{:S(2)}) async-start(f32[64,24,128]{2,1,0:T(8,128)} %bitcast.4), calls=%async_computation | async-start | bytes 1572864 | tf_op jit(solution)/shard_map/all_to_all | solution.py:689
  74.2 3.9 %collective-permute-start.9 = (f32[1,2,128,512]{3,2,1,0:T(8,128)}, f32[1,2,128,512]{3,2,1,0:T(8,128)}, u32[]{:S(2)}, u32[]{:S(2)}) collective-permute-start(f32[1,2,128,512]{3,2,1,0:T(8,128)} %get-tuple-element.23), channel_id=1, source_target_pairs={{0,16},{16,32},{32,48},{48,64},{64,80},{80,96},{96,112},{1,17},{17... | collective-permute-start | bytes 1572872 | tf_op jit(solution)/shard_map/ppermute | solution.py:670
  78.1 1.9 %collective-permute-start.10 = (f32[1,2,128,512]{3,2,1,0:T(8,128)}, f32[1,2,128,512]{3,2,1,0:T(8,128)}, u32[]{:S(2)}, u32[]{:S(2)}) collective-permute-start(f32[1,2,128,512]{3,2,1,0:T(8,128)} %get-tuple-element.24), channel_id=1, source_target_pairs={{0,16},{16,32},{32,48},{48,64},{64,80},{80,96},{96,112},{1,17},{17... | collective-permute-start | bytes 1572872 | tf_op jit(solution)/shard_map/ppermute | solution.py:670
  80.0 3.1 %collective-permute-start.7 = (f32[2,2,128,128]{3,2,1,0:T(8,128)}, f32[2,2,128,128]{3,2,1,0:T(8,128)S(1)}, u32[]{:S(2)}, u32[]{:S(2)}) collective-permute-start(f32[2,2,128,128]{3,2,1,0:T(8,128)} %get-tuple-element.21), channel_id=1, source_target_pairs={{0,1},{1,2},{2,3},{3,4},{4,5},{5,6},{6,7},{7,8},{8,9},{9,10},{10,1... | collective-permute-start | bytes 786440 | tf_op jit(solution)/shard_map/ppermute | solution.py:670
  83.1 5.5 %collective-permute-start.11 = (f32[2,2,128,128]{3,2,1,0:T(8,128)}, f32[2,2,128,128]{3,2,1,0:T(8,128)}, u32[]{:S(2)}, u32[]{:S(2)}) collective-permute-start(f32[2,2,128,128]{3,2,1,0:T(8,128)} %get-tuple-element.25), channel_id=1, source_target_pairs={{0,17},{1,18},{2,19},{3,20},{4,21},{5,22},{6,23},{7,24},{8,25},{9,... | collective-permute-start | bytes 786440 | tf_op jit(solution)/shard_map/ppermute | solution.py:670
  88.6 5.9 %inside.1.partial = f32[2,2,512,512]{3,2,1,0:T(8,128)} custom-call(s32[1,1]{1,0:T(1,128)S(6)} %copy.13.count_ref, s32[2,4]{1,0:T(2,128)} %bitcast.17, f32[2,2,512,512]{3,2,1,0:T(8,128)} %tile.5, f32[4,2,2,128,128]{4,3,2,1,0:T(8,128)} %get-tuple-element.20.term_in), custom_call_target="tpu_custom_call" | custom-call | flops 268435456 | bytes 8388608 | tf_op jit(solution)/shard_map/inside/pallas_call | solution.py:494
  94.5 0.0 all-to-all-done
  94.5 0.1 reduce_sum.9
  94.6 0.9 broadcast_in_dim.2
  95.5 8.4 %all-to-all-start.1 = ((f32[64,24,128]{2,1,0:T(8,128)}), f32[64,24,128]{2,1,0:T(8,128)S(1)}, u32[]{:S(2)}, u32[]{:S(2)}) async-start(f32[64,24,128]{2,1,0:T(8,128)} %broadcast_in_dim.2), calls=%async_computation.1 | async-start | bytes 1572864 | tf_op jit(solution)/shard_map/all_to_all | solution.py:696
  103.9 0.0 copy-start
  104.0 0.0 collective-permute-done.7.left_top_in
  104.0 0.0 copy-start.5
  104.0 0.0 collective-permute-done.11.corner_in
  104.0 0.0 collective-permute-done.9.above_first_in
  104.0 0.0 collective-permute-done.10.above_second_in
  104.0 0.0 collective-permute-done.8.left_rest_in
  104.0 0.7 copy-done.5
  104.7 0.0 copy-start.4
  104.7 0.9 copy-done.4
  105.6 3.6 %settle.1 = f32[2,2,512,512]{3,2,1,0:T(8,128)} custom-call(f32[2,2,512,512]{3,2,1,0:T(8,128)} %inside.1.partial, f32[2,2,128,128]{3,2,1,0:T(8,128)} %copy-done.5, f32[2,2,384,128]{3,2,1,0:T(8,128)} %copy-done.4, f32[1,2,128,512]{3,2,1,0:T(8,128)} %collective-permute-done.9.above_first_in, ...), custom_call_target="tpu_custom_call", output_to_operand_aliasing={{}: (0, {})} | custom-call | flops 137438953472 | bytes 8388608 | tf_op jit(solution)/shard_map/settle/pallas_call | solution.py:514
  109.2 9.3 %all-to-all-done.1 = f32[64,24,128]{2,1,0:T(8,128)S(1)} async-done(((f32[64,24,128]{2,1,0:T(8,128)}), f32[64,24,128]{2,1,0:T(8,128)S(1)}, u32[]{:S(2)}, u32[]{:S(2)}) %all-to-all-start.1) | async-done | bytes 786464 | tf_op jit(solution)/shard_map/all_to_all | solution.py:696
  118.5 2.5 %collective-permute-start.12 = (f32[12,128,128]{2,1,0:T(8,128)S(1)}, f32[12,128,128]{2,1,0:T(8,128)S(1)}, u32[]{:S(2)}, u32[]{:S(2)}) collective-permute-start(f32[12,128,128]{2,1,0:T(8,128)S(1)} %bitcast.10), channel_id=1, source_target_pairs={{0,16},{16,0},{32,48},{48,32},{64,80},{80,64},{96,112},{112,96},{1... | collective-permute-start | bytes 2359304 | tf_op jit(solution)/shard_map/ppermute | solution.py:670
  121.0 1.9 %collective-permute-done.12.other = f32[12,128,128]{2,1,0:T(8,128)S(1)} collective-permute-done((f32[12,128,128]{2,1,0:T(8,128)S(1)}, f32[12,128,128]{2,1,0:T(8,128)S(1)}, u32[]{:S(2)}, u32[]{:S(2)}) %collective-permute-start.12) | collective-permute-done | bytes 786464 | tf_op jit(solution)/shard_map/ppermute | solution.py:670
  122.9 0.0 copy-done
  122.9 5.8 %orthogonalize.1 = f32[24,128,128]{2,1,0:T(8,128)} custom-call(s32[1,1]{1,0:T(1,128)} %bitcast.1.core_ref, f32[24,128,128]{2,1,0:T(8,128)S(1)} %bitcast.9, f32[12,128,128]{2,1,0:T(8,128)S(1)} %bitcast.11, f32[12,128,128]{2,1,0:T(8,128)S(1)} %collective-permute-done.12.other), custom_call_target="tpu_custom_call" | custom-call | tf_op jit(solution)/shard_map/orthogonalize/pallas_call | solution.py:651
  (1 shorter events, 0.0 us)
Async XLA Ops:
  1.6 11.6 %collective-permute-start = (f32[2,2,160,128]{3,2,1,0:T(8,128)S(1)}, f32[2,2,160,128]{3,2,1,0:T(8,128)S(1)}, u32[]{:S(2)}, u32[]{:S(2)}) collective-permute-start(f32[2,2,160,128]{3,2,1,0:T(8,128)S(1)} %slice.22), channel_id=1, source_target_pairs={{1,0},{2,1},{3,2},{4,3},{5,4},{6,5},{7,6},{8,7},{9,8},{10,9},{11,1... | collective-permute-start | bytes 983048 | tf_op jit(solution)/shard_map/ppermute | solution.py:670
  4.2 12.6 %collective-permute-start.4 = (f32[1,2,128,512]{3,2,1,0:T(8,128)S(1)}, f32[1,2,128,512]{3,2,1,0:T(8,128)S(1)}, u32[]{:S(2)}, u32[]{:S(2)}) collective-permute-start(f32[1,2,128,512]{3,2,1,0:T(8,128)S(1)} %get-tuple-element.28), channel_id=1, source_target_pairs={{16,0},{32,16},{48,32},{64,48},{80,64},{96,80},{112,96},{17,1},{33... | collective-permute-start | bytes 1572872 | tf_op jit(solution)/shard_map/ppermute | solution.py:670
  7.6 14.5 %collective-permute-start.3 = (f32[1,2,128,512]{3,2,1,0:T(8,128)S(1)}, f32[1,2,128,512]{3,2,1,0:T(8,128)S(1)}, u32[]{:S(2)}, u32[]{:S(2)}) collective-permute-start(f32[1,2,128,512]{3,2,1,0:T(8,128)S(1)} %get-tuple-element.29), channel_id=1, source_target_pairs={{16,0},{32,16},{48,32},{64,48},{80,64},{96,80},{112,96},{17,1},{33... | collective-permute-start | bytes 1572872 | tf_op jit(solution)/shard_map/ppermute | solution.py:670
  10.7 35.7 %collective-permute-start.2 = (f32[2,2,176,128]{3,2,1,0:T(8,128)S(1)}, f32[2,2,176,128]{3,2,1,0:T(8,128)}, u32[]{:S(2)}, u32[]{:S(2)}) collective-permute-start(f32[2,2,176,128]{3,2,1,0:T(8,128)S(1)} %get-tuple-element.30), channel_id=1, source_target_pairs={{1,0},{2,1},{3,2},{4,3},{5,4},{6,5},{7,6},{8,7},{9,8},{10,9},{11,1... | collective-permute-start | bytes 1081352 | tf_op jit(solution)/shard_map/ppermute | solution.py:670
  12.0 34.4 %collective-permute-start.1 = (f32[2,2,176,128]{3,2,1,0:T(8,128)S(1)}, f32[2,2,176,128]{3,2,1,0:T(8,128)}, u32[]{:S(2)}, u32[]{:S(2)}) collective-permute-start(f32[2,2,176,128]{3,2,1,0:T(8,128)S(1)} %get-tuple-element.31), channel_id=1, source_target_pairs={{1,0},{2,1},{3,2},{4,3},{5,4},{6,5},{7,6},{8,7},{9,8},{10,9},{11,1... | collective-permute-start | bytes 1081352 | tf_op jit(solution)/shard_map/ppermute | solution.py:670
  13.3 33.1 %copy-start.3 = (f32[2,2,160,128]{3,2,1,0:T(8,128)}, f32[2,2,160,128]{3,2,1,0:T(8,128)S(1)}, u32[]{:S(2)}) copy-start(f32[2,2,160,128]{3,2,1,0:T(8,128)S(1)} %collective-permute-done.top) | copy-start | bytes 983044
  13.3 33.1 %collective-permute-start.5 = (f32[2,2,128,128]{3,2,1,0:T(8,128)S(1)}, f32[2,2,128,128]{3,2,1,0:T(8,128)}, u32[]{:S(2)}, u32[]{:S(2)}) collective-permute-start(f32[2,2,128,128]{3,2,1,0:T(8,128)S(1)} %slice.28), channel_id=1, source_target_pairs={{16,0},{32,16},{48,32},{64,48},{80,64},{96,80},{112,96},{17,1},{33... | collective-permute-start | bytes 786440 | tf_op jit(solution)/shard_map/ppermute | solution.py:670
  16.9 5.2 %copy-start.1 = (f32[1,2,128,512]{3,2,1,0:T(8,128)}, f32[1,2,128,512]{3,2,1,0:T(8,128)S(1)}, u32[]{:S(2)}) copy-start(f32[1,2,128,512]{3,2,1,0:T(8,128)S(1)} %collective-permute-done.4.below_second) | copy-start | bytes 1572868
  22.0 0.8 copy-start.2
  59.1 2.6 %collective-permute-start.6 = (f32[12,128,128]{2,1,0:T(8,128)}, f32[12,128,128]{2,1,0:T(8,128)S(1)}, u32[]{:S(2)}, u32[]{:S(2)}) collective-permute-start(f32[12,128,128]{2,1,0:T(8,128)} %get-tuple-element.19), channel_id=1, source_target_pairs={{0,16},{16,0},{32,48},{48,32},{64,80},{80,64},{96,112},{112,96},{1... | collective-permute-start | bytes 2359304 | tf_op jit(solution)/shard_map/ppermute | solution.py:670
  59.1 44.9 %collective-permute-start.8 = (f32[2,2,384,128]{3,2,1,0:T(8,128)}, f32[2,2,384,128]{3,2,1,0:T(8,128)S(1)}, u32[]{:S(2)}, u32[]{:S(2)}) collective-permute-start(f32[2,2,384,128]{3,2,1,0:T(8,128)} %get-tuple-element.22), channel_id=1, source_target_pairs={{0,1},{1,2},{2,3},{3,4},{4,5},{5,6},{6,7},{7,8},{8,9},{9,10},{10,1... | collective-permute-start | bytes 2359304 | tf_op jit(solution)/shard_map/ppermute | solution.py:670
  63.7 30.7 %all-to-all-start = ((f32[64,24,128]{2,1,0:T(8,128)}), f32[64,24,128]{2,1,0:T(8,128)S(1)}, u32[]{:S(2)}, u32[]{:S(2)}) async-start(f32[64,24,128]{2,1,0:T(8,128)} %bitcast.4), calls=%async_computation | async-start | bytes 1572864 | tf_op jit(solution)/shard_map/all_to_all | solution.py:689
  74.2 29.8 %collective-permute-start.9 = (f32[1,2,128,512]{3,2,1,0:T(8,128)}, f32[1,2,128,512]{3,2,1,0:T(8,128)}, u32[]{:S(2)}, u32[]{:S(2)}) collective-permute-start(f32[1,2,128,512]{3,2,1,0:T(8,128)} %get-tuple-element.23), channel_id=1, source_target_pairs={{0,16},{16,32},{32,48},{48,64},{64,80},{80,96},{96,112},{1,17},{17... | collective-permute-start | bytes 1572872 | tf_op jit(solution)/shard_map/ppermute | solution.py:670
  78.1 25.9 %collective-permute-start.10 = (f32[1,2,128,512]{3,2,1,0:T(8,128)}, f32[1,2,128,512]{3,2,1,0:T(8,128)}, u32[]{:S(2)}, u32[]{:S(2)}) collective-permute-start(f32[1,2,128,512]{3,2,1,0:T(8,128)} %get-tuple-element.24), channel_id=1, source_target_pairs={{0,16},{16,32},{32,48},{48,64},{64,80},{80,96},{96,112},{1,17},{17... | collective-permute-start | bytes 1572872 | tf_op jit(solution)/shard_map/ppermute | solution.py:670
  80.0 23.9 %collective-permute-start.7 = (f32[2,2,128,128]{3,2,1,0:T(8,128)}, f32[2,2,128,128]{3,2,1,0:T(8,128)S(1)}, u32[]{:S(2)}, u32[]{:S(2)}) collective-permute-start(f32[2,2,128,128]{3,2,1,0:T(8,128)} %get-tuple-element.21), channel_id=1, source_target_pairs={{0,1},{1,2},{2,3},{3,4},{4,5},{5,6},{6,7},{7,8},{8,9},{9,10},{10,1... | collective-permute-start | bytes 786440 | tf_op jit(solution)/shard_map/ppermute | solution.py:670
  83.1 20.9 %collective-permute-start.11 = (f32[2,2,128,128]{3,2,1,0:T(8,128)}, f32[2,2,128,128]{3,2,1,0:T(8,128)}, u32[]{:S(2)}, u32[]{:S(2)}) collective-permute-start(f32[2,2,128,128]{3,2,1,0:T(8,128)} %get-tuple-element.25), channel_id=1, source_target_pairs={{0,17},{1,18},{2,19},{3,20},{4,21},{5,22},{6,23},{7,24},{8,25},{9,... | collective-permute-start | bytes 786440 | tf_op jit(solution)/shard_map/ppermute | solution.py:670
  95.5 23.0 %all-to-all-start.1 = ((f32[64,24,128]{2,1,0:T(8,128)}), f32[64,24,128]{2,1,0:T(8,128)S(1)}, u32[]{:S(2)}, u32[]{:S(2)}) async-start(f32[64,24,128]{2,1,0:T(8,128)} %broadcast_in_dim.2), calls=%async_computation.1 | async-start | bytes 1572864 | tf_op jit(solution)/shard_map/all_to_all | solution.py:696
  103.9 19.0 %copy-start = (f32[12,2,128,128]{3,2,1,0:T(8,128)S(1)}, f32[12,2,128,128]{3,2,1,0:T(8,128)}, u32[]{:S(2)}) copy-start(f32[12,2,128,128]{3,2,1,0:T(8,128)} %param.8) | copy-start | bytes 4718596
  104.0 0.7 copy-start.5
  104.7 0.9 copy-start.4
  118.5 4.4 %collective-permute-start.12 = (f32[12,128,128]{2,1,0:T(8,128)S(1)}, f32[12,128,128]{2,1,0:T(8,128)S(1)}, u32[]{:S(2)}, u32[]{:S(2)}) collective-permute-start(f32[12,128,128]{2,1,0:T(8,128)S(1)} %bitcast.10), channel_id=1, source_target_pairs={{0,16},{16,0},{32,48},{48,32},{64,80},{80,64},{96,112},{112,96},{1... | collective-permute-start | bytes 2359304 | tf_op jit(solution)/shard_map/ppermute | solution.py:670
